TPU v7x, 32 devices: a whole 2x2x4 slice. The times are simulated.
32 devices in a mesh: expert: 8 (over z, x), hidden: 4 (over y, core).
Axes of the slice: x: 2, y: 2, z: 4, core: 2. Of those that a mesh axis runs over, the one named last changes fastest.
Arguments:
- tokens: bfloat16 [2048, 1152], P('expert'), may hold values from -6 to 6
- cotangent: bfloat16 [2048, 1152], P('expert'), may hold values from -6 to 6
- seq_lengths: int32 [8, 2], P('expert'), may hold values from 128 to 128, as said below
- routes: int32 [2048, 1], P('expert'), may hold values from 0 to 7; in each aligned block of 256 rows (0 to 255, 256 to 511, ...) at most 48 rows name the same one
- mixer_gain: bfloat16 [1152], P('expert'), may hold values from 0.5 to 1.5
- proj_x: bfloat16 [1152, 2304], P(None, ('expert', 'hidden')), may hold values from -0.1875 to 0.1875
- proj_z: bfloat16 [1152, 2304], P(None, ('expert', 'hidden')), may hold values from -0.1875 to 0.1875
- conv_weight: bfloat16 [4, 2304], P(None, ('expert', 'hidden')), may hold values from -3 to 3
- conv_bias: bfloat16 [2304], P(('expert', 'hidden')), may hold values from -3 to 3
- state_proj: bfloat16 [2304, 104], P(('expert', 'hidden')), may hold values from -0.125 to 0.125
- step_proj: bfloat16 [72, 2304], P(None, ('expert', 'hidden')), may hold values from -0.75 to 0.75
- step_bias: bfloat16 [2304], P(('expert', 'hidden')), may hold values from -6 to -2
- decay_log: bfloat16 [16, 2304], P(None, ('expert', 'hidden')), may hold values from 0 to 2.765625
- skip_gain: bfloat16 [2304], P(('expert', 'hidden')), may hold values from 0.5 to 1.5
- out_proj: bfloat16 [2304, 1152], P(('expert', 'hidden')), may hold values from -0.125 to 0.125
- moe_gain: bfloat16 [1152], P('expert'), may hold values from 0.5 to 1.5
- router: bfloat16 [1152, 8], P('expert'), may hold values from -0.09375 to 0.09375
- expert_up: bfloat16 [8, 1152, 3072], P(None, None, 'hidden'), may hold values from -0.1875 to 0.1875
- expert_down: bfloat16 [8, 3072, 1152], P(None, 'hidden'), may hold values from -0.15625 to 0.15625
Outputs:
- layer_out: bfloat16 [2048, 1152], P('expert')
- tokens_grad: float32 [2048, 1152], P('expert')
- mixer_gain_grad: float32 [1152], P('expert')
- proj_x_grad: float32 [1152, 2304], P(None, ('expert', 'hidden'))
- proj_z_grad: float32 [1152, 2304], P(None, ('expert', 'hidden'))
- conv_weight_grad: float32 [4, 2304], P(None, ('expert', 'hidden'))
- conv_bias_grad: float32 [2304], P(('expert', 'hidden'))
- state_proj_grad: float32 [2304, 104], P(('expert', 'hidden'))
- step_proj_grad: float32 [72, 2304], P(None, ('expert', 'hidden'))
- step_bias_grad: float32 [2304], P(('expert', 'hidden'))
- decay_log_grad: float32 [16, 2304], P(None, ('expert', 'hidden'))
- skip_gain_grad: float32 [2304], P(('expert', 'hidden'))
- out_proj_grad: float32 [2304, 1152], P(('expert', 'hidden'))
- moe_gain_grad: float32 [1152], P('expert')
- router_grad: float32 [1152, 8], P('expert')
- expert_up_grad: float32 [8, 1152, 3072], P(None, 'expert', 'hidden')
- expert_down_grad: float32 [8, 3072, 1152], P(None, 'hidden', 'expert')
Inputs may be any that keep to these rules, and one draw needn't show every extreme that they name: `seq_lengths`: on each index of expert the two lengths sum to at most 256, and to exactly 256 on some index. `routes`: among the 256 rows of one device no expert is named by more than 48 rows.
All inputs are finite; a program needn't handle non-finite values.
Results may differ from a plain program's by a relative error of at most 0.015.
Values may be sent and summed in bfloat16 or wider, within the bound.
No kernel may reach another device: no remote copies, remote signals or barrier semaphores. Data moves between devices by JAX's collectives and lax.ppermute only.
A program may use at most 256 MiB of HBM per device.

v0:
```python
import jax
import jax.numpy as jnp
from jax import lax
from jax.sharding import PartitionSpec as P

SINK_ITERS = 8


epsilon = 1e-05


def product(left, right):
    return jnp.dot(left, right, preferred_element_type=jnp.float32)


def rms_scale(values):
    return lax.rsqrt(jnp.mean(values * values, axis=-1, keepdims=True) + epsilon)


def causal_conv(values, segment, kernel, offset):
    taps = kernel.shape[0]
    length = values.shape[0]
    result = offset[None, :] + kernel[taps - 1][None, :] * values
    for delay in range(1, taps):
        moved = jnp.concatenate(
            [jnp.zeros((delay, values.shape[1]), values.dtype), values[: length - delay]], axis=0
        )
        moved_seg = jnp.concatenate([jnp.full((delay,), -1, jnp.int32), segment[: length - delay]])
        same = (moved_seg == segment).astype(values.dtype)
        result = result + kernel[taps - 1 - delay][None, :] * moved * same[:, None]
    return result


def combine_pair(earlier, later):
    return (earlier[0] * later[0], later[0] * earlier[1] + later[1])


def mixer_core(activity, gate_z, step_pre, in_b, in_c, step_bias, decay_log, skip_gain, persist):
    step_size = jax.nn.softplus(step_pre + step_bias[None, :])
    decay_rates = -jnp.exp(decay_log)
    positions, channels = step_size.shape
    states_width = decay_rates.shape[0]
    block_len = 16
    block_count = positions // block_len

    def shaped(values):
        return values.reshape(block_count, block_len, values.shape[-1])

    def advance(memory, pieces):
        step_block, act_block, b_block, c_block, keep_block = pieces
        decays = jnp.exp(step_block[:, None, :] * decay_rates[None, :, :]) * keep_block[:, :, None]
        inputs = (step_block * act_block)[:, None, :] * b_block[:, :, None]
        factor, offset = lax.associative_scan(combine_pair, (decays, inputs), axis=0)
        states = factor * memory[None] + offset
        return (states[-1], jnp.sum(c_block[:, :, None] * states, axis=1))

    initial = jnp.zeros((states_width, channels), jnp.float32)
    _, outputs = lax.scan(
        advance,
        initial,
        (
            shaped(step_size),
            shaped(activity),
            shaped(in_b),
            shaped(in_c),
            persist.reshape(block_count, block_len, 1),
        ),
    )
    outputs = outputs.reshape(positions, channels)
    return (outputs + skip_gain[None, :] * activity) * jax.nn.silu(gate_z)


def local(
    tokens,
    cotangent,
    seq_lengths,
    routes,
    mixer_gain,
    proj_x,
    proj_z,
    conv_weight,
    conv_bias,
    state_proj,
    step_proj,
    step_bias,
    decay_log,
    skip_gain,
    out_proj,
    moe_gain,
    router,
    expert_up,
    expert_down,
):
    gathered = (
        lax.all_gather(mixer_gain, "expert", axis=0, tiled=True),
        lax.all_gather(proj_x, "expert", axis=1, tiled=True),
        lax.all_gather(proj_z, "expert", axis=1, tiled=True),
        lax.all_gather(conv_weight, "expert", axis=1, tiled=True),
        lax.all_gather(conv_bias, "expert", axis=0, tiled=True),
        lax.all_gather(state_proj, "expert", axis=0, tiled=True),
        lax.all_gather(step_proj, "expert", axis=1, tiled=True),
        lax.all_gather(step_bias, "expert", axis=0, tiled=True),
        lax.all_gather(decay_log, "expert", axis=1, tiled=True),
        lax.all_gather(skip_gain, "expert", axis=0, tiled=True),
        lax.all_gather(out_proj, "expert", axis=0, tiled=True),
        lax.all_gather(moe_gain, "expert", axis=0, tiled=True),
        lax.all_gather(router, "expert", axis=0, tiled=True),
    )
    (
        gain_one,
        weight_x,
        weight_z,
        conv_full,
        conv_shift,
        state_full,
        step_full,
        step_shift,
        decay_full,
        skip_full,
        out_full,
        gain_two,
        router_full,
    ) = gathered
    positions = tokens.shape[0]
    model_width = tokens.shape[1]
    devices = lax.axis_size("expert")
    expert_count = expert_up.shape[0]
    replicas = devices // expert_count
    capacity = 3 * positions // (2 * expert_count)
    sub_slots = capacity // replicas
    own_expert = lax.axis_index("expert") % expert_count
    rank_width = step_full.shape[0]
    state_width = decay_full.shape[0]
    places = jnp.arange(positions, dtype=jnp.int32)
    first = seq_lengths[0, 0]
    ending = first + seq_lengths[0, 1]
    segment = (places >= first).astype(jnp.int32) + (places >= ending).astype(jnp.int32)
    valid = places < ending
    valid_float = valid.astype(jnp.float32)
    earlier = jnp.concatenate([jnp.full((1,), -1, jnp.int32), segment[:-1]])
    persist = (segment == earlier).astype(jnp.float32)
    resid = tokens.astype(jnp.float32)
    scale_one = rms_scale(resid)
    unit_one = resid * scale_one
    gain_one_f = gain_one.astype(jnp.float32)
    normed = (unit_one * gain_one_f[None, :]).astype(jnp.bfloat16)
    inner_x = product(normed, weight_x)
    inner_z = product(normed, weight_z)
    conv_kernel = conv_full.astype(jnp.float32)
    conv_offset = conv_shift.astype(jnp.float32)
    activity_low = jax.nn.silu(causal_conv(inner_x, segment, conv_kernel, conv_offset)).astype(
        jnp.bfloat16
    )
    activity_f = activity_low.astype(jnp.float32)
    projected = lax.psum(product(activity_low, state_full), "hidden")
    rank_low = projected[:, :rank_width].astype(jnp.bfloat16)
    in_b = projected[:, rank_width : rank_width + state_width]
    in_c = projected[:, rank_width + state_width :]
    step_pre = product(rank_low, step_full)
    step_bias_f = step_shift.astype(jnp.float32)
    decay_f = decay_full.astype(jnp.float32)
    skip_f = skip_full.astype(jnp.float32)

    def core_fn(activity, gate_z, pre_step, basis_b, basis_c, bias_step, decay_values, skip_values):
        return mixer_core(
            activity,
            gate_z,
            pre_step,
            basis_b,
            basis_c,
            bias_step,
            decay_values,
            skip_values,
            persist,
        )

    gated, core_back = jax.vjp(
        core_fn, activity_f, inner_z, step_pre, in_b, in_c, step_bias_f, decay_f, skip_f
    )
    mixed = gated.astype(jnp.bfloat16)
    branch = lax.psum(product(mixed, out_full), "hidden")
    hidden_res = resid + branch
    scale_two = rms_scale(hidden_res)
    unit_two = hidden_res * scale_two
    gain_two_f = gain_two.astype(jnp.float32)
    normed_two = (unit_two * gain_two_f[None, :]).astype(jnp.bfloat16)
    router_logits = product(normed_two, router_full)
    start_weights = jnp.exp(router_logits)
    weights = start_weights
    history = []
    for sweep_index in range(SINK_ITERS):
        columns = lax.psum(jnp.sum(weights * valid_float[:, None], axis=0), "expert")
        scaled = weights / columns[None, :]
        row_sums = jnp.sum(scaled, axis=1, keepdims=True)
        weights = scaled / row_sums
        history.append((columns, scaled, row_sums, weights))
    expert_ids = jnp.arange(expert_count, dtype=jnp.int32)
    route_vec = routes[:, 0]
    onehot = (route_vec[:, None] == expert_ids[None, :]).astype(jnp.float32)
    gate_values = expert_count * jnp.sum(weights * onehot, axis=1)
    member = ((route_vec[:, None] == expert_ids[None, :]) & valid[:, None]).astype(jnp.int32)
    before = jnp.cumsum(member, axis=0) - member
    slot = jnp.sum(before * member, axis=1)
    placed = (
        slot // sub_slots * (expert_count * sub_slots) + route_vec * sub_slots + slot % sub_slots
    )
    target = jnp.where(valid, placed, -1)
    slot_ids = jnp.arange(devices * sub_slots, dtype=jnp.int32)
    picker = (slot_ids[:, None] == target[None, :]).astype(jnp.bfloat16)
    safe_target = jnp.maximum(target, 0)
    sent = product(picker, normed_two).astype(jnp.bfloat16).reshape(devices, sub_slots, model_width)
    arrived = lax.all_to_all(sent, "expert", split_axis=0, concat_axis=0, tiled=True).reshape(
        devices * sub_slots, model_width
    )
    up_weight = lax.dynamic_index_in_dim(expert_up, own_expert, 0, keepdims=False)
    down_weight = lax.dynamic_index_in_dim(expert_down, own_expert, 0, keepdims=False)
    pre_act = product(arrived, up_weight)
    active_f, gelu_back = jax.vjp(jax.nn.gelu, pre_act)
    active = active_f.astype(jnp.bfloat16)
    partial_value = product(active, down_weight)
    returned_back = lax.all_to_all(
        partial_value.reshape(devices, sub_slots, model_width),
        "expert",
        split_axis=0,
        concat_axis=0,
        tiled=True,
    )
    per_token = jnp.take(
        returned_back.reshape(devices * sub_slots, model_width), safe_target, axis=0
    )
    returned = lax.psum(per_token, "hidden").astype(jnp.bfloat16)
    returned_f = returned.astype(jnp.float32)
    layer_out = (valid_float[:, None] * (hidden_res + gate_values[:, None] * returned_f)).astype(
        jnp.bfloat16
    )
    grad_out = cotangent.astype(jnp.float32) * valid_float[:, None]
    grad_gate = jnp.sum(grad_out * returned_f, axis=1)
    grad_ret = (gate_values[:, None] * grad_out).astype(jnp.bfloat16)
    grad_sent = (
        product(picker, grad_ret).astype(jnp.bfloat16).reshape(devices, sub_slots, model_width)
    )
    grad_rows = lax.all_to_all(
        grad_sent, "expert", split_axis=0, concat_axis=0, tiled=True
    ).reshape(devices * sub_slots, model_width)
    grad_active = jnp.einsum(
        "rd,fd->rf", grad_rows, down_weight, preferred_element_type=jnp.float32
    )
    down_grad = jnp.einsum("rf,rd->fd", active, grad_rows, preferred_element_type=jnp.float32)
    grad_pre = gelu_back(grad_active)[0].astype(jnp.bfloat16)
    up_grad = jnp.einsum("rd,rf->df", arrived, grad_pre, preferred_element_type=jnp.float32)
    grad_in_part = jnp.einsum("rf,df->rd", grad_pre, up_weight, preferred_element_type=jnp.float32)
    grad_back = lax.all_to_all(
        grad_in_part.reshape(devices, sub_slots, model_width),
        "expert",
        split_axis=0,
        concat_axis=0,
        tiled=True,
    )
    grad_token = jnp.take(grad_back.reshape(devices * sub_slots, model_width), safe_target, axis=0)
    grad_low = lax.psum(grad_token, "hidden").astype(jnp.bfloat16)
    grad_expert_in = grad_low.astype(jnp.float32) * valid_float[:, None]
    grad_weights = expert_count * grad_gate[:, None] * onehot
    for sweep_index in range(SINK_ITERS - 1, -1, -1):
        columns, scaled, row_sums, result = history[sweep_index]
        grad_scaled = (
            grad_weights - jnp.sum(grad_weights * result, axis=1, keepdims=True)
        ) / row_sums
        column_term = lax.psum(jnp.sum(grad_scaled * scaled, axis=0), "expert")
        grad_weights = (grad_scaled - valid_float[:, None] * column_term[None, :]) / columns[
            None, :
        ]
    grad_logits = (grad_weights * start_weights).astype(jnp.bfloat16)
    router_grad = jnp.einsum(
        "td,te->de", normed_two, grad_logits, preferred_element_type=jnp.float32
    )
    grad_normed_two = (
        jnp.einsum("te,de->td", grad_logits, router_full, preferred_element_type=jnp.float32)
        + grad_expert_in
    )
    gain_two_grad = jnp.sum(grad_normed_two * unit_two, axis=0)
    grad_unit_two = grad_normed_two * gain_two_f[None, :]
    grad_hidden = grad_out + scale_two * (
        grad_unit_two - unit_two * jnp.mean(grad_unit_two * unit_two, axis=-1, keepdims=True)
    )
    grad_branch = grad_hidden.astype(jnp.bfloat16)
    out_grad = jnp.einsum("tc,td->cd", mixed, grad_branch, preferred_element_type=jnp.float32)
    grad_mixed = jnp.einsum("td,cd->tc", grad_branch, out_full, preferred_element_type=jnp.float32)
    grad_act_scan, grad_z, grad_step_pre, grad_b, grad_c, step_bias_grad, decay_grad, skip_grad = (
        core_back(grad_mixed)
    )
    grad_step_low = grad_step_pre.astype(jnp.bfloat16)
    step_proj_grad = jnp.einsum(
        "tr,tc->rc", rank_low, grad_step_low, preferred_element_type=jnp.float32
    )
    grad_rank = jnp.einsum(
        "tc,rc->tr", grad_step_low, step_full, preferred_element_type=jnp.float32
    )
    grad_projected = lax.psum(jnp.concatenate([grad_rank, grad_b, grad_c], axis=1), "hidden")
    grad_proj_low = grad_projected.astype(jnp.bfloat16)
    state_grad = jnp.einsum(
        "tc,tk->ck", activity_low, grad_proj_low, preferred_element_type=jnp.float32
    )
    grad_activity = grad_act_scan + jnp.einsum(
        "tk,ck->tc", grad_proj_low, state_full, preferred_element_type=jnp.float32
    )

    def conv_fn(values, kernel, offset):
        return jax.nn.silu(causal_conv(values, segment, kernel, offset))

    _, conv_back = jax.vjp(conv_fn, inner_x, conv_kernel, conv_offset)
    grad_inner_x, conv_weight_grad, conv_bias_grad = conv_back(grad_activity)
    grad_x_low = grad_inner_x.astype(jnp.bfloat16)
    grad_z_low = grad_z.astype(jnp.bfloat16)
    proj_x_grad = jnp.einsum("td,tc->dc", normed, grad_x_low, preferred_element_type=jnp.float32)
    proj_z_grad = jnp.einsum("td,tc->dc", normed, grad_z_low, preferred_element_type=jnp.float32)
    grad_normed_part = jnp.einsum(
        "tc,dc->td", grad_x_low, weight_x, preferred_element_type=jnp.float32
    ) + jnp.einsum("tc,dc->td", grad_z_low, weight_z, preferred_element_type=jnp.float32)
    grad_normed = lax.psum(grad_normed_part, "hidden")
    gain_one_grad = jnp.sum(grad_normed * unit_one, axis=0)
    grad_unit_one = grad_normed * gain_one_f[None, :]
    tokens_grad = grad_hidden + scale_one * (
        grad_unit_one - unit_one * jnp.mean(grad_unit_one * unit_one, axis=-1, keepdims=True)
    )
    own_pick = (expert_ids == own_expert).astype(jnp.float32)
    up_placed = own_pick[:, None, None] * up_grad[None]
    down_placed = own_pick[:, None, None] * down_grad[None]
    shares = (
        lax.psum_scatter(gain_one_grad, "expert", scatter_dimension=0, tiled=True),
        lax.psum_scatter(proj_x_grad, "expert", scatter_dimension=1, tiled=True),
        lax.psum_scatter(proj_z_grad, "expert", scatter_dimension=1, tiled=True),
        lax.psum_scatter(conv_weight_grad, "expert", scatter_dimension=1, tiled=True),
        lax.psum_scatter(conv_bias_grad, "expert", scatter_dimension=0, tiled=True),
        lax.psum_scatter(state_grad, "expert", scatter_dimension=0, tiled=True),
        lax.psum_scatter(step_proj_grad, "expert", scatter_dimension=1, tiled=True),
        lax.psum_scatter(step_bias_grad, "expert", scatter_dimension=0, tiled=True),
        lax.psum_scatter(decay_grad, "expert", scatter_dimension=1, tiled=True),
        lax.psum_scatter(skip_grad, "expert", scatter_dimension=0, tiled=True),
        lax.psum_scatter(out_grad, "expert", scatter_dimension=0, tiled=True),
        lax.psum_scatter(gain_two_grad, "expert", scatter_dimension=0, tiled=True),
        lax.psum_scatter(router_grad, "expert", scatter_dimension=0, tiled=True),
        lax.psum_scatter(up_placed, "expert", scatter_dimension=1, tiled=True),
        lax.psum_scatter(down_placed, "expert", scatter_dimension=2, tiled=True),
    )
    return (
        layer_out,
        tokens_grad,
        shares[0],
        shares[1],
        shares[2],
        shares[3],
        shares[4],
        shares[5],
        shares[6],
        shares[7],
        shares[8],
        shares[9],
        shares[10],
        shares[11],
        shares[12],
        shares[13],
        shares[14],
    )


def solution(mesh):
    in_specs = (
        P("expert", None),
        P("expert", None),
        P("expert", None),
        P("expert", None),
        P("expert"),
        P(None, ("expert", "hidden")),
        P(None, ("expert", "hidden")),
        P(None, ("expert", "hidden")),
        P(("expert", "hidden")),
        P(("expert", "hidden"), None),
        P(None, ("expert", "hidden")),
        P(("expert", "hidden")),
        P(None, ("expert", "hidden")),
        P(("expert", "hidden")),
        P(("expert", "hidden"), None),
        P("expert"),
        P("expert", None),
        P(None, None, "hidden"),
        P(None, "hidden", None),
    )
    out_specs = (
        P("expert", None),
        P("expert", None),
        P("expert"),
        P(None, ("expert", "hidden")),
        P(None, ("expert", "hidden")),
        P(None, ("expert", "hidden")),
        P(("expert", "hidden")),
        P(("expert", "hidden"), None),
        P(None, ("expert", "hidden")),
        P(("expert", "hidden")),
        P(None, ("expert", "hidden")),
        P(("expert", "hidden")),
        P(("expert", "hidden"), None),
        P("expert"),
        P("expert", None),
        P(None, "expert", "hidden"),
        P(None, "hidden", "expert"),
    )
    return jax.shard_map(local, mesh=mesh, in_specs=in_specs, out_specs=out_specs, check_vma=False)
```

profile of v0, /device:TPU:0, one launch (start us, length us, event | category | flops | bytes accessed | tf_op | source)
XLA Modules:
  0.0 3421.7 jit_solution(11133576471350222730)
XLA Ops:
  14.8 39.3 %all-reduce.81 = (bf16[576]{0:T(1024)(128)(2,1)S(1)}, bf16[1152]{0:T(1024)(128)(2,1)S(1)}, bf16[576]{0:T(1024)(128)(2,1)S(1)}, bf16[576]{0:T(1024)(128)(2,1)S(1)}, bf16[1152]{0:T(1024)(128)(2,1)S(1)}) all-reduce(bf16[576]{0:T(1024)(128)(2,1)S(1)} %dynamic-update-slice.2, ...), channel_id=1, replica_groups=mesh['expert'=8,'hidden'=4] {'expert'}, use_global_device_ids=true, to_apply=%add.65 | all-reduce | flops 4032 | bytes 16128
  73.4 30.8 all_gather.43
  114.4 30.6 all_gather.44
  145.8 30.5 all-gather.1
  187.4 807.8 %while.97 = (s32[]{:T(128)}, f32[16,576]{1,0:T(8,128)}, f32[16,16,576]{2,1,0:T(8,128)}, f32[16,16,1,576]{3,2,1,0:T(1,128)}, f32[16,16,16,576]{3,2,1,0:T(8,128)},...) while((s32[]{:T(128)}, f32[16,576]{1,0:T(8,128)}, ...), condition=%wide.region_4.5_spmd, body=%wide.region_2.4_spmd.sunk | while | flops 3124226 | bytes 41253696 | solution.py:58
  1005.1 34.4 %all-reduce.91.cloned.1.call-done = f32[256,1152]{1,0:T(8,128)} async-done(((f32[256,1152]{1,0:T(8,128)}), f32[256,1152]{1,0:T(8,128)}) %all-reduce.91.cloned.1.call-update) | async-done | bytes 1179664 | tf_op jit(solution)/shard_map/psum | solution.py:181
  1048.1 42.7 %all-gather.2 = bf16[8,144,8]{1,2,0:T(8,128)(2,1)S(1)} all-gather(bf16[1,144,8]{1,2,0:T(8,128)(2,1)S(1)} %bitcast.470), channel_id=1, replica_groups=mesh['expert'=8,'hidden'=4] {'expert'}, dimensions={0}, use_global_device_ids=true | all-gather | bytes 20736 | tf_op jit(solution)/shard_map/all_gather | solution.py:107
  1103.9 38.5 %psum.156 = f32[8]{0:T(128)} all-reduce(f32[8]{0:T(128)S(1)} %get-tuple-element.1941), channel_id=1, replica_groups=mesh['expert'=8,'hidden'=4] {'expert'}, use_global_device_ids=true, to_apply=%region_8.9 | all-reduce | flops 8 | bytes 64 | tf_op jit(solution)/shard_map/psum | solution.py:192
  1144.5 24.9 psum.157
  1173.4 17.8 psum.158
  1195.0 19.8 psum.159
  1240.5 19.8 psum.161
  1264.3 17.8 psum.162
  1286.2 19.7 psum.163
  1311.7 26.1 all-reduce.96
  1342.7 25.9 all_to_all.20
  1381.3 43.2 %psum.165 = f32[8]{0:T(128)} all-reduce(f32[8]{0:T(128)} %multiply_reduce_fusion.27), channel_id=1, replica_groups=mesh['expert'=8,'hidden'=4] {'expert'}, use_global_device_ids=true, to_apply=%region_39.41 | all-reduce | flops 8 | bytes 64 | tf_op jit(solution)/shard_map/psum | solution.py:268
  1427.5 25.3 psum.166
  1476.4 19.8 psum.168
  1499.2 17.8 psum.169
  1519.8 19.7 psum.170
  1562.9 19.7 psum.172
  1588.6 26.6 all-reduce.97
  1625.7 472.9 %while.98 = (s32[]{:T(128)}, f32[16,576]{1,0:T(8,128)}, f32[16,576]{1,0:T(8,128)}, f32[16,16,576]{2,1,0:T(8,128)}, f32[16,16,576]{2,1,0:T(8,128)}, /*index=5*/f3...) while((s32[]{:T(128)}, f32[16,576]{1,0:T(8,128)}, ...), condition=%wide.region_70.72_spmd.clone, body=%wide.region_63.71_spmd.clone.sunk | while | flops 5851652 | bytes 44768176 | solution.py:58
  2159.0 25.7 all-reduce.95.cloned.1.call-done
  2186.3 37.4 %all-reduce.93.cloned.1.call-done = f32[256,1152]{1,0:T(8,128)} async-done(((f32[256,1152]{1,0:T(8,128)}), f32[256,1152]{1,0:T(8,128)}) %all-reduce.93.cloned.1.call-update) | async-done | bytes 1179664 | tf_op jit(solution)/shard_map/psum | solution.py:319
  2225.5 38.2 %all-reduce.80 = (f32[1152]{0:T(1024)S(1)}, f32[4,576]{1,0:T(4,128)S(1)}, f32[576]{0:T(1024)S(1)}, f32[576]{0:T(1024)S(1)}, f32[16,576]{1,0:T(8,128)S(1)}, /*index=5*/f32[576]{0:T(1024)S(1)}, f32[1152]{0:T(1024)S(1)}) all-reduce(f32[1152]{0:T(1024)S(1)} %get-tuple-element.1606, ...), channel_id=2, replica_groups=mesh['expert'=8,'hidden'=4] {'expert'}, use_global_device_ids=true, to_apply=%region_75.77.clone | all-reduce | flops 15552 | bytes 124416
  2286.8 74.3 %reduce-scatter.33.cloned.1.call-done = f32[72,1152]{1,0:T(8,128)} async-done(((f32[576,1152]{1,0:T(8,128)}), f32[72,1152]{1,0:T(8,128)}) %reduce-scatter.33.cloned.1.call-update) | async-done | bytes 331792
  2361.1 74.0 %reduce-scatter.27.cloned.1.call-done = f32[1152,72]{0,1:T(8,128)} async-done(((f32[1152,576]{0,1:T(8,128)}), f32[1152,72]{0,1:T(8,128)}) %reduce-scatter.27.cloned.1.call-update) | async-done | bytes 331792
  2435.1 74.6 %reduce-scatter.29.cloned.1.call-done = f32[1152,72]{0,1:T(8,128)} async-done(((f32[1152,576]{0,1:T(8,128)}), f32[1152,72]{0,1:T(8,128)}) %reduce-scatter.29.cloned.1.call-update) | async-done | bytes 331792
  2509.6 452.3 %reduce-scatter.23.cloned.1.call-done = f32[8,768,144]{1,2,0:T(8,128)} async-done(((f32[8,768,1152]{1,2,0:T(8,128)}), f32[8,768,144]{1,2,0:T(8,128)}) %reduce-scatter.23.cloned.1.call-update) | async-done | bytes 3538960 | tf_op jit(solution)/shard_map/reduce_scatter | solution.py:343
  2962.0 452.8 %reduce-scatter.21.cloned.1.call-done = f32[8,144,768]{2,1,0:T(8,128)} async-done(((f32[8,1152,768]{2,1,0:T(8,128)}), f32[8,144,768]{2,1,0:T(8,128)}) %reduce-scatter.21.cloned.1.call-update) | async-done | bytes 3538960 | tf_op jit(solution)/shard_map/reduce_scatter | solution.py:342
  (3392 shorter events, 1570.7 us)
Async XLA Ops:
  7.2 100.5 %all-gather.7.cloned.1.call-start = ((), (), s32[]{:S(2)}) async-start(), calls=%async_computation.11 | async-start | bytes 1492992 | tf_op jit(solution)/shard_map/all_gather | solution.py:96
  7.9 172.4 %all-reduce.89.cloned.1.call-start = ((), (), s32[]{:S(2)}) async-start(), calls=%async_computation.12 | async-start | bytes 212992 | tf_op jit(solution)/shard_map/psum | solution.py:155
  54.1 942.4 %copy-start.75 = (f32[1152]{0:T(1024)}, f32[1152]{0:T(1024)S(1)}, u32[]{:S(2)}) copy-start(f32[1152]{0:T(1024)S(1)} %convert_element_type.176) | copy-start | bytes 13828
  107.6 888.9 %copy-start.102 = (f32[256]{0:T(256)}, f32[256]{0:T(256)S(1)}, u32[]{:S(2)}) copy-start(f32[256]{0:T(256)S(1)} %add_rsqrt_fusion.1) | copy-start | bytes 3076
  109.9 35.8 %copy-start.123 = (bf16[16,72]{1,0:T(8,128)(2,1)S(1)}, bf16[16,72]{1,0:T(8,128)(2,1)}, u32[]{:S(2)}) copy-start(bf16[16,72]{1,0:T(8,128)(2,1)} %param.37) | copy-start | bytes 6916
  111.7 68.6 %copy-start.38 = (bf16[256,576]{0,1:T(8,128)(2,1)}, bf16[256,576]{0,1:T(8,128)(2,1)S(1)}, u32[]{:S(2)}) copy-start(bf16[256,576]{0,1:T(8,128)(2,1)S(1)} %get-tuple-element.1839) | copy-start | bytes 884740
  112.6 883.9 %all-gather.9.cloned.1.call-start = ((), (), s32[]{:S(2)}) async-start(), calls=%async_computation.13 | async-start | bytes 1492992 | tf_op jit(solution)/shard_map/all_gather | solution.py:97
  113.4 886.4 %all-gather.11.cloned.1.call-start = ((), (), s32[]{:S(2)}) async-start(), calls=%async_computation.14 | async-start | bytes 1492992 | tf_op jit(solution)/shard_map/all_gather | solution.py:105
  114.0 925.6 %all-reduce.91.cloned.1.call-start = ((), (), s32[]{:S(2)}) async-start(), calls=%async_computation.15 | async-start | bytes 2359296 | tf_op jit(solution)/shard_map/psum | solution.py:181
  145.0 37.6 %copy-start.66 = (bf16[72,576]{0,1:T(8,128)(2,1)}, bf16[72,576]{0,1:T(8,128)(2,1)S(1)}, u32[]{:S(2)}) copy-start(bf16[72,576]{0,1:T(8,128)(2,1)S(1)} %all_gather.44) | copy-start | bytes 248836
  179.3 817.2 %copy-start.108 = (f32[576]{0:T(1024)}, f32[576]{0:T(1024)S(1)}, u32[]{:S(2)}) copy-start(f32[576]{0:T(1024)S(1)} %convert_element_type.190) | copy-start | bytes 6916
  1003.6 36.0 %copy-start.13 = (bf16[256,1152]{1,0:T(8,128)(2,1)S(1)}, bf16[256,1152]{1,0:T(8,128)(2,1)}, u32[]{:S(2)}) copy-start(bf16[256,1152]{1,0:T(8,128)(2,1)} %param.25) | copy-start | bytes 1769476
  1003.6 37.4 %copy-start.83 = (f32[1152]{0:T(1024)}, f32[1152]{0:T(1024)S(1)}, u32[]{:S(2)}) copy-start(f32[1152]{0:T(1024)S(1)} %convert_element_type.192) | copy-start | bytes 13828
  1005.1 36.1 %copy-start.110 = (s32[256]{0:T(256)}, s32[256]{0:T(256)S(1)}, u32[]{:S(2)}) copy-start(s32[256]{0:T(256)S(1)} %get-tuple-element.1818) | copy-start | bytes 3076
  1042.6 48.9 %all-to-all-start = ((bf16[8,48,1152]{2,1,0:T(8,128)(2,1)}), bf16[8,48,1152]{2,1,0:T(8,128)(2,1)S(1)}, u32[]{:S(2)}, u32[]{:S(2)}) async-start(bf16[8,48,1152]{2,1,0:T(8,128)(2,1)} %bitcast.57), calls=%async_computation | async-start | bytes 1769472 | tf_op jit(solution)/shard_map/all_to_all | solution.py:212
  1099.2 208.7 %all-to-all-start.1 = ((f32[8,48,1152]{2,1,0:T(8,128)}), f32[8,48,1152]{2,1,0:T(8,128)S(1)}, u32[]{:S(2)}, u32[]{:S(2)}) async-start(f32[8,48,1152]{2,1,0:T(8,128)} %fusion.26), calls=%async_computation.1 | async-start | bytes 3538944 | tf_op jit(solution)/shard_map/all_to_all | solution.py:221
  1340.9 27.7 copy-start.121
  1340.9 27.7 copy-start.125
  1376.3 208.4 %all-to-all-start.3 = ((f32[8,48,1152]{2,1,0:T(8,128)}), f32[8,48,1152]{2,1,0:T(8,128)S(1)}, u32[]{:S(2)}, u32[]{:S(2)}) async-start(f32[8,48,1152]{2,1,0:T(8,128)} %fusion.24), calls=%async_computation.3 | async-start | bytes 3538944 | tf_op jit(solution)/shard_map/all_to_all | solution.py:252
  1379.9 777.5 %reduce-scatter.25.cloned.1.call-start = ((), (), s32[]{:S(2)}) async-start(), calls=%async_computation.19 | async-start | bytes 663552
  1584.6 600.1 %all-reduce.95.cloned.1.call-start = ((), (), s32[]{:S(2)}) async-start(), calls=%async_computation.20 | async-start | bytes 368640
  2100.1 13.8 copy-start.44
  2100.7 13.4 copy-start.47
  2117.7 106.0 %all-reduce.93.cloned.1.call-start = ((), (), s32[]{:S(2)}) async-start(), calls=%async_computation.16 | async-start | bytes 2359296 | tf_op jit(solution)/shard_map/psum | solution.py:319
  2122.5 164.3 %reduce-scatter.31.cloned.1.call-start = ((), (), s32[]{:S(2)}) async-start(), calls=%async_computation.23 | async-start | bytes 331776
  2123.5 237.6 %reduce-scatter.33.cloned.1.call-start = ((), (), s32[]{:S(2)}) async-start(), calls=%async_computation.24 | async-start | bytes 2985984
  2126.0 309.1 %reduce-scatter.27.cloned.1.call-start = ((), (), s32[]{:S(2)}) async-start(), calls=%async_computation.21 | async-start | bytes 2985984
  2129.2 380.4 %reduce-scatter.29.cloned.1.call-start = ((), (), s32[]{:S(2)}) async-start(), calls=%async_computation.22 | async-start | bytes 2985984
  2131.8 830.2 %reduce-scatter.23.cloned.1.call-start = ((), (), s32[]{:S(2)}) async-start(), calls=%async_computation.18 | async-start | bytes 31850496 | tf_op jit(solution)/shard_map/reduce_scatter | solution.py:343
  2143.9 1270.9 %reduce-scatter.21.cloned.1.call-start = ((), (), s32[]{:S(2)}) async-start(), calls=%async_computation.17 | async-start | bytes 31850496 | tf_op jit(solution)/shard_map/reduce_scatter | solution.py:342
  2156.1 69.5 %copy-start.100 = (f32[1152]{0:T(1024)S(1)}, f32[1152]{0:T(1024)}, u32[]{:S(2)}) copy-start(f32[1152]{0:T(1024)} %get-tuple-element.1604) | copy-start | bytes 13828
  2223.7 44.4 %copy-start.37 = (f32[256,1152]{1,0:T(8,128)S(1)}, f32[256,1152]{1,0:T(8,128)}, u32[]{:S(2)}) copy-start(f32[256,1152]{1,0:T(8,128)} %all-reduce.93.cloned.1.call-done) | copy-start | bytes 3538948
  (578 other events, 1438.3 us)
Sparse Core Ops, SparseCore 0:
  10.2 45.0 all-gather.6
  112.8 28.0 all-reduce.88
  143.3 44.0 all-gather.8
  189.7 40.8 all-gather.10
  1003.7 35.7 all-reduce.90
  1584.7 58.9 reduce-scatter.24
  2117.8 66.8 all-reduce.94
  2187.2 36.4 all-reduce.92
  2227.9 58.8 reduce-scatter.30
  2291.3 69.6 reduce-scatter.32
  2365.3 69.6 reduce-scatter.26
  2439.6 70.0 reduce-scatter.28
  2514.1 447.7 reduce-scatter.22
  2966.8 447.8 reduce-scatter.20
where the time goes:
time: 3480 us; the launch traced here: 3420 us
  waiting for transfers between devices  1240 us (36%)
  local copies, waits for them, and re-layouts  752 us (22%)
  blocking collectives  677 us (19%)
  other arithmetic  652 us (19%)
  matrix products  50.6 us (1%)
    reduce_scatter x1, waiting for transfers between devices, local(): lax.psum_scatter(up_placed, 'expert', scatter_dimension=1, tiled=True)  453 us
    reduce_scatter x1, waiting for transfers between devices, local(): lax.psum_scatter(down_placed, 'expert', scatter_dimension=2, tiled=True)  452 us
    pad x544, local copies, waits for them, and re-layouts, advance(): lax.associative_scan(combine_pair, (decays, inputs), axis=0)  432 us
    unnamed x20, waiting for transfers between devices  268 us
    mul x208, other arithmetic, combine_pair(): return (earlier[0] * later[0], later[0] * earlier[1] + later[1])  190 us
    psum x8, blocking collectives, local(): column_term = lax.psum(jnp.sum(grad_scaled * scaled, axis=0), 'expert')  181 us
    psum x8, blocking collectives, local(): lax.psum(jnp.sum(weights * valid_float[:, None], axis=0), 'expert')  176 us
    dynamic_update_slice x192, local copies, waits for them, and re-layouts, mixer_core(): lax.scan(advance, initial, (shaped(step_size), shaped(activity), shaped(i...  140 us
  transfers between devices with their start and end apart: 17, of which 9 were waited for; matrix products, arithmetic and copies ran while one was open for 41% of the time, Pallas kernels for 0%

commit v1 on v0

v1 whole, which is shorter than its diff:
```python
import jax
import jax.numpy as jnp
from jax import lax
from jax.experimental import pallas as pl
from jax.experimental.pallas import tpu as pltpu
from jax.sharding import PartitionSpec as P

SINK_ITERS = 8
GROUP = 8
LANES = 128
ROWS = 8
FAR = 1e30
LOG2E = 1.4426950408889634
epsilon = 1e-05
f32 = jnp.float32
bf16 = jnp.bfloat16


def product(left, right):
    return jnp.dot(left, right, preferred_element_type=f32)


def ein(spec, left, right):
    return jnp.einsum(spec, left, right, preferred_element_type=f32)


def rms_scale(values):
    return lax.rsqrt(jnp.mean(values * values, axis=-1, keepdims=True) + epsilon)


def swap(values, axis, bits):
    size = lax.axis_size(axis)
    return lax.ppermute(values, axis, [(i, i ^ bits) for i in range(size)])


def gather_doubling(values, axis):
    held = values[None]
    bits = 1
    while bits < lax.axis_size(axis):
        held = jnp.concatenate([held, swap(held, axis, bits)])
        bits *= 2
    return held


def gather_direct(values, axis):
    size = lax.axis_size(axis)
    if size > GROUP:
        return gather_doubling(values, axis)
    return jnp.stack([values] + [swap(values, axis, r) for r in range(1, size)])


def scatter_sum(values, axis):
    size = values.shape[0]
    while size > 1:
        size //= 2
        values = values[:size] + swap(values[size:].astype(bf16), axis, size).astype(f32)
    return values[0]


def exchange(values, axis):
    size = values.shape[0]
    if size > GROUP:
        order = jnp.arange(size) ^ lax.axis_index(axis)
        moved = lax.all_to_all(jnp.take(values, order, axis=0), axis, 0, 0, tiled=True)
        return jnp.take(moved, order, axis=0)
    return jnp.stack([values[0]] + [swap(values[r], axis, r) for r in range(1, size)])


def hidden_sum(values):
    half = values.shape[0] // 2
    place = lax.axis_index("hidden") % 2
    kept = lax.dynamic_slice_in_dim(values, place * half, half, 0)
    given = lax.dynamic_slice_in_dim(values, (1 - place) * half, half, 0)
    total = kept.astype(bf16).astype(f32) + swap(given.astype(bf16), "hidden", 1).astype(f32)
    low = total.astype(bf16)
    low = (low.astype(f32) + swap(low, "hidden", 2).astype(f32)).astype(bf16)
    other = swap(low, "hidden", 1)
    return jnp.where(
        place == 0, jnp.concatenate([low, other]), jnp.concatenate([other, low])
    ).astype(f32)


def hidden_sum_small(values):
    values = values + swap(values, "hidden", 1)
    return values + swap(values, "hidden", 2)


def gather_tokens(values, base):
    place = lax.axis_index("hidden")
    size = values.shape[0] // 4
    own = lax.dynamic_slice_in_dim(values, place * size, size, 0)
    if base > 0:
        own = swap(own, "expert", base)
    group = min(lax.axis_size("expert"), GROUP)
    held = jnp.stack([own] + [swap(own, "expert", r) for r in range(1, group)])
    far = swap(held, "hidden", 2)
    near = swap(held, "hidden", 1)
    both = swap(far, "hidden", 1)
    count = held.shape[0]
    whole = jnp.zeros((count, 4 * size, values.shape[1]), values.dtype)
    for r, piece in ((0, held), (1, near), (2, far), (3, both)):
        whole = lax.dynamic_update_slice(whole, piece, (0, (place ^ r) * size, 0))
    return whole


def causal_conv(values, segment, kernel, offset):
    taps = kernel.shape[0]
    length = values.shape[0]
    result = offset[None, :] + kernel[taps - 1][None, :] * values
    for delay in range(1, taps):
        moved = jnp.concatenate(
            [jnp.zeros((delay, values.shape[1]), values.dtype), values[: length - delay]], axis=0
        )
        moved_seg = jnp.concatenate([jnp.full((delay,), -1, jnp.int32), segment[: length - delay]])
        same = (moved_seg == segment).astype(values.dtype)
        result = result + kernel[taps - 1 - delay][None, :] * moved * same[:, None]
    return result


def softplus(values):
    return jnp.maximum(values, 0.0) + jnp.log1p(jnp.exp(-jnp.abs(values)))


def sigmoid(values):
    return 1.0 / (1.0 + jnp.exp(-values))


def put(ref, values):
    width = values.shape[1]
    ref[:, :width] = values
    if ref.shape[1] > width:
        ref[:, width:] = jnp.zeros((values.shape[0], ref.shape[1] - width), ref.dtype)


def widen(tile, width):
    return jnp.concatenate([tile] * (width // LANES), axis=1)


def fold(values):
    total = values[:, :LANES]
    for k in range(1, values.shape[1] // LANES):
        total = total + values[:, k * LANES : (k + 1) * LANES]
    return total


def scan_forward_body(
    pre, act, gate, basis_b, basis_c, bias, decay, skip, keep,
    mixed, out, states, far_steps, inputs, rates, sums,
):
    width = far_steps.shape[1]
    channels = pre.shape[1]
    step = softplus(pre[...] + bias[...])
    put(far_steps, jnp.where(keep[...] > 0, step, FAR))
    put(inputs, step * act[...])
    put(rates, -LOG2E * jnp.exp(decay[...]))
    rate = rates[...]

    def block(i, memory):
        base = pl.multiple_of(i * ROWS, ROWS)
        step_rows = far_steps[pl.ds(base, ROWS), :]
        input_rows = inputs[pl.ds(base, ROWS), :]
        rows = []
        for j in range(ROWS):
            factor = jnp.exp2(step_rows[j : j + 1] * rate)
            memory = factor * memory + input_rows[j : j + 1] * widen(basis_b[base + j], width)
            states[base + j] = memory
            rows.append(jnp.sum(widen(basis_c[base + j], width) * memory, axis=0, keepdims=True))
        sums[pl.ds(base, ROWS), :] = jnp.concatenate(rows, axis=0)
        return memory

    lax.fori_loop(0, pre.shape[0] // ROWS, block, jnp.zeros(rate.shape, f32))
    total = sums[:, :channels]
    out[...] = total
    silu = gate[...] * sigmoid(gate[...])
    mixed[...] = ((total + skip[...] * act[...]) * silu).astype(bf16)


def scan_backward_body(
    grad, out, act, gate, pre, bias, decay, skip, keep, basis_b, basis_c, states,
    grad_act, grad_gate, grad_pre, part_b, part_c, grad_bias, grad_decay, grad_skip,
    far_steps, steps, inputs, outer, rates, sum_input, sum_step,
):
    width = far_steps.shape[1]
    channels = pre.shape[1]
    step = softplus(pre[...] + bias[...])
    put(far_steps, jnp.where(keep[...] > 0, step, FAR))
    put(steps, step)
    put(inputs, step * act[...])
    put(rates, -jnp.exp(decay[...]))
    shade = sigmoid(gate[...])
    through = grad[...] * gate[...] * shade
    put(outer, through)
    grad_gate[...] = (
        grad[...]
        * (out[...] + skip[...] * act[...])
        * (shade * (1.0 + gate[...] * (1.0 - shade)))
    ).astype(bf16)
    grad_skip[...] = jnp.sum(through * act[...], axis=0, keepdims=True)
    rate = rates[...]
    quick = rate * LOG2E
    blocks = pre.shape[0] // ROWS

    def block(i, carried):
        later, rate_sum = carried
        base = pl.multiple_of((blocks - 1 - i) * ROWS, ROWS)
        far_rows = far_steps[pl.ds(base, ROWS), :]
        step_rows = steps[pl.ds(base, ROWS), :]
        input_rows = inputs[pl.ds(base, ROWS), :]
        outer_rows = outer[pl.ds(base, ROWS), :]
        input_sums = [None] * ROWS
        step_sums = [None] * ROWS
        for j in reversed(range(ROWS)):
            tile_b = widen(basis_b[base + j], width)
            outside = outer_rows[j : j + 1]
            inside = input_rows[j : j + 1]
            state = states[base + j]
            flow = widen(basis_c[base + j], width) * outside + later
            later = jnp.exp2(far_rows[j : j + 1] * quick) * flow
            part_c[base + j] = fold(outside * state)
            part_b[base + j] = fold(flow * inside)
            input_sums[j] = jnp.sum(flow * tile_b, axis=0, keepdims=True)
            turned = flow * (state - inside * tile_b)
            step_sums[j] = jnp.sum(turned * rate, axis=0, keepdims=True)
            rate_sum = rate_sum + turned * step_rows[j : j + 1]
        sum_input[pl.ds(base, ROWS), :] = jnp.concatenate(input_sums, axis=0)
        sum_step[pl.ds(base, ROWS), :] = jnp.concatenate(step_sums, axis=0)
        return later, rate_sum

    zero = jnp.zeros(rate.shape, f32)
    _, rate_sum = lax.fori_loop(0, blocks, block, (zero, zero))
    grad_decay[...] = (rate_sum * rate)[:, :channels]
    back_input = sum_input[:, :channels]
    grad_act[...] = outer[:, :channels] * skip[...] + back_input * step
    grad_step = (back_input * act[...] + sum_step[:, :channels]) * sigmoid(pre[...] + bias[...])
    grad_pre[...] = grad_step.astype(bf16)
    grad_bias[...] = jnp.sum(grad_step, axis=0, keepdims=True)


def shape_of(*dims):
    return jax.ShapeDtypeStruct(dims, f32)


def scan_forward(pre, act, gate, basis_b, basis_c, bias, decay, skip, keep):
    positions, channels = pre.shape
    entries = decay.shape[0]
    width = -(-channels // LANES) * LANES
    return pl.pallas_call(
        scan_forward_body,
        out_shape=(
            jax.ShapeDtypeStruct((positions, channels), bf16),
            shape_of(positions, channels),
            shape_of(positions, entries, width),
        ),
        scratch_shapes=[
            pltpu.VMEM((positions, width), f32),
            pltpu.VMEM((positions, width), f32),
            pltpu.VMEM((entries, width), f32),
            pltpu.VMEM((positions, width), f32),
        ],
        compiler_params=pltpu.CompilerParams(vmem_limit_bytes=48 * 2**20),
        name="scan_forward",
    )(pre, act, gate, basis_b, basis_c, bias, decay, skip, keep)


def scan_backward(
    grad, out, act, gate, pre, bias, decay, skip, keep, basis_b, basis_c, states
):
    positions, channels = pre.shape
    entries, width = states.shape[1:]
    wide = pltpu.VMEM((positions, width), f32)
    return pl.pallas_call(
        scan_backward_body,
        out_shape=(
            shape_of(positions, channels),
            jax.ShapeDtypeStruct((positions, channels), bf16),
            jax.ShapeDtypeStruct((positions, channels), bf16),
            shape_of(positions, entries, LANES),
            shape_of(positions, entries, LANES),
            shape_of(1, channels),
            shape_of(entries, channels),
            shape_of(1, channels),
        ),
        scratch_shapes=[wide, wide, wide, wide, pltpu.VMEM((entries, width), f32), wide, wide],
        compiler_params=pltpu.CompilerParams(vmem_limit_bytes=56 * 2**20),
        name="scan_backward",
    )(grad, out, act, gate, pre, bias, decay, skip, keep, basis_b, basis_c, states)


def sweeps(start, valid):
    weights = start
    history = []
    for _ in range(SINK_ITERS):
        columns = jnp.sum(jnp.sum(weights * valid, axis=2, keepdims=True), axis=0, keepdims=True)
        scaled = weights / columns
        row_sums = jnp.sum(scaled, axis=1, keepdims=True)
        weights = scaled / row_sums
        history.append((columns, scaled, row_sums, weights))
    return weights, history


def chosen(codes, shape):
    return (lax.broadcasted_iota(jnp.int32, shape, 1).astype(f32) == codes).astype(f32)


def sinkhorn_body(logits, routes, gates):
    start = jnp.exp(logits[...])
    valid = (routes[:, 1:2, :] > 0).astype(f32)
    weights, _ = sweeps(start, valid)
    onehot = chosen(routes[:, 0:1, :], start.shape)
    gates[...] = start.shape[1] * jnp.sum(weights * onehot, axis=1, keepdims=True)


def sinkhorn_back_body(logits, routes, grad_gates, grad_logits):
    start = jnp.exp(logits[...])
    valid = (routes[:, 1:2, :] > 0).astype(f32)
    _, history = sweeps(start, valid)
    onehot = chosen(routes[:, 0:1, :], start.shape)
    grads = start.shape[1] * grad_gates[...] * onehot
    for columns, scaled, row_sums, result in reversed(history):
        grads = (grads - jnp.sum(grads * result, axis=1, keepdims=True)) / row_sums
        term = jnp.sum(jnp.sum(grads * scaled, axis=2, keepdims=True), axis=0, keepdims=True)
        grads = (grads - valid * term) / columns
    grad_logits[...] = (grads * start)[0]


def sinkhorn(logits, routes):
    count, experts, positions = logits.shape
    return pl.pallas_call(
        sinkhorn_body,
        out_shape=shape_of(count, 1, positions),
        compiler_params=pltpu.CompilerParams(vmem_limit_bytes=48 * 2**20),
        name="sinkhorn_forward",
    )(logits, routes)


def sinkhorn_back(logits, routes, grad_gates):
    count, experts, positions = logits.shape
    return pl.pallas_call(
        sinkhorn_back_body,
        out_shape=shape_of(experts, positions),
        compiler_params=pltpu.CompilerParams(vmem_limit_bytes=48 * 2**20),
        name="sinkhorn_backward",
    )(logits, routes, grad_gates)


def expert_grads(picker, rows, grad_rows, up, down, place, block):
    count, slots, _ = picker.shape
    experts, width, _ = up.shape

    def spread(values):
        picked = ein("nst,ntd->nsd", picker, values).astype(bf16)
        picked = picked.reshape(count, experts, slots // experts, width)
        return picked.transpose(1, 0, 2, 3).reshape(experts, count * slots // experts, width)

    arrived = spread(rows)
    arrived_grad = spread(grad_rows)
    active, back = jax.vjp(jax.nn.gelu, ein("erd,edf->erf", arrived, up))
    grad_pre = back(ein("erd,efd->erf", arrived_grad, down))[0].astype(bf16)
    own = lax.dynamic_slice_in_dim(arrived, place * block, block, 2)
    own_grad = lax.dynamic_slice_in_dim(arrived_grad, place * block, block, 2)
    return (
        ein("erd,erf->edf", own, grad_pre),
        ein("erf,erd->efd", active.astype(bf16), own_grad),
    )


def local(
    tokens,
    cotangent,
    seq_lengths,
    routes,
    mixer_gain,
    proj_x,
    proj_z,
    conv_weight,
    conv_bias,
    state_proj,
    step_proj,
    step_bias,
    decay_log,
    skip_gain,
    out_proj,
    moe_gain,
    router,
    expert_up,
    expert_down,
):
    devices = lax.axis_size("expert")
    index = lax.axis_index("expert")
    order = jnp.arange(devices) ^ index
    positions, width = tokens.shape
    block = mixer_gain.shape[0]
    experts = expert_up.shape[0]
    own_channels = proj_x.shape[1]
    channels = devices * own_channels
    rank = step_proj.shape[0]
    entries = decay_log.shape[0]
    taps = conv_weight.shape[0]
    capacity = 3 * positions // (2 * experts)

    places = jnp.arange(positions, dtype=jnp.int32)
    first = seq_lengths[0, 0]
    ending = first + seq_lengths[0, 1]
    segment = (places >= first).astype(jnp.int32) + (places >= ending).astype(jnp.int32)
    valid = places < ending
    valid_float = valid.astype(f32)
    earlier = jnp.concatenate([jnp.full((1,), -1, jnp.int32), segment[:-1]])
    persist = (segment == earlier).astype(f32)

    vectors = jnp.concatenate([mixer_gain[None], moe_gain[None], router.T])
    vectors = jnp.take(gather_doubling(vectors, "expert"), order, axis=0)
    vectors = vectors.transpose(1, 0, 2).reshape(2 + experts, width)
    gain_one = vectors[0].astype(f32)
    gain_two = vectors[1].astype(f32)
    router_full = vectors[2:]
    small = jnp.concatenate(
        [
            conv_weight,
            conv_bias[None],
            step_bias[None],
            skip_gain[None],
            decay_log,
            step_proj,
            state_proj.T,
        ]
    )
    small = gather_doubling(small, "expert").transpose(1, 0, 2).reshape(-1, channels)
    conv_kernel = small[:taps].astype(f32)
    conv_offset = small[taps].astype(f32)
    step_shift = small[taps + 1 : taps + 2].astype(f32)
    skip_full = small[taps + 2 : taps + 3].astype(f32)
    decay_full = small[taps + 3 : taps + 3 + entries].astype(f32)
    step_full = small[taps + 3 + entries : taps + 3 + entries + rank]
    state_full = small[taps + 3 + entries + rank :]
    weight_x = gather_direct(proj_x.T, "expert").reshape(channels, width)
    proj_z, weight_x = lax.optimization_barrier((proj_z, weight_x))
    weight_z = gather_direct(proj_z.T, "expert").reshape(channels, width)
    out_proj, weight_z = lax.optimization_barrier((out_proj, weight_z))
    out_full = gather_direct(out_proj, "expert").reshape(channels, width)
    codes = jnp.stack([routes[:, 0].astype(f32), valid_float])
    codes = gather_doubling(codes, "expert")

    resid = tokens.astype(f32)
    scale_one = rms_scale(resid)
    unit_one = resid * scale_one
    normed = (unit_one * gain_one[None, :]).astype(bf16)
    inner_x = ein("td,cd->tc", normed, weight_x)
    activity_low = jax.nn.silu(causal_conv(inner_x, segment, conv_kernel, conv_offset)).astype(bf16)
    activity = activity_low.astype(f32)
    projected = hidden_sum_small(ein("tc,kc->tk", activity_low, state_full))
    inner_z = ein("td,cd->tc", normed, weight_z)
    rank_low = projected[:, :rank].astype(bf16)
    in_b = projected[:, rank : rank + entries]
    in_c = projected[:, rank + entries :]
    basis_b = jnp.broadcast_to(in_b[:, :, None], (positions, entries, LANES))
    basis_c = jnp.broadcast_to(in_c[:, :, None], (positions, entries, LANES))
    step_pre = product(rank_low, step_full)
    keep = persist[:, None]
    mixed, scanned, states = scan_forward(
        step_pre, activity, inner_z, basis_b, basis_c, step_shift, decay_full, skip_full, keep
    )
    branch = hidden_sum(product(mixed, out_full))
    hidden_res = resid + branch
    scale_two = rms_scale(hidden_res)
    unit_two = hidden_res * scale_two
    normed_two = (unit_two * gain_two[None, :]).astype(bf16)
    logits = gather_doubling(ein("ed,td->et", router_full, normed_two), "expert")
    gates = sinkhorn(logits, codes)
    gate_values = gates[0, 0]

    prior = (places[:, None] > places[None, :]).astype(bf16)
    slot_ids = jnp.arange(experts * capacity, dtype=f32)

    def pick(some):
        member = (some[:, 0, :, None] == jnp.arange(experts, dtype=f32)) & (some[:, 1, :, None] > 0)
        member = member.astype(bf16)
        slot = jnp.sum(ein("pt,nte->npe", prior, member) * member.astype(f32), axis=2)
        target = jnp.where(some[:, 1] > 0, some[:, 0] * capacity + slot, -1.0)
        return (slot_ids[None, :, None] == target[:, None, :]).astype(bf16)

    group = min(devices, GROUP)
    picker = pick(codes[:group])
    own_picker = picker[0]

    def spread(values):
        return product(own_picker, values).astype(bf16).reshape(experts, capacity, width)

    def collect(values):
        return ein("st,sd->td", own_picker, values.astype(bf16).reshape(-1, width)).astype(bf16)

    sent = spread(normed_two)
    sent_grad = spread(cotangent)
    active, gelu_back = jax.vjp(jax.nn.gelu, ein("erd,edf->erf", sent, expert_up))
    active_low = active.astype(bf16)
    plain_active = ein("erd,efd->erf", sent_grad, expert_down)
    plain_pre = gelu_back(plain_active)[0].astype(bf16)
    gate_slots = jnp.sum(active_low.astype(f32) * plain_active, axis=2).reshape(-1)
    grad_gate = jnp.sum(own_picker.astype(f32) * gate_slots[:, None], axis=0)
    grad_gate = gather_doubling(hidden_sum_small(grad_gate[None]), "expert")
    plain_in = hidden_sum(collect(ein("erf,edf->erd", plain_pre, expert_up)))
    returned = hidden_sum(collect(ein("erf,efd->erd", active_low, expert_down)))
    layer_out = (valid_float[:, None] * (hidden_res + gate_values[:, None] * returned)).astype(bf16)
    grad_expert_in = plain_in * (gate_values * valid_float)[:, None]

    grad_logits = sinkhorn_back(logits, codes, grad_gate).astype(bf16)
    router_grad = ein("td,et->ed", normed_two, grad_logits)
    grad_normed_two = ein("et,ed->td", grad_logits, router_full) + grad_expert_in
    grad_out = cotangent.astype(f32) * valid_float[:, None]
    gain_two_grad = jnp.sum(grad_normed_two * unit_two, axis=0)
    grad_unit_two = grad_normed_two * gain_two[None, :]
    grad_hidden = grad_out + scale_two * (
        grad_unit_two - unit_two * jnp.mean(grad_unit_two * unit_two, axis=-1, keepdims=True)
    )
    grad_branch = grad_hidden.astype(bf16)
    out_grad = ein("tc,td->cd", mixed, grad_branch).reshape(devices, own_channels, width)
    out_grad = scatter_sum(out_grad, "expert")
    grad_mixed = ein("td,cd->tc", grad_branch, out_full)
    (
        grad_act_scan,
        grad_z_low,
        grad_step_low,
        part_b,
        part_c,
        step_bias_grad,
        decay_grad,
        skip_grad,
    ) = scan_backward(
        grad_mixed,
        scanned,
        activity,
        inner_z,
        step_pre,
        step_shift,
        decay_full,
        skip_full,
        keep,
        basis_b,
        basis_c,
        states,
    )
    step_proj_grad = ein("tr,tc->rc", rank_low, grad_step_low)
    grad_rank = ein("tc,rc->tr", grad_step_low, step_full)
    grad_projected = hidden_sum_small(
        jnp.concatenate([grad_rank, jnp.sum(part_b, axis=2), jnp.sum(part_c, axis=2)], axis=1)
    )
    grad_proj_low = grad_projected.astype(bf16)
    state_grad = ein("tc,tk->kc", activity_low, grad_proj_low)
    grad_activity = grad_act_scan + ein("tk,kc->tc", grad_proj_low, state_full)

    def conv_fn(values, kernel, offset):
        return jax.nn.silu(causal_conv(values, segment, kernel, offset))

    _, conv_back = jax.vjp(conv_fn, inner_x, conv_kernel, conv_offset)
    grad_inner_x, conv_weight_grad, conv_bias_grad = conv_back(grad_activity)
    grad_x_low = grad_inner_x.astype(bf16)
    both = jnp.stack([grad_x_low, grad_z_low]).reshape(2, positions, devices, own_channels)
    both = exchange(both.transpose(2, 0, 1, 3), "expert")
    grad_normed = hidden_sum(product(grad_x_low, weight_x) + product(grad_z_low, weight_z))
    gain_one_grad = jnp.sum(grad_normed * unit_one, axis=0)
    grad_unit_one = grad_normed * gain_one[None, :]
    tokens_grad = grad_hidden + scale_one * (
        grad_unit_one - unit_one * jnp.mean(grad_unit_one * unit_one, axis=-1, keepdims=True)
    )

    totals = None
    sources = (normed, normed_two, cotangent)
    for base in range(0, devices, group):
        if base > 0:
            sources, totals = lax.optimization_barrier((sources, totals))
            picker = pick(codes[base : base + group])
        normed_all, rows_all, cotangent_all = [gather_tokens(v, base) for v in sources]
        grad_all = cotangent_all.astype(f32) * gates[base : base + group, 0, :, None]
        parts = expert_grads(
            picker, rows_all, grad_all.astype(bf16), expert_up, expert_down, index, block
        ) + (
            ein("ntd,ntc->dc", normed_all, both[base : base + group, 0]),
            ein("ntd,ntc->dc", normed_all, both[base : base + group, 1]),
        )
        totals = parts if base == 0 else tuple(a + b for a, b in zip(totals, parts))
    up_grad, down_grad, proj_x_grad, proj_z_grad = totals

    vector_grads = jnp.concatenate([gain_one_grad[None], gain_two_grad[None], router_grad])
    vector_grads = vector_grads.reshape(2 + experts, devices, block).transpose(1, 0, 2)
    vector_grads = scatter_sum(jnp.take(vector_grads, order, axis=0), "expert")
    small_grads = jnp.concatenate(
        [
            conv_weight_grad,
            conv_bias_grad[None],
            step_bias_grad,
            skip_grad,
            decay_grad,
            step_proj_grad,
            state_grad,
        ]
    )
    small_grads = small_grads.reshape(-1, devices, own_channels).transpose(1, 0, 2)
    small_grads = scatter_sum(small_grads, "expert")
    return (
        layer_out,
        tokens_grad,
        vector_grads[0],
        proj_x_grad,
        proj_z_grad,
        small_grads[:taps],
        small_grads[taps],
        small_grads[taps + 3 + entries + rank :].T,
        small_grads[taps + 3 + entries : taps + 3 + entries + rank],
        small_grads[taps + 1],
        small_grads[taps + 3 : taps + 3 + entries],
        small_grads[taps + 2],
        out_grad,
        vector_grads[1],
        vector_grads[2:].T,
        up_grad,
        down_grad,
    )


def solution(mesh):
    in_specs = (
        P("expert", None),
        P("expert", None),
        P("expert", None),
        P("expert", None),
        P("expert"),
        P(None, ("expert", "hidden")),
        P(None, ("expert", "hidden")),
        P(None, ("expert", "hidden")),
        P(("expert", "hidden")),
        P(("expert", "hidden"), None),
        P(None, ("expert", "hidden")),
        P(("expert", "hidden")),
        P(None, ("expert", "hidden")),
        P(("expert", "hidden")),
        P(("expert", "hidden"), None),
        P("expert"),
        P("expert", None),
        P(None, None, "hidden"),
        P(None, "hidden", None),
    )
    out_specs = (
        P("expert", None),
        P("expert", None),
        P("expert"),
        P(None, ("expert", "hidden")),
        P(None, ("expert", "hidden")),
        P(None, ("expert", "hidden")),
        P(("expert", "hidden")),
        P(("expert", "hidden"), None),
        P(None, ("expert", "hidden")),
        P(("expert", "hidden")),
        P(None, ("expert", "hidden")),
        P(("expert", "hidden")),
        P(("expert", "hidden"), None),
        P("expert"),
        P("expert", None),
        P(None, "expert", "hidden"),
        P(None, "hidden", "expert"),
    )
    return jax.shard_map(local, mesh=mesh, in_specs=in_specs, out_specs=out_specs, check_vma=False)
```

time: 3480 us -> 657 us (0.19); the launches traced: 3420 us -> 647 us
  waiting for transfers between devices: 1240 us -> 236 us
  blocking collectives: 677 us -> 0 us
  local copies, waits for them, and re-layouts: 752 us -> 112 us
  other arithmetic: 652 us -> 22.9 us
  starting transfers between devices: 13.5 us -> 132 us
  matrix products: 50.6 us -> 108 us
    reduce_scatter x2 -> x0, waiting for transfers between devices: 905 us -> none  [the longest x1 453 us: local(): lax.psum_scatter(up_placed, 'expert', scatter_dimension=1, tiled=True)]
    pad x544 -> x0, local copies, waits for them, and re-layouts: 432 us -> none  [advance(): lax.associative_scan(combine_pair, (decays, inputs), axis=0)]
    psum x19 -> x0, blocking collectives: 423 us -> none  [the longest x8 181 us: local(): column_term = lax.psum(jnp.sum(grad_scaled * scaled, axis=0), 'expert')]
    unnamed x20 -> x0, waiting for transfers between devices: 268 us -> none
    mul x261 -> x1, other arithmetic: 248 us -> 0.01 us  [local(): grad_expert_in = plain_in * (gate_values * valid_float)[:, None]]
    ppermute x0 -> x100, waiting for transfers between devices: none -> 236 us  [swap(): return lax.ppermute(values, axis, [(i, i ^ bits) for i in range(size)])]
    all_gather x5 -> x0, blocking collectives: 151 us -> none  [the longest x1 42.7 us: local(): lax.all_gather(router, 'expert', axis=0, tiled=True)]
    ppermute x0 -> x100, starting transfers between devices: none -> 132 us  [swap(): return lax.ppermute(values, axis, [(i, i ^ bits) for i in range(size)])]
  transfers between devices with their start and end apart: 17 -> 100, of which waited for: 9 -> 51; matrix products, arithmetic and copies ran while one was open for 41% -> 28% of each run, Pallas kernels for 0% -> 5%
where the time goes in v1:
time: 657 us; the launch traced here: 647 us
  waiting for transfers between devices  236 us (36%)
  starting transfers between devices  132 us (20%)
  local copies, waits for them, and re-layouts  112 us (17%)
  matrix products  108 us (16%)
  Pallas kernels  32 us (5%)
  other arithmetic  22.9 us (3%)
    ppermute x100, waiting for transfers between devices, swap(): return lax.ppermute(values, axis, [(i, i ^ bits) for i in range(size)])  236 us
    ppermute x100, starting transfers between devices, swap(): return lax.ppermute(values, axis, [(i, i ^ bits) for i in range(size)])  132 us
    dot_general x25, matrix products, ein(): return jnp.einsum(spec, left, right, preferred_element_type=f32)  102 us
    unnamed x237, local copies, waits for them, and re-layouts  41.7 us
    dynamic_update_slice x12, local copies, waits for them, and re-layouts, gather_tokens(): whole = lax.dynamic_update_slice(whole, piece, (0, (place ^ r) * size, 0))  23.6 us
    pallas_call x1, Pallas kernels, scan_backward(): pl.pallas_call(scan_backward_body, out_shape=(shape_of(positions, channel...  18.9 us
  transfers between devices with their start and end apart: 100, of which 51 were waited for; matrix products, arithmetic and copies ran while one was open for 28% of the time, Pallas kernels for 5%

profile of v1, /device:TPU:0, one launch (start us, length us, event | category | flops | bytes accessed | tf_op | source)
XLA Modules:
  0.0 647.1 jit_solution(11373350812186183761)
XLA Ops:
  70.3 9.5 %collective-permute-done.93 = bf16[64,1152]{1,0:T(8,128)(2,1)S(1)} collective-permute-done((bf16[64,1152]{1,0:T(8,128)(2,1)}, bf16[64,1152]{1,0:T(8,128)(2,1)S(1)}, u32[]{:S(2)}, u32[]{:S(2)}) %collective-permute-start.93) | collective-permute-done | bytes 147488 | tf_op jit(solution)/shard_map/ppermute | solution.py:33
  81.1 8.8 %collective-permute-done.94 = bf16[64,1152]{1,0:T(8,128)(2,1)S(1)} collective-permute-done((bf16[64,1152]{1,0:T(8,128)(2,1)}, bf16[64,1152]{1,0:T(8,128)(2,1)S(1)}, u32[]{:S(2)}, u32[]{:S(2)}) %collective-permute-start.94) | collective-permute-done | bytes 147488 | tf_op jit(solution)/shard_map/ppermute | solution.py:33
  92.0 5.3 collective-permute-done.95
  100.0 6.5 %collective-permute-done.96 = bf16[64,1152]{1,0:T(8,128)(2,1)S(1)} collective-permute-done((bf16[64,1152]{1,0:T(8,128)(2,1)}, bf16[64,1152]{1,0:T(8,128)(2,1)S(1)}, u32[]{:S(2)}, u32[]{:S(2)}) %collective-permute-start.96) | collective-permute-done | bytes 147488 | tf_op jit(solution)/shard_map/ppermute | solution.py:33
  106.6 6.5 collective-permute-start.10
  126.3 6.4 collective-permute-start.60
  179.1 7.7 %collective-permute-done.18 = bf16[72,1152]{1,0:T(8,128)(2,1)S(1)} collective-permute-done((bf16[72,1152]{1,0:T(8,128)(2,1)}, bf16[72,1152]{1,0:T(8,128)(2,1)S(1)}, u32[]{:S(2)}, u32[]{:S(2)}) %collective-permute-start.18) | collective-permute-done | bytes 165920 | tf_op jit(solution)/shard_map/ppermute | solution.py:33
  188.2 9.3 %collective-permute-done.19 = bf16[72,1152]{1,0:T(8,128)(2,1)S(1)} collective-permute-done((bf16[72,1152]{1,0:T(8,128)(2,1)}, bf16[72,1152]{1,0:T(8,128)(2,1)S(1)}, u32[]{:S(2)}, u32[]{:S(2)}) %collective-permute-start.19) | collective-permute-done | bytes 165920 | tf_op jit(solution)/shard_map/ppermute | solution.py:33
  200.0 5.8 collective-permute-done.20
  208.5 5.5 collective-permute-done.21
  222.9 10.4 %scan_forward.1 = (bf16[256,576]{1,0:T(8,128)(2,1)S(1)}, f32[256,576]{1,0:T(8,128)S(1)}, f32[256,16,640]{2,1,0:T(8,128)}) custom-call(f32[256,576]{1,0:T(8,128)S(1)} %fusion.57.pre, f32[256,576]{1,0:T(8,128)S(1)} %get-tuple-element.172.act, f32[256,576]{1,0:T(8,128)S(1)} %fusion.99.gate, f32[256,16,128]{2,1,0:T(8,128)S(1)} %broadcast_in_dim.54.basis_b, ...), custom_call_target="tpu_custom_call" | custom-call | tf_op jit(solution)/shard_map/scan_forward/pallas_call | solution.py:247
  233.4 5.7 collective-permute-done.23
  249.3 8.4 %collective-permute-done.25 = bf16[72,1152]{1,0:T(8,128)(2,1)S(1)} collective-permute-done((bf16[72,1152]{1,0:T(8,128)(2,1)}, bf16[72,1152]{1,0:T(8,128)(2,1)S(1)}, u32[]{:S(2)}, u32[]{:S(2)}) %collective-permute-start.25) | collective-permute-done | bytes 165920 | tf_op jit(solution)/shard_map/ppermute | solution.py:33
  258.2 10.6 %collective-permute-done.26 = bf16[72,1152]{1,0:T(8,128)(2,1)S(1)} collective-permute-done((bf16[72,1152]{1,0:T(8,128)(2,1)}, bf16[72,1152]{1,0:T(8,128)(2,1)S(1)}, u32[]{:S(2)}, u32[]{:S(2)}) %collective-permute-start.26) | collective-permute-done | bytes 165920 | tf_op jit(solution)/shard_map/ppermute | solution.py:33
  278.0 6.5 %collective-permute-done.28 = bf16[72,1152]{1,0:T(8,128)(2,1)S(1)} collective-permute-done((bf16[72,1152]{1,0:T(8,128)(2,1)}, bf16[72,1152]{1,0:T(8,128)(2,1)S(1)}, u32[]{:S(2)}, u32[]{:S(2)}) %collective-permute-start.28) | collective-permute-done | bytes 165920 | tf_op jit(solution)/shard_map/ppermute | solution.py:33
  303.1 18.7 %collective-permute-done.65 = bf16[8,64,1152]{2,1,0:T(8,128)(2,1)} collective-permute-done((bf16[8,64,1152]{2,1,0:T(8,128)(2,1)S(1)}, bf16[8,64,1152]{2,1,0:T(8,128)(2,1)}, u32[]{:S(2)}, u32[]{:S(2)}) %collective-permute-start.65) | collective-permute-done | bytes 1179680 | tf_op jit(solution)/shard_map/ppermute | solution.py:33
  333.3 7.4 %convolution_convert_fusion.5 = bf16[8,48,1152]{2,1,0:T(8,128)(2,1)S(1)} fusion(bf16[8,768,1152]{2,1,0:T(8,128)(2,1)} %param.37, f32[8,48,768]{2,1,0:T(8,128)S(1)} %fusion.101), kind=kOutput, calls=%fused_computation.24 | convolution fusion | flops 682573824 | bytes 16220160 | tf_op jit(solution)/shard_map/erf,efd->erd/dot_general | solution.py:24
  343.0 9.5 %multiply_reduce_fusion.2 = (f32[8,48]{1,0:T(8,128)S(1)}, f32[8,48,768]{2,1,0:T(8,128)S(1)}) fusion(f32[8,48,768]{2,1,0:T(8,128)S(1)} %fusion.101, bf16[8,48,1152]{2,1,0:T(8,128)(2,1)S(1)} %bitcast.333, bf16[8,768,1152]{2,1,0:T(8,128)(2,1)} %param.37), kind=kOutput, calls=%fused_computation.63 | convolution fusion | flops 683015808 | bytes 17401344 | tf_op jit(solution)/shard_map/erd,efd->erf/dot_general | solution.py:24
  352.4 9.3 %convolution_convert_fusion.4 = bf16[8,48,1152]{2,1,0:T(8,128)(2,1)S(1)} fusion(bf16[8,1152,768]{2,1,0:T(8,128)(2,1)} %param.36, f32[8,48,768]{2,1,0:T(8,128)S(1)} %fusion.101, f32[8,48,768]{2,1,0:T(8,128)S(1)} %get-tuple-element.202), kind=kOutput, calls=%fused_computation.23 | convolution fusion | flops 685817856 | bytes 17399808 | tf_op jit(solution)/shard_map/erf,edf->erd/dot_general | solution.py:24
  407.1 5.7 collective-permute-done.83
  420.0 7.7 %collective-permute-done.39 = bf16[128,1152]{1,0:T(8,128)(2,1)S(1)} collective-permute-done((bf16[128,1152]{1,0:T(8,128)(2,1)S(1)}, bf16[128,1152]{1,0:T(8,128)(2,1)S(1)}, u32[]{:S(2)}, u32[]{:S(2)}) %collective-permute-start.39) | collective-permute-done | bytes 294944 | tf_op jit(solution)/shard_map/ppermute | solution.py:33
  427.9 5.3 collective-permute-done.47
  443.2 18.9 %scan_backward.1 = (f32[256,576]{1,0:T(8,128)}, bf16[256,576]{1,0:T(8,128)(2,1)}, bf16[256,576]{1,0:T(8,128)(2,1)}, f32[256,16,128]{2,1,0:T(8,128)}, f32[256,16,...) custom-call(f32[256,576]{1,0:T(8,128)} %fusion.48.grad, f32[256,576]{1,0:T(8,128)} %copy-done.7, ...), custom_call_target="tpu_custom_call" | custom-call | tf_op jit(solution)/shard_map/scan_backward/pallas_call | solution.py:271
  523.2 6.3 collective-permute-done.71
  530.2 5.4 collective-permute-done.72
  542.7 6.1 collective-permute-done.74
  577.8 7.2 %collective-permute-done.78 = bf16[2,72,1152]{2,1,0:T(8,128)(2,1)S(1)} collective-permute-done((bf16[2,72,1152]{2,1,0:T(8,128)(2,1)S(1)}, bf16[2,72,1152]{2,1,0:T(8,128)(2,1)S(1)}, u32[]{:S(2)}, u32[]{:S(2)}) %collective-permute-start.78) | collective-permute-done | bytes 331808 | tf_op jit(solution)/shard_map/ppermute | solution.py:33
  596.2 5.1 convolution_convert_fusion.1
  601.4 6.8 %copy.313 = bf16[8,8,48,1152]{3,2,0,1:T(8,128)(2,1)} copy(bf16[8,8,48,1152]{3,2,1,0:T(8,128)(2,1)} %bitcast.320) | data formatting | bytes 14155776 | tf_op jit(solution)/shard_map/reshape | solution.py:352
  608.2 10.7 %fusion.105 = f32[8,384,768]{2,1,0:T(8,128)} fusion(bf16[8,384,1152]{2,1,0:T(8,128)(2,1)} %bitcast.325, bf16[8,1152,768]{2,1,0:T(8,128)(2,1)S(1)} %bitcast.313), kind=kOutput, calls=%fused_computation.337 | convolution fusion | flops 5435817984 | bytes 30670848 | tf_op jit(solution)/shard_map/erd,edf->erf/dot_general | solution.py:24
  618.9 18.2 %fusion.9 = f32[8,144,768]{2,1,0:T(8,128)} fusion(f32[8,384,768]{2,1,0:T(8,128)} %fusion.105, bf16[8,384,1152]{2,1,0:T(8,128)(2,1)} %bitcast.326, s32[]{:T(128)S(6)} %select_n.125, bf16[8,384,1152]{2,1,0:T(8,128)(2,1)} %bitcast.323, bf16[8,768,1152]{2,1,0:T(8,128)(2,1)} %param.37), kind=kOutput, calls=%fused_computation.17 | convolution fusion | flops 6162481152 | bytes 35782660 | tf_op jit(solution)/shard_map/erd,erf->edf/dot_general | solution.py:24
  637.0 9.9 %fusion.8 = f32[8,768,144]{1,2,0:T(8,128)} fusion(f32[8,384,768]{2,1,0:T(8,128)} %fusion.105, bf16[8,384,1152]{2,1,0:T(8,128)(2,1)} %bitcast.324, s32[]{:T(128)S(6)} %select_n.125), kind=kOutput, calls=%fused_computation.16 | convolution fusion | flops 700710912 | bytes 14548996 | tf_op jit(solution)/shard_map/erf,erd->efd/dot_general | solution.py:24
  (632 shorter events, 372.0 us)
Async XLA Ops:
  0.7 115.1 %collective-permute-start.6 = (bf16[72,1152]{1,0:T(8,128)(2,1)}, bf16[72,1152]{1,0:T(8,128)(2,1)}, u32[]{:S(2)}, u32[]{:S(2)}) collective-permute-start(bf16[72,1152]{1,0:T(8,128)(2,1)} %bitcast.348), channel_id=1, source_target_pairs={{0,4},{4,0},{8,12},{12,8},{16,20},{20,16},{24,28},{28,24},{1,5},{5... | collective-permute-start | bytes 497672 | tf_op jit(solution)/shard_map/ppermute | solution.py:33
  3.7 114.6 %collective-permute-start.7 = (bf16[72,1152]{1,0:T(8,128)(2,1)}, bf16[72,1152]{1,0:T(8,128)(2,1)}, u32[]{:S(2)}, u32[]{:S(2)}) collective-permute-start(bf16[72,1152]{1,0:T(8,128)(2,1)} %bitcast.349), channel_id=1, source_target_pairs={{0,8},{4,12},{8,0},{12,4},{16,24},{20,28},{24,16},{28,20},{1,9},{5... | collective-permute-start | bytes 497672 | tf_op jit(solution)/shard_map/ppermute | solution.py:33
  5.3 116.4 %collective-permute-start.8 = (bf16[72,1152]{1,0:T(8,128)(2,1)}, bf16[72,1152]{1,0:T(8,128)(2,1)}, u32[]{:S(2)}, u32[]{:S(2)}) collective-permute-start(bf16[72,1152]{1,0:T(8,128)(2,1)} %bitcast.350), channel_id=1, source_target_pairs={{0,12},{4,8},{8,4},{12,0},{16,28},{20,24},{24,20},{28,16},{1,13},{... | collective-permute-start | bytes 497672 | tf_op jit(solution)/shard_map/ppermute | solution.py:33
  10.9 37.0 %collective-permute-start = (bf16[1,199,72]{2,0,1:T(2,128)(2,1)S(1)}, bf16[1,199,72]{2,0,1:T(2,128)(2,1)S(1)}, u32[]{:S(2)}, u32[]{:S(2)}) collective-permute-start(bf16[1,199,72]{2,0,1:T(2,128)(2,1)S(1)} %copy.275), channel_id=1, source_target_pairs={{0,4},{4,0},{8,12},{12,8},{16,20},{20,16},{24,28},{28,24},{1,5},{5... | collective-permute-start | bytes 85976 | tf_op jit(solution)/shard_map/ppermute | solution.py:33
  54.1 70.0 %collective-permute-start.9 = (bf16[72,1152]{1,0:T(8,128)(2,1)S(1)}, bf16[72,1152]{1,0:T(8,128)(2,1)S(1)}, u32[]{:S(2)}, u32[]{:S(2)}) collective-permute-start(bf16[72,1152]{1,0:T(8,128)(2,1)S(1)} %bitcast.351), channel_id=1, source_target_pairs={{0,16},{4,20},{8,24},{12,28},{16,0},{20,4},{24,8},{28,12},{1,17},{... | collective-permute-start | bytes 497672 | tf_op jit(solution)/shard_map/ppermute | solution.py:33
  106.6 17.6 %collective-permute-start.10 = (bf16[72,1152]{1,0:T(8,128)(2,1)S(1)}, bf16[72,1152]{1,0:T(8,128)(2,1)S(1)}, u32[]{:S(2)}, u32[]{:S(2)}) collective-permute-start(bf16[72,1152]{1,0:T(8,128)(2,1)S(1)} %bitcast.352), channel_id=1, source_target_pairs={{0,20},{4,16},{8,28},{12,24},{16,4},{20,0},{24,12},{28,8},{1,21},{... | collective-permute-start | bytes 497672 | tf_op jit(solution)/shard_map/ppermute | solution.py:33
  118.3 14.5 %collective-permute-start.12 = (bf16[72,1152]{1,0:T(8,128)(2,1)S(1)}, bf16[72,1152]{1,0:T(8,128)(2,1)S(1)}, u32[]{:S(2)}, u32[]{:S(2)}) collective-permute-start(bf16[72,1152]{1,0:T(8,128)(2,1)S(1)} %bitcast.354), channel_id=1, source_target_pairs={{0,28},{4,24},{8,20},{12,16},{16,12},{20,8},{24,4},{28,0},{1,29},{... | collective-permute-start | bytes 497672 | tf_op jit(solution)/shard_map/ppermute | solution.py:33
  121.7 20.7 %collective-permute-start.57 = (bf16[64,1152]{1,0:T(8,128)(2,1)}, bf16[64,1152]{1,0:T(8,128)(2,1)S(1)}, u32[]{:S(2)}, u32[]{:S(2)}) collective-permute-start(bf16[64,1152]{1,0:T(8,128)(2,1)} %get-tuple-element.171), channel_id=1, source_target_pairs={{0,4},{4,0},{8,12},{12,8},{16,20},{20,16},{24,28},{28,24},{1,5},{5... | collective-permute-start | bytes 442376 | tf_op jit(solution)/shard_map/ppermute | solution.py:33
  124.1 20.8 %collective-permute-start.58 = (bf16[64,1152]{1,0:T(8,128)(2,1)}, bf16[64,1152]{1,0:T(8,128)(2,1)S(1)}, u32[]{:S(2)}, u32[]{:S(2)}) collective-permute-start(bf16[64,1152]{1,0:T(8,128)(2,1)} %get-tuple-element.171), channel_id=1, source_target_pairs={{0,8},{4,12},{8,0},{12,4},{16,24},{20,28},{24,16},{28,20},{1,9},{5... | collective-permute-start | bytes 442376 | tf_op jit(solution)/shard_map/ppermute | solution.py:33
  124.2 23.0 %collective-permute-start.59 = (bf16[64,1152]{1,0:T(8,128)(2,1)}, bf16[64,1152]{1,0:T(8,128)(2,1)S(1)}, u32[]{:S(2)}, u32[]{:S(2)}) collective-permute-start(bf16[64,1152]{1,0:T(8,128)(2,1)} %get-tuple-element.171), channel_id=1, source_target_pairs={{0,12},{4,8},{8,4},{12,0},{16,28},{20,24},{24,20},{28,16},{1,13},{... | collective-permute-start | bytes 442376 | tf_op jit(solution)/shard_map/ppermute | solution.py:33
  126.3 21.6 %collective-permute-start.60 = (bf16[64,1152]{1,0:T(8,128)(2,1)}, bf16[64,1152]{1,0:T(8,128)(2,1)S(1)}, u32[]{:S(2)}, u32[]{:S(2)}) collective-permute-start(bf16[64,1152]{1,0:T(8,128)(2,1)} %get-tuple-element.171), channel_id=1, source_target_pairs={{0,16},{4,20},{8,24},{12,28},{16,0},{20,4},{24,8},{28,12},{1,17},{... | collective-permute-start | bytes 442376 | tf_op jit(solution)/shard_map/ppermute | solution.py:33
  132.8 15.9 %collective-permute-start.61 = (bf16[64,1152]{1,0:T(8,128)(2,1)}, bf16[64,1152]{1,0:T(8,128)(2,1)S(1)}, u32[]{:S(2)}, u32[]{:S(2)}) collective-permute-start(bf16[64,1152]{1,0:T(8,128)(2,1)} %get-tuple-element.171), channel_id=1, source_target_pairs={{0,20},{4,16},{8,28},{12,24},{16,4},{20,0},{24,12},{28,8},{1,21},{... | collective-permute-start | bytes 442376 | tf_op jit(solution)/shard_map/ppermute | solution.py:33
  142.3 143.3 %collective-permute-start.62 = (bf16[64,1152]{1,0:T(8,128)(2,1)}, bf16[64,1152]{1,0:T(8,128)(2,1)}, u32[]{:S(2)}, u32[]{:S(2)}) collective-permute-start(bf16[64,1152]{1,0:T(8,128)(2,1)} %get-tuple-element.171), channel_id=1, source_target_pairs={{0,24},{4,28},{8,16},{12,20},{16,8},{20,12},{24,0},{28,4},{1,25},{... | collective-permute-start | bytes 442376 | tf_op jit(solution)/shard_map/ppermute | solution.py:33
  144.9 144.2 %collective-permute-start.63 = (bf16[64,1152]{1,0:T(8,128)(2,1)}, bf16[64,1152]{1,0:T(8,128)(2,1)}, u32[]{:S(2)}, u32[]{:S(2)}) collective-permute-start(bf16[64,1152]{1,0:T(8,128)(2,1)} %get-tuple-element.171), channel_id=1, source_target_pairs={{0,28},{4,24},{8,20},{12,16},{16,12},{20,8},{24,4},{28,0},{1,29},{... | collective-permute-start | bytes 442376 | tf_op jit(solution)/shard_map/ppermute | solution.py:33
  147.9 150.4 %collective-permute-start.97 = (bf16[8,64,1152]{2,1,0:T(8,128)(2,1)}, bf16[8,64,1152]{2,1,0:T(8,128)(2,1)}, u32[]{:S(2)}, u32[]{:S(2)}) collective-permute-start(bf16[8,64,1152]{2,1,0:T(8,128)(2,1)} %bitcast_dynamic-update-slice_fusion.24), channel_id=1, source_target_pairs={{0,1},{1,0},{2,3},{3,2},{4,5},{5,4},{6,7},{7,6},{8,9},{9,8},{10,11... | collective-permute-start | bytes 3538952 | tf_op jit(solution)/shard_map/ppermute | solution.py:33
  148.7 15.4 %collective-permute-start.15 = (bf16[72,1152]{1,0:T(8,128)(2,1)}, bf16[72,1152]{1,0:T(8,128)(2,1)}, u32[]{:S(2)}, u32[]{:S(2)}) collective-permute-start(bf16[72,1152]{1,0:T(8,128)(2,1)} %bitcast.23), channel_id=1, source_target_pairs={{0,4},{4,0},{8,12},{12,8},{16,20},{20,16},{24,28},{28,24},{1,5},{5... | collective-permute-start | bytes 497672 | tf_op jit(solution)/shard_map/ppermute | solution.py:33
  161.6 136.1 %collective-permute-start.98 = (bf16[8,64,1152]{2,1,0:T(8,128)(2,1)}, bf16[8,64,1152]{2,1,0:T(8,128)(2,1)}, u32[]{:S(2)}, u32[]{:S(2)}) collective-permute-start(bf16[8,64,1152]{2,1,0:T(8,128)(2,1)} %bitcast_dynamic-update-slice_fusion.24), channel_id=1, source_target_pairs={{0,2},{1,3},{2,0},{3,1},{4,6},{5,7},{6,4},{7,5},{8,10},{9,11},{10,... | collective-permute-start | bytes 3538952 | tf_op jit(solution)/shard_map/ppermute | solution.py:33
  218.8 14.5 %collective-permute-start.22 = (bf16[72,1152]{1,0:T(8,128)(2,1)}, bf16[72,1152]{1,0:T(8,128)(2,1)S(1)}, u32[]{:S(2)}, u32[]{:S(2)}) collective-permute-start(bf16[72,1152]{1,0:T(8,128)(2,1)} %param.33), channel_id=1, source_target_pairs={{0,4},{4,0},{8,12},{12,8},{16,20},{20,16},{24,28},{28,24},{1,5},{5... | collective-permute-start | bytes 497672 | tf_op jit(solution)/shard_map/ppermute | solution.py:33
  290.1 31.8 %collective-permute-start.64 = (bf16[8,64,1152]{2,1,0:T(8,128)(2,1)S(1)}, bf16[8,64,1152]{2,1,0:T(8,128)(2,1)S(1)}, u32[]{:S(2)}, u32[]{:S(2)}) collective-permute-start(bf16[8,64,1152]{2,1,0:T(8,128)(2,1)S(1)} %bitcast_dynamic-update-slice_fusion.40), channel_id=1, source_target_pairs={{0,1},{1,0},{2,3},{3,2},{4,5},{5,4},{6,7},{7,6},{8,9},{9,8},{10,11... | collective-permute-start | bytes 3538952 | tf_op jit(solution)/shard_map/ppermute | solution.py:33
  290.1 31.7 %collective-permute-start.65 = (bf16[8,64,1152]{2,1,0:T(8,128)(2,1)S(1)}, bf16[8,64,1152]{2,1,0:T(8,128)(2,1)}, u32[]{:S(2)}, u32[]{:S(2)}) collective-permute-start(bf16[8,64,1152]{2,1,0:T(8,128)(2,1)S(1)} %bitcast_dynamic-update-slice_fusion.40), channel_id=1, source_target_pairs={{0,2},{1,3},{2,0},{3,1},{4,6},{5,7},{6,4},{7,5},{8,10},{9,11},{10,... | collective-permute-start | bytes 3538952 | tf_op jit(solution)/shard_map/ppermute | solution.py:33
  297.7 27.7 %collective-permute-start.31 = (bf16[128,1152]{1,0:T(8,128)(2,1)S(1)}, bf16[128,1152]{1,0:T(8,128)(2,1)S(1)}, u32[]{:S(2)}, u32[]{:S(2)}) collective-permute-start(bf16[128,1152]{1,0:T(8,128)(2,1)S(1)} %add_convert_fusion.7), channel_id=1, source_target_pairs={{0,1},{1,0},{2,3},{3,2},{4,5},{5,4},{6,7},{7,6},{8,9},{9,8},{10,11... | collective-permute-start | bytes 884744 | tf_op jit(solution)/shard_map/ppermute | solution.py:33
  297.8 192.9 %collective-permute-start.99 = (bf16[8,64,1152]{2,1,0:T(8,128)(2,1)}, bf16[8,64,1152]{2,1,0:T(8,128)(2,1)}, u32[]{:S(2)}, u32[]{:S(2)}) collective-permute-start(bf16[8,64,1152]{2,1,0:T(8,128)(2,1)} %collective-permute-done.98), channel_id=1, source_target_pairs={{0,1},{1,0},{2,3},{3,2},{4,5},{5,4},{6,7},{7,6},{8,9},{9,8},{10,11... | collective-permute-start | bytes 3538952 | tf_op jit(solution)/shard_map/ppermute | solution.py:33
  321.8 179.5 %collective-permute-start.66 = (bf16[8,64,1152]{2,1,0:T(8,128)(2,1)}, bf16[8,64,1152]{2,1,0:T(8,128)(2,1)}, u32[]{:S(2)}, u32[]{:S(2)}) collective-permute-start(bf16[8,64,1152]{2,1,0:T(8,128)(2,1)} %collective-permute-done.65), channel_id=1, source_target_pairs={{0,1},{1,0},{2,3},{3,2},{4,5},{5,4},{6,7},{7,6},{8,9},{9,8},{10,11... | collective-permute-start | bytes 3538952 | tf_op jit(solution)/shard_map/ppermute | solution.py:33
  328.4 70.2 %collective-permute-start.80 = (bf16[64,1152]{1,0:T(8,128)(2,1)}, bf16[64,1152]{1,0:T(8,128)(2,1)}, u32[]{:S(2)}, u32[]{:S(2)}) collective-permute-start(bf16[64,1152]{1,0:T(8,128)(2,1)} %get-tuple-element.163), channel_id=1, source_target_pairs={{0,4},{4,0},{8,12},{12,8},{16,20},{20,16},{24,28},{28,24},{1,5},{5... | collective-permute-start | bytes 442376 | tf_op jit(solution)/shard_map/ppermute | solution.py:33
  330.7 70.3 %collective-permute-start.81 = (bf16[64,1152]{1,0:T(8,128)(2,1)}, bf16[64,1152]{1,0:T(8,128)(2,1)S(1)}, u32[]{:S(2)}, u32[]{:S(2)}) collective-permute-start(bf16[64,1152]{1,0:T(8,128)(2,1)} %get-tuple-element.163), channel_id=1, source_target_pairs={{0,8},{4,12},{8,0},{12,4},{16,24},{20,28},{24,16},{28,20},{1,9},{5... | collective-permute-start | bytes 442376 | tf_op jit(solution)/shard_map/ppermute | solution.py:33
  400.9 14.9 %collective-permute-start.84 = (bf16[64,1152]{1,0:T(8,128)(2,1)}, bf16[64,1152]{1,0:T(8,128)(2,1)S(1)}, u32[]{:S(2)}, u32[]{:S(2)}) collective-permute-start(bf16[64,1152]{1,0:T(8,128)(2,1)} %get-tuple-element.163), channel_id=1, source_target_pairs={{0,20},{4,16},{8,28},{12,24},{16,4},{20,0},{24,12},{28,8},{1,21},{... | collective-permute-start | bytes 442376 | tf_op jit(solution)/shard_map/ppermute | solution.py:33
  412.8 20.5 %collective-permute-start.86 = (bf16[64,1152]{1,0:T(8,128)(2,1)}, bf16[64,1152]{1,0:T(8,128)(2,1)S(1)}, u32[]{:S(2)}, u32[]{:S(2)}) collective-permute-start(bf16[64,1152]{1,0:T(8,128)(2,1)} %get-tuple-element.163), channel_id=1, source_target_pairs={{0,28},{4,24},{8,20},{12,16},{16,12},{20,8},{24,4},{28,0},{1,29},{... | collective-permute-start | bytes 442376 | tf_op jit(solution)/shard_map/ppermute | solution.py:33
  434.0 130.4 %collective-permute-start.87 = (bf16[8,64,1152]{2,1,0:T(8,128)(2,1)}, bf16[8,64,1152]{2,1,0:T(8,128)(2,1)}, u32[]{:S(2)}, u32[]{:S(2)}) collective-permute-start(bf16[8,64,1152]{2,1,0:T(8,128)(2,1)} %bitcast_dynamic-update-slice_fusion.32), channel_id=1, source_target_pairs={{0,1},{1,0},{2,3},{3,2},{4,5},{5,4},{6,7},{7,6},{8,9},{9,8},{10,11... | collective-permute-start | bytes 3538952 | tf_op jit(solution)/shard_map/ppermute | solution.py:33
  436.7 126.4 %collective-permute-start.88 = (bf16[8,64,1152]{2,1,0:T(8,128)(2,1)}, bf16[8,64,1152]{2,1,0:T(8,128)(2,1)}, u32[]{:S(2)}, u32[]{:S(2)}) collective-permute-start(bf16[8,64,1152]{2,1,0:T(8,128)(2,1)} %bitcast_dynamic-update-slice_fusion.32), channel_id=1, source_target_pairs={{0,2},{1,3},{2,0},{3,1},{4,6},{5,7},{6,4},{7,5},{8,10},{9,11},{10,... | collective-permute-start | bytes 3538952 | tf_op jit(solution)/shard_map/ppermute | solution.py:33
  475.5 97.2 %collective-permute-start.77 = (bf16[4,72,1152]{2,1,0:T(8,128)(2,1)}, bf16[4,72,1152]{2,1,0:T(8,128)(2,1)}, u32[]{:S(2)}, u32[]{:S(2)}) collective-permute-start(bf16[4,72,1152]{2,1,0:T(8,128)(2,1)} %bitcast.347), channel_id=1, source_target_pairs={{0,16},{4,20},{8,24},{12,28},{16,0},{20,4},{24,8},{28,12},{1,17},{... | collective-permute-start | bytes 1990664 | tf_op jit(solution)/shard_map/ppermute | solution.py:33
  490.7 72.4 %collective-permute-start.51 = (bf16[128,1152]{1,0:T(8,128)(2,1)S(1)}, bf16[128,1152]{1,0:T(8,128)(2,1)S(1)}, u32[]{:S(2)}, u32[]{:S(2)}) collective-permute-start(bf16[128,1152]{1,0:T(8,128)(2,1)S(1)} %dynamic-slice_convert_fusion), channel_id=1, source_target_pairs={{0,1},{1,0},{2,3},{3,2},{4,5},{5,4},{6,7},{7,6},{8,9},{9,8},{10,11... | collective-permute-start | bytes 884744 | tf_op jit(solution)/shard_map/ppermute | solution.py:33
  563.0 31.7 %collective-permute-start.89 = (bf16[8,64,1152]{2,1,0:T(8,128)(2,1)}, bf16[8,64,1152]{2,1,0:T(8,128)(2,1)}, u32[]{:S(2)}, u32[]{:S(2)}) collective-permute-start(bf16[8,64,1152]{2,1,0:T(8,128)(2,1)} %collective-permute-done.88), channel_id=1, source_target_pairs={{0,1},{1,0},{2,3},{3,2},{4,5},{5,4},{6,7},{7,6},{8,9},{9,8},{10,11... | collective-permute-start | bytes 3538952 | tf_op jit(solution)/shard_map/ppermute | solution.py:33
  (159 other events, 1691.7 us)

commit v2 on v1

--- a/solution.py
+++ b/solution.py
@@ -33,37 +33,35 @@
     return lax.ppermute(values, axis, [(i, i ^ bits) for i in range(size)])
 
 
-def gather_doubling(values, axis):
-    held = values[None]
-    bits = 1
-    while bits < lax.axis_size(axis):
-        held = jnp.concatenate([held, swap(held, axis, bits)])
-        bits *= 2
-    return held
-
-
 def gather_direct(values, axis):
     size = lax.axis_size(axis)
     if size > GROUP:
-        return gather_doubling(values, axis)
-    return jnp.stack([values] + [swap(values, axis, r) for r in range(1, size)])
+        return lax.all_gather(values, axis)
+    place = lax.axis_index(axis)
+    whole = jnp.zeros((size,) + values.shape, values.dtype)
+    for r in range(size):
+        piece = swap(values, axis, r) if r > 0 else values
+        whole = lax.dynamic_update_slice(whole, piece[None], (place ^ r,) + (0,) * values.ndim)
+    return whole
+
+
+def gather_small(values, axis):
+    size = lax.axis_size(axis)
+    copies = jnp.broadcast_to(values[None], (size,) + values.shape)
+    return lax.all_to_all(copies, axis, 0, 0, tiled=True)
 
 
 def scatter_sum(values, axis):
     size = values.shape[0]
+    order = jnp.arange(size) ^ lax.axis_index(axis)
+    values = jnp.take(values, order, axis=0)
+    bits = 1
     while size > 1:
         size //= 2
-        values = values[:size] + swap(values[size:].astype(bf16), axis, size).astype(f32)
+        pairs = values.reshape((size, 2) + values.shape[1:])
+        values = pairs[:, 0] + swap(pairs[:, 1].astype(bf16), axis, bits).astype(f32)
+        bits *= 2
     return values[0]
-
-
-def exchange(values, axis):
-    size = values.shape[0]
-    if size > GROUP:
-        order = jnp.arange(size) ^ lax.axis_index(axis)
-        moved = lax.all_to_all(jnp.take(values, order, axis=0), axis, 0, 0, tiled=True)
-        return jnp.take(moved, order, axis=0)
-    return jnp.stack([values[0]] + [swap(values[r], axis, r) for r in range(1, size)])
 
 
 def hidden_sum(values):
@@ -81,26 +79,7 @@
 
 
 def hidden_sum_small(values):
-    values = values + swap(values, "hidden", 1)
-    return values + swap(values, "hidden", 2)
-
-
-def gather_tokens(values, base):
-    place = lax.axis_index("hidden")
-    size = values.shape[0] // 4
-    own = lax.dynamic_slice_in_dim(values, place * size, size, 0)
-    if base > 0:
-        own = swap(own, "expert", base)
-    group = min(lax.axis_size("expert"), GROUP)
-    held = jnp.stack([own] + [swap(own, "expert", r) for r in range(1, group)])
-    far = swap(held, "hidden", 2)
-    near = swap(held, "hidden", 1)
-    both = swap(far, "hidden", 1)
-    count = held.shape[0]
-    whole = jnp.zeros((count, 4 * size, values.shape[1]), values.dtype)
-    for r, piece in ((0, held), (1, near), (2, far), (3, both)):
-        whole = lax.dynamic_update_slice(whole, piece, (0, (place ^ r) * size, 0))
-    return whole
+    return jnp.sum(lax.all_gather(values, "hidden"), axis=0)
 
 
 def causal_conv(values, segment, kernel, offset):
@@ -286,7 +265,13 @@
     )(grad, out, act, gate, pre, bias, decay, skip, keep, basis_b, basis_c, states)
 
 
-def sweeps(start, valid):
+def sinkhorn_body(place, packed, gates, grad_logits, all_grads):
+    experts = grad_logits.shape[0]
+    start = jnp.exp(packed[:, 0, :experts, :])
+    codes = packed[:, 0, experts : experts + 1, :]
+    grad_gates = jnp.sum(packed[:, :, experts + 1 : experts + 2, :], axis=1)
+    valid = (codes >= 0).astype(f32)
+    onehot = (lax.broadcasted_iota(jnp.int32, start.shape, 1).astype(f32) == codes).astype(f32)
     weights = start
     history = []
     for _ in range(SINK_ITERS):
@@ -295,73 +280,188 @@
         row_sums = jnp.sum(scaled, axis=1, keepdims=True)
         weights = scaled / row_sums
         history.append((columns, scaled, row_sums, weights))
-    return weights, history
-
-
-def chosen(codes, shape):
-    return (lax.broadcasted_iota(jnp.int32, shape, 1).astype(f32) == codes).astype(f32)
-
-
-def sinkhorn_body(logits, routes, gates):
-    start = jnp.exp(logits[...])
-    valid = (routes[:, 1:2, :] > 0).astype(f32)
-    weights, _ = sweeps(start, valid)
-    onehot = chosen(routes[:, 0:1, :], start.shape)
-    gates[...] = start.shape[1] * jnp.sum(weights * onehot, axis=1, keepdims=True)
-
-
-def sinkhorn_back_body(logits, routes, grad_gates, grad_logits):
-    start = jnp.exp(logits[...])
-    valid = (routes[:, 1:2, :] > 0).astype(f32)
-    _, history = sweeps(start, valid)
-    onehot = chosen(routes[:, 0:1, :], start.shape)
-    grads = start.shape[1] * grad_gates[...] * onehot
+    gates[...] = experts * jnp.sum(weights * onehot, axis=1, keepdims=True)
+    grads = experts * grad_gates * onehot
     for columns, scaled, row_sums, result in reversed(history):
         grads = (grads - jnp.sum(grads * result, axis=1, keepdims=True)) / row_sums
         term = jnp.sum(jnp.sum(grads * scaled, axis=2, keepdims=True), axis=0, keepdims=True)
         grads = (grads - valid * term) / columns
-    grad_logits[...] = (grads * start)[0]
-
-
-def sinkhorn(logits, routes):
-    count, experts, positions = logits.shape
+    all_grads[...] = grads * start
+    grad_logits[...] = all_grads[place[0]]
+
+
+def sinkhorn(place, packed, experts):
+    count, _, _, positions = packed.shape
     return pl.pallas_call(
         sinkhorn_body,
-        out_shape=shape_of(count, 1, positions),
+        in_specs=[pl.BlockSpec(memory_space=pltpu.SMEM), pl.BlockSpec(memory_space=pltpu.VMEM)],
+        out_shape=(shape_of(count, 1, positions), shape_of(experts, positions)),
+        scratch_shapes=[pltpu.VMEM((count, experts, positions), f32)],
         compiler_params=pltpu.CompilerParams(vmem_limit_bytes=48 * 2**20),
-        name="sinkhorn_forward",
-    )(logits, routes)
-
-
-def sinkhorn_back(logits, routes, grad_gates):
-    count, experts, positions = logits.shape
+        name="sinkhorn",
+    )(place, packed)
+
+
+def dot(left, right, left_dim=1, right_dim=0):
+    return lax.dot_general(
+        left, right, (((left_dim,), (right_dim,)), ((), ())), preferred_element_type=f32
+    )
+
+
+def slots_of(codes, experts, capacity):
+    positions = codes.shape[1]
+    member = lax.broadcasted_iota(jnp.int32, (experts, positions), 0).astype(f32) == codes
+    member = member.astype(bf16)
+    shape = (positions, positions)
+    prior = lax.broadcasted_iota(jnp.int32, shape, 0) < lax.broadcasted_iota(jnp.int32, shape, 1)
+    before = dot(member, prior.astype(f32).astype(bf16))
+    rank = jnp.sum(before * member.astype(f32), axis=0, keepdims=True)
+    return jnp.where(codes >= 0, codes * capacity + rank, -1.0)
+
+
+def picks(slots, first, count):
+    shape = (count, slots.shape[1])
+    return (lax.broadcasted_iota(jnp.int32, shape, 0) + first).astype(f32) == slots
+
+
+def gelu_pair(values):
+    root = 0.7978845608028654
+    square = values * values
+    bent = jnp.tanh(root * values * (1.0 + 0.044715 * square))
+    half = 0.5 * (1.0 + bent)
+    slope = half + 0.5 * values * (1.0 - bent * bent) * root * (1.0 + 3 * 0.044715 * square)
+    return values * half, slope
+
+
+def experts_body(codes, rows, grads, up, down, out, back, gate_sum, slots, outs, backs):
+    step = pl.program_id(0)
+    experts = pl.num_programs(0)
+    capacity = outs.shape[0] // experts
+
+    @pl.when(step == 0)
+    def _():
+        slots[...] = slots_of(codes[...], experts, capacity)
+        gate_sum[...] = jnp.zeros_like(gate_sum)
+
+    first = pl.multiple_of(step * capacity, capacity)
+    chosen = picks(slots[...], first, capacity).astype(f32)
+    pick = chosen.astype(bf16)
+    sent = dot(pick, rows[...]).astype(bf16)
+    sent_grad = dot(pick, grads[...]).astype(bf16)
+    active, slope = gelu_pair(dot(sent, up[0]))
+    plain = dot(sent_grad, down[0], 1, 1)
+    low = active.astype(bf16)
+    gate_slots = jnp.sum(low.astype(f32) * plain, axis=1, keepdims=True)
+    gate_sum[...] += jnp.sum(chosen * gate_slots, axis=0, keepdims=True)
+    outs[pl.ds(first, capacity), :] = dot(low, down[0]).astype(bf16)
+    backs[pl.ds(first, capacity), :] = dot((plain * slope).astype(bf16), up[0], 1, 1).astype(bf16)
+
+    @pl.when(step == experts - 1)
+    def _():
+        every = picks(slots[...], 0, outs.shape[0]).astype(f32).astype(bf16)
+        out[...] = dot(every, outs[...], 0, 0).astype(bf16)
+        back[...] = dot(every, backs[...], 0, 0).astype(bf16)
+
+
+def whole(shape):
+    return pl.BlockSpec(shape, lambda i: (0,) * len(shape), pipeline_mode=pl.Buffered(1))
+
+
+def experts_local(codes, rows, grads, up, down):
+    positions, width = rows.shape
+    experts, _, hidden = up.shape
+    slots = 3 * positions // 2
+    low = jax.ShapeDtypeStruct((positions, width), bf16)
     return pl.pallas_call(
-        sinkhorn_back_body,
-        out_shape=shape_of(experts, positions),
-        compiler_params=pltpu.CompilerParams(vmem_limit_bytes=48 * 2**20),
-        name="sinkhorn_backward",
-    )(logits, routes, grad_gates)
-
-
-def expert_grads(picker, rows, grad_rows, up, down, place, block):
-    count, slots, _ = picker.shape
-    experts, width, _ = up.shape
-
-    def spread(values):
-        picked = ein("nst,ntd->nsd", picker, values).astype(bf16)
-        picked = picked.reshape(count, experts, slots // experts, width)
-        return picked.transpose(1, 0, 2, 3).reshape(experts, count * slots // experts, width)
-
-    arrived = spread(rows)
-    arrived_grad = spread(grad_rows)
-    active, back = jax.vjp(jax.nn.gelu, ein("erd,edf->erf", arrived, up))
-    grad_pre = back(ein("erd,efd->erf", arrived_grad, down))[0].astype(bf16)
-    own = lax.dynamic_slice_in_dim(arrived, place * block, block, 2)
-    own_grad = lax.dynamic_slice_in_dim(arrived_grad, place * block, block, 2)
-    return (
-        ein("erd,erf->edf", own, grad_pre),
-        ein("erf,erd->efd", active.astype(bf16), own_grad),
-    )
+        experts_body,
+        grid=(experts,),
+        in_specs=[
+            whole((1, positions)),
+            whole((positions, width)),
+            whole((positions, width)),
+            pl.BlockSpec((1, width, hidden), lambda i: (i, 0, 0)),
+            pl.BlockSpec((1, hidden, width), lambda i: (i, 0, 0)),
+        ],
+        out_specs=(whole((positions, width)), whole((positions, width)), whole((1, positions))),
+        out_shape=(low, low, shape_of(1, positions)),
+        scratch_shapes=[
+            pltpu.VMEM((1, positions), f32),
+            pltpu.VMEM((slots, width), bf16),
+            pltpu.VMEM((slots, width), bf16),
+        ],
+        compiler_params=pltpu.CompilerParams(vmem_limit_bytes=40 * 2**20),
+        name="experts_local",
+    )(codes, rows, grads, up, down)
+
+
+def expert_grads_body(
+    codes, gates, rows, grads, own_rows, own_grads, up, down, up_grad, down_grad,
+    sent, sent_grads, own_sent, own_sent_grads,
+):
+    step = pl.program_id(0)
+    experts = pl.num_programs(0)
+    count, _, positions = codes.shape
+    capacity = sent.shape[1] // count
+
+    @pl.when(step == 0)
+    def _():
+        for r in range(count):
+            slots = slots_of(codes[r], experts, capacity)
+            chosen = picks(slots, 0, sent.shape[0] * capacity).astype(f32)
+            gate = jnp.sum(chosen * gates[r], axis=1, keepdims=True)
+            pick = chosen.astype(bf16)
+            part = pl.ds(r * positions, positions)
+            place = pl.ds(r * capacity, capacity)
+            for source, target, scale in (
+                (rows, sent, None),
+                (own_rows, own_sent, None),
+                (grads, sent_grads, gate),
+                (own_grads, own_sent_grads, gate),
+            ):
+                moved = dot(pick, source[part, :])
+                moved = (moved if scale is None else moved * scale).astype(bf16)
+                for i in range(sent.shape[0]):
+                    target[i, place, :] = moved[i * capacity : (i + 1) * capacity]
+
+    active, slope = gelu_pair(dot(sent[step], up[0]))
+    grad_pre = (dot(sent_grads[step], down[0], 1, 1) * slope).astype(bf16)
+    up_grad[0] = dot(own_sent[step], grad_pre, 0, 0)
+    down_grad[0] = dot(active.astype(bf16), own_sent_grads[step], 0, 0)
+
+
+def expert_grads(codes, gates, rows, grads, own_rows, own_grads, up, down):
+    count, _, positions = codes.shape
+    total, width = rows.shape
+    block = own_rows.shape[1]
+    experts, _, hidden = up.shape
+    slots = count * (3 * positions // (2 * experts))
+    return pl.pallas_call(
+        expert_grads_body,
+        grid=(experts,),
+        in_specs=[
+            whole((count, 1, positions)),
+            whole((count, 1, positions)),
+            whole((total, width)),
+            whole((total, width)),
+            whole((total, block)),
+            whole((total, block)),
+            pl.BlockSpec((1, width, hidden), lambda i: (i, 0, 0)),
+            pl.BlockSpec((1, hidden, width), lambda i: (i, 0, 0)),
+        ],
+        out_specs=(
+            pl.BlockSpec((1, block, hidden), lambda i: (i, 0, 0)),
+            pl.BlockSpec((1, hidden, block), lambda i: (i, 0, 0)),
+        ),
+        out_shape=(shape_of(experts, block, hidden), shape_of(experts, hidden, block)),
+        scratch_shapes=[
+            pltpu.VMEM((experts, slots, width), bf16),
+            pltpu.VMEM((experts, slots, width), bf16),
+            pltpu.VMEM((experts, slots, block), bf16),
+            pltpu.VMEM((experts, slots, block), bf16),
+        ],
+        compiler_params=pltpu.CompilerParams(vmem_limit_bytes=58 * 2**20),
+        name="expert_grads",
+    )(codes, gates, rows, grads, own_rows, own_grads, up, down)
 
 
 def local(
@@ -386,8 +486,8 @@
     expert_down,
 ):
     devices = lax.axis_size("expert")
+    hidden = lax.axis_size("hidden")
     index = lax.axis_index("expert")
-    order = jnp.arange(devices) ^ index
     positions, width = tokens.shape
     block = mixer_gain.shape[0]
     experts = expert_up.shape[0]
@@ -396,7 +496,6 @@
     rank = step_proj.shape[0]
     entries = decay_log.shape[0]
     taps = conv_weight.shape[0]
-    capacity = 3 * positions // (2 * experts)
 
     places = jnp.arange(positions, dtype=jnp.int32)
     first = seq_lengths[0, 0]
@@ -406,25 +505,32 @@
     valid_float = valid.astype(f32)
     earlier = jnp.concatenate([jnp.full((1,), -1, jnp.int32), segment[:-1]])
     persist = (segment == earlier).astype(f32)
-
+    codes = jnp.where(valid, routes[:, 0].astype(f32), -1.0)[None]
+
+    weight_x = gather_direct(proj_x.T, "expert").reshape(channels, width)
+    later = lax.all_gather(jnp.concatenate([proj_z.T, out_proj]), "expert")
+    weight_z = later[:, :own_channels].reshape(channels, width)
+    out_full = later[:, own_channels:].reshape(channels, width)
     vectors = jnp.concatenate([mixer_gain[None], moe_gain[None], router.T])
-    vectors = jnp.take(gather_doubling(vectors, "expert"), order, axis=0)
-    vectors = vectors.transpose(1, 0, 2).reshape(2 + experts, width)
+    small = [
+        conv_weight,
+        conv_bias[None],
+        step_bias[None],
+        skip_gain[None],
+        decay_log,
+        step_proj,
+        state_proj.T,
+    ]
+    count = sum(piece.shape[0] for piece in small)
+    spare = -(-vectors.size // own_channels) * own_channels - vectors.size
+    small.append(jnp.pad(vectors.reshape(-1), (0, spare)).reshape(-1, own_channels))
+    small = gather_small(jnp.concatenate(small), "expert")
+    vectors = small[:, count:].reshape(devices, -1)[:, : vectors.size]
+    vectors = vectors.reshape(devices, -1, block).transpose(1, 0, 2).reshape(-1, width)
     gain_one = vectors[0].astype(f32)
     gain_two = vectors[1].astype(f32)
     router_full = vectors[2:]
-    small = jnp.concatenate(
-        [
-            conv_weight,
-            conv_bias[None],
-            step_bias[None],
-            skip_gain[None],
-            decay_log,
-            step_proj,
-            state_proj.T,
-        ]
-    )
-    small = gather_doubling(small, "expert").transpose(1, 0, 2).reshape(-1, channels)
+    small = small[:, :count].transpose(1, 0, 2).reshape(count, channels)
     conv_kernel = small[:taps].astype(f32)
     conv_offset = small[taps].astype(f32)
     step_shift = small[taps + 1 : taps + 2].astype(f32)
@@ -432,13 +538,6 @@
     decay_full = small[taps + 3 : taps + 3 + entries].astype(f32)
     step_full = small[taps + 3 + entries : taps + 3 + entries + rank]
     state_full = small[taps + 3 + entries + rank :]
-    weight_x = gather_direct(proj_x.T, "expert").reshape(channels, width)
-    proj_z, weight_x = lax.optimization_barrier((proj_z, weight_x))
-    weight_z = gather_direct(proj_z.T, "expert").reshape(channels, width)
-    out_proj, weight_z = lax.optimization_barrier((out_proj, weight_z))
-    out_full = gather_direct(out_proj, "expert").reshape(channels, width)
-    codes = jnp.stack([routes[:, 0].astype(f32), valid_float])
-    codes = gather_doubling(codes, "expert")
 
     resid = tokens.astype(f32)
     scale_one = rms_scale(resid)
@@ -464,45 +563,29 @@
     scale_two = rms_scale(hidden_res)
     unit_two = hidden_res * scale_two
     normed_two = (unit_two * gain_two[None, :]).astype(bf16)
-    logits = gather_doubling(ein("ed,td->et", router_full, normed_two), "expert")
-    gates = sinkhorn(logits, codes)
-    gate_values = gates[0, 0]
-
-    prior = (places[:, None] > places[None, :]).astype(bf16)
-    slot_ids = jnp.arange(experts * capacity, dtype=f32)
-
-    def pick(some):
-        member = (some[:, 0, :, None] == jnp.arange(experts, dtype=f32)) & (some[:, 1, :, None] > 0)
-        member = member.astype(bf16)
-        slot = jnp.sum(ein("pt,nte->npe", prior, member) * member.astype(f32), axis=2)
-        target = jnp.where(some[:, 1] > 0, some[:, 0] * capacity + slot, -1.0)
-        return (slot_ids[None, :, None] == target[:, None, :]).astype(bf16)
-
-    group = min(devices, GROUP)
-    picker = pick(codes[:group])
-    own_picker = picker[0]
-
-    def spread(values):
-        return product(own_picker, values).astype(bf16).reshape(experts, capacity, width)
-
-    def collect(values):
-        return ein("st,sd->td", own_picker, values.astype(bf16).reshape(-1, width)).astype(bf16)
-
-    sent = spread(normed_two)
-    sent_grad = spread(cotangent)
-    active, gelu_back = jax.vjp(jax.nn.gelu, ein("erd,edf->erf", sent, expert_up))
-    active_low = active.astype(bf16)
-    plain_active = ein("erd,efd->erf", sent_grad, expert_down)
-    plain_pre = gelu_back(plain_active)[0].astype(bf16)
-    gate_slots = jnp.sum(active_low.astype(f32) * plain_active, axis=2).reshape(-1)
-    grad_gate = jnp.sum(own_picker.astype(f32) * gate_slots[:, None], axis=0)
-    grad_gate = gather_doubling(hidden_sum_small(grad_gate[None]), "expert")
-    plain_in = hidden_sum(collect(ein("erf,edf->erd", plain_pre, expert_up)))
-    returned = hidden_sum(collect(ein("erf,efd->erd", active_low, expert_down)))
+
+    rows = jnp.concatenate([normed, cotangent, normed_two], axis=1)
+    quarter = positions // hidden
+    rows = lax.dynamic_slice_in_dim(rows, lax.axis_index("hidden") * quarter, quarter, 0)
+    rows = lax.all_gather(rows, ("expert", "hidden"), tiled=True)
+
+    logits = ein("ed,td->et", router_full, normed_two)
+    out_part, back_part, gate_part = experts_local(
+        codes, normed_two, cotangent, expert_up, expert_down
+    )
+    packed = jnp.concatenate(
+        [logits, codes, gate_part, jnp.zeros((ROWS - 2, positions), f32)]
+    )
+    packed = gather_small(packed, ("expert", "hidden"))
+    packed = packed.reshape((devices, hidden) + packed.shape[1:])
+    plain_in = hidden_sum(back_part)
+    returned = hidden_sum(out_part)
+    gates, grad_logits = sinkhorn(index[None], packed, experts)
+    gate_values = lax.dynamic_index_in_dim(gates, index, 0, keepdims=False)[0]
     layer_out = (valid_float[:, None] * (hidden_res + gate_values[:, None] * returned)).astype(bf16)
     grad_expert_in = plain_in * (gate_values * valid_float)[:, None]
 
-    grad_logits = sinkhorn_back(logits, codes, grad_gate).astype(bf16)
+    grad_logits = grad_logits.astype(bf16)
     router_grad = ein("td,et->ed", normed_two, grad_logits)
     grad_normed_two = ein("et,ed->td", grad_logits, router_full) + grad_expert_in
     grad_out = cotangent.astype(f32) * valid_float[:, None]
@@ -512,9 +595,9 @@
         grad_unit_two - unit_two * jnp.mean(grad_unit_two * unit_two, axis=-1, keepdims=True)
     )
     grad_branch = grad_hidden.astype(bf16)
+    grad_mixed = ein("td,cd->tc", grad_branch, out_full)
     out_grad = ein("tc,td->cd", mixed, grad_branch).reshape(devices, own_channels, width)
     out_grad = scatter_sum(out_grad, "expert")
-    grad_mixed = ein("td,cd->tc", grad_branch, out_full)
     (
         grad_act_scan,
         grad_z_low,
@@ -538,12 +621,25 @@
         basis_c,
         states,
     )
+
+    def cut(values):
+        return values.astype(bf16).reshape(-1, devices, own_channels).transpose(1, 0, 2)
+
     step_proj_grad = ein("tr,tc->rc", rank_low, grad_step_low)
     grad_rank = ein("tc,rc->tr", grad_step_low, step_full)
     grad_projected = hidden_sum_small(
         jnp.concatenate([grad_rank, jnp.sum(part_b, axis=2), jnp.sum(part_c, axis=2)], axis=1)
     )
     grad_proj_low = grad_projected.astype(bf16)
+    vector_grads = jnp.concatenate([gain_two_grad[None], router_grad]).astype(bf16)
+    vector_grads = vector_grads.reshape(-1, devices, block).transpose(1, 0, 2)
+    shared = [
+        cut(jnp.concatenate([grad_z_low, step_bias_grad.astype(bf16)])),
+        cut(jnp.concatenate([skip_grad, decay_grad, step_proj_grad])),
+        vector_grads.reshape(devices, -1, own_channels),
+    ]
+    early = lax.all_to_all(jnp.concatenate(shared, axis=1), "expert", 0, 0, tiled=True)
+
     state_grad = ein("tc,tk->kc", activity_low, grad_proj_low)
     grad_activity = grad_act_scan + ein("tk,kc->tc", grad_proj_low, state_full)
 
@@ -553,64 +649,76 @@
     _, conv_back = jax.vjp(conv_fn, inner_x, conv_kernel, conv_offset)
     grad_inner_x, conv_weight_grad, conv_bias_grad = conv_back(grad_activity)
     grad_x_low = grad_inner_x.astype(bf16)
-    both = jnp.stack([grad_x_low, grad_z_low]).reshape(2, positions, devices, own_channels)
-    both = exchange(both.transpose(2, 0, 1, 3), "expert")
-    grad_normed = hidden_sum(product(grad_x_low, weight_x) + product(grad_z_low, weight_z))
-    gain_one_grad = jnp.sum(grad_normed * unit_one, axis=0)
+    grad_normed_part = product(grad_x_low, weight_x) + product(grad_z_low, weight_z)
+    gain_one_part = jnp.sum(grad_normed_part * unit_one, axis=0).astype(bf16)
+    shared = [
+        cut(grad_x_low),
+        cut(jnp.concatenate([conv_weight_grad, conv_bias_grad[None], state_grad])),
+        gain_one_part.reshape(devices, -1, own_channels),
+    ]
+    late = lax.all_to_all(jnp.concatenate(shared, axis=1), "expert", 0, 0, tiled=True)
+    grad_normed = hidden_sum(grad_normed_part)
     grad_unit_one = grad_normed * gain_one[None, :]
     tokens_grad = grad_hidden + scale_one * (
         grad_unit_one - unit_one * jnp.mean(grad_unit_one * unit_one, axis=-1, keepdims=True)
     )
 
-    totals = None
-    sources = (normed, normed_two, cotangent)
-    for base in range(0, devices, group):
-        if base > 0:
-            sources, totals = lax.optimization_barrier((sources, totals))
-            picker = pick(codes[base : base + group])
-        normed_all, rows_all, cotangent_all = [gather_tokens(v, base) for v in sources]
-        grad_all = cotangent_all.astype(f32) * gates[base : base + group, 0, :, None]
-        parts = expert_grads(
-            picker, rows_all, grad_all.astype(bf16), expert_up, expert_down, index, block
-        ) + (
-            ein("ntd,ntc->dc", normed_all, both[base : base + group, 0]),
-            ein("ntd,ntc->dc", normed_all, both[base : base + group, 1]),
+    early_sum = jnp.sum(early[:, positions:].astype(f32), axis=0)
+    late_sum = jnp.sum(late[:, positions:].astype(f32), axis=0)
+    vector_grads = early_sum[2 + entries + rank :].reshape(-1, block)
+    gain_one_grad = hidden_sum_small(late_sum[taps + 1 + state_full.shape[0] :]).reshape(-1)
+    inner_all = [part[:, :positions].reshape(-1, own_channels) for part in (late, early)]
+    normed_all = rows[:, :width]
+    proj_x_grad = ein("td,tc->dc", normed_all, inner_all[0])
+    proj_z_grad = ein("td,tc->dc", normed_all, inner_all[1])
+
+    def add_group(start):
+        size = group * positions
+        grads_all = lax.dynamic_slice(rows, (start * positions, width), (size, width))
+        rows_all = lax.dynamic_slice(rows, (start * positions, 2 * width), (size, width))
+        own = index * block
+        return expert_grads(
+            lax.dynamic_slice_in_dim(packed[:, 0, experts : experts + 1], start, group, 0),
+            lax.dynamic_slice_in_dim(gates, start, group, 0),
+            rows_all,
+            grads_all,
+            lax.dynamic_slice_in_dim(rows_all, own, block, 1),
+            lax.dynamic_slice_in_dim(grads_all, own, block, 1),
+            expert_up,
+            expert_down,
         )
-        totals = parts if base == 0 else tuple(a + b for a, b in zip(totals, parts))
-    up_grad, down_grad, proj_x_grad, proj_z_grad = totals
-
-    vector_grads = jnp.concatenate([gain_one_grad[None], gain_two_grad[None], router_grad])
-    vector_grads = vector_grads.reshape(2 + experts, devices, block).transpose(1, 0, 2)
-    vector_grads = scatter_sum(jnp.take(vector_grads, order, axis=0), "expert")
-    small_grads = jnp.concatenate(
-        [
-            conv_weight_grad,
-            conv_bias_grad[None],
-            step_bias_grad,
-            skip_grad,
-            decay_grad,
-            step_proj_grad,
-            state_grad,
-        ]
-    )
-    small_grads = small_grads.reshape(-1, devices, own_channels).transpose(1, 0, 2)
-    small_grads = scatter_sum(small_grads, "expert")
+
+    group = min(devices, GROUP)
+    if group == devices:
+        up_grad, down_grad = add_group(0)
+    else:
+
+        def add(total, start):
+            part = add_group(start)
+            return (total[0] + part[0], total[1] + part[1]), None
+
+        zero = (
+            jnp.zeros((experts, block, expert_up.shape[2]), f32),
+            jnp.zeros((experts, expert_down.shape[1], block), f32),
+        )
+        (up_grad, down_grad), _ = lax.scan(add, zero, jnp.arange(0, devices, group))
+
     return (
         layer_out,
         tokens_grad,
-        vector_grads[0],
+        gain_one_grad,
         proj_x_grad,
         proj_z_grad,
-        small_grads[:taps],
-        small_grads[taps],
-        small_grads[taps + 3 + entries + rank :].T,
-        small_grads[taps + 3 + entries : taps + 3 + entries + rank],
-        small_grads[taps + 1],
-        small_grads[taps + 3 : taps + 3 + entries],
-        small_grads[taps + 2],
+        late_sum[:taps],
+        late_sum[taps],
+        late_sum[taps + 1 : taps + 1 + state_full.shape[0]].T,
+        early_sum[2 + entries : 2 + entries + rank],
+        early_sum[0],
+        early_sum[2 : 2 + entries],
+        early_sum[1],
         out_grad,
-        vector_grads[1],
-        vector_grads[2:].T,
+        vector_grads[0],
+        vector_grads[1:].T,
         up_grad,
         down_grad,
     )

time: 657 us -> 382 us (0.58)
  waiting for transfers between devices: 236 us -> 97.8 us
  starting transfers between devices: 132 us -> 44.4 us
  matrix products: 108 us -> 23.9 us
  local copies, waits for them, and re-layouts: 112 us -> 61.4 us
  Pallas kernels: 32 us -> 81.6 us
  blocking collectives: 0 us -> 19.5 us
  between operations: 4.19 us -> 17.2 us
  other arithmetic: 22.9 us -> 31.1 us
    ppermute x100 -> x22, waiting for transfers between devices: 236 us -> 64.8 us  [swap(): return lax.ppermute(values, axis, [(i, i ^ bits) for i in range(size)])]
    ppermute x100 -> x22, starting transfers between devices: 132 us -> 26.6 us  [swap(): return lax.ppermute(values, axis, [(i, i ^ bits) for i in range(size)])]
    dot_general x25 -> x14, matrix products: 102 us -> 19.5 us  [ein(): return jnp.einsum(spec, left, right, preferred_element_type=f32)]
    pallas_call x2 -> x3, Pallas kernels: 2.72 us -> 51 us  [the longest x1 30.5 us: expert_grads(): pl.pallas_call(expert_grads_body, grid=(experts,), in_specs=[whole((count...]
    all_gather x0 -> x2, waiting for transfers between devices: none -> 32 us  [the longest x1 32 us: local(): later = lax.all_gather(jnp.concatenate([proj_z.T, out_proj]), 'expert')]
    unnamed x237 -> x164, local copies, waits for them, and re-layouts: 41.7 us -> 17.2 us
    dynamic_update_slice x12 -> x8, local copies, waits for them, and re-layouts: 23.6 us -> 0.19 us  [gather_direct(): lax.dynamic_update_slice(whole, piece[None], (place ^ r,) + (0,) * values...]
    all_gather x0 -> x3, blocking collectives: none -> 19.5 us  [hidden_sum_small(): return jnp.sum(lax.all_gather(values, 'hidden'), axis=0)]
  transfers between devices with their start and end apart: 100 -> 28, of which waited for: 51 -> 12; matrix products, arithmetic and copies ran while one was open for 28% -> 21% of each run, Pallas kernels for 5% -> 11%
where the time goes in v2:
time: 382 us; the launch traced here: 377 us
  waiting for transfers between devices  97.8 us (26%)
  Pallas kernels  81.6 us (21%)
  local copies, waits for them, and re-layouts  61.4 us (16%)
  starting transfers between devices  44.4 us (12%)
  other arithmetic  31.1 us (8%)
  matrix products  23.9 us (6%)
  blocking collectives  19.5 us (5%)
  between operations  17.2 us (5%)
    ppermute x22, waiting for transfers between devices, swap(): return lax.ppermute(values, axis, [(i, i ^ bits) for i in range(size)])  64.8 us
    all_gather x1, waiting for transfers between devices, local(): later = lax.all_gather(jnp.concatenate([proj_z.T, out_proj]), 'expert')  32 us
    pallas_call x1, Pallas kernels, expert_grads(): pl.pallas_call(expert_grads_body, grid=(experts,), in_specs=[whole((count...  30.5 us
    ppermute x22, starting transfers between devices, swap(): return lax.ppermute(values, axis, [(i, i ^ bits) for i in range(size)])  26.6 us
    pallas_call x1, Pallas kernels, scan_backward(): pl.pallas_call(scan_backward_body, out_shape=(shape_of(positions, channel...  20.8 us
    all_gather x3, blocking collectives, hidden_sum_small(): return jnp.sum(lax.all_gather(values, 'hidden'), axis=0)  19.5 us
    dot_general x14, matrix products, ein(): return jnp.einsum(spec, left, right, preferred_element_type=f32)  19.5 us
    pallas_call x1, Pallas kernels, experts_local(): pl.pallas_call(experts_body, grid=(experts,), in_specs=[whole((1, positio...  18.7 us
  transfers between devices with their start and end apart: 28, of which 12 were waited for; matrix products, arithmetic and copies ran while one was open for 21% of the time, Pallas kernels for 11%

profile of v2, /device:TPU:0, one launch (start us, length us, event | category | flops | bytes accessed | tf_op | source)
XLA Modules:
  0.0 376.9 jit_solution(14946002713583563294)
XLA Ops:
  7.2 3.0 collective-permute-start
  11.8 3.0 collective-permute-start.3
  24.6 4.9 %all-to-all-start = ((bf16[8,219,72]{1,2,0:T(8,128)(2,1)}), bf16[8,219,72]{1,2,0:T(8,128)(2,1)S(1)}, u32[]{:S(2)}, u32[]{:S(2)}) async-start(bf16[8,219,72]{1,2,0:T(8,128)(2,1)} %broadcast_in_dim.59), calls=%async_computation | async-start | bytes 589824 | tf_op jit(solution)/shard_map/all_to_all | solution.py:51
  35.7 3.8 %collective-permute-start.5 = (bf16[72,1152]{1,0:T(8,128)(2,1)S(1)}, bf16[72,1152]{1,0:T(8,128)(2,1)S(1)}, u32[]{:S(2)}, u32[]{:S(2)}) collective-permute-start(bf16[72,1152]{1,0:T(8,128)(2,1)S(1)} %bitcast.188), channel_id=1, source_target_pairs={{0,24},{4,28},{8,16},{12,20},{16,8},{20,12},{24,0},{28,4},{1,25},{... | collective-permute-start | bytes 497672 | tf_op jit(solution)/shard_map/ppermute | solution.py:33
  43.4 4.7 %collective-permute-done.6 = bf16[72,1152]{1,0:T(8,128)(2,1)S(1)} collective-permute-done((bf16[72,1152]{1,0:T(8,128)(2,1)S(1)}, bf16[72,1152]{1,0:T(8,128)(2,1)S(1)}, u32[]{:S(2)}, u32[]{:S(2)}) %collective-permute-start.6) | collective-permute-done | bytes 165920 | tf_op jit(solution)/shard_map/ppermute | solution.py:33
  52.5 7.2 %all-gather = f32[1024,104]{0,1:T(8,128)S(1)} all-gather(f32[256,104]{0,1:T(8,128)S(1)} %fusion.56), channel_id=2, replica_groups=mesh['expert'=8,'hidden'=4] {'hidden'}, dimensions={0}, use_global_device_ids=true | all-gather | bytes 532480 | tf_op jit(solution)/shard_map/all_gather | solution.py:82
  62.4 32.0 %all-gather.10.cloned.1.call-done = bf16[1152,1152]{1,0:T(8,128)(2,1)} async-done(((bf16[144,1152]{1,0:T(8,128)(2,1)}), bf16[1152,1152]{1,0:T(8,128)(2,1)}) %all-gather.10.cloned.1.call-update) | async-done | bytes 2654224 | tf_op jit(solution)/shard_map/all_gather | solution.py:511
  100.0 9.8 %scan_forward.1 = (bf16[256,576]{1,0:T(8,128)(2,1)S(1)}, f32[256,576]{1,0:T(8,128)S(1)}, f32[256,16,640]{2,1,0:T(8,128)}) custom-call(f32[256,576]{1,0:T(8,128)S(1)} %copy-done.3, f32[256,576]{1,0:T(8,128)S(1)} %get-tuple-element.188.act, f32[256,576]{1,0:T(8,128)S(1)} %fusion.57.gate, f32[256,16,128]{2,1,0:T(8,128)S(1)} %broadcast_in_dim.128.basis_b, ...), custom_call_target="tpu_custom_call" | custom-call | tf_op jit(solution)/shard_map/scan_forward/pallas_call | solution.py:226
  114.0 7.6 %collective-permute-done.8 = bf16[128,1152]{1,0:T(8,128)(2,1)S(1)} collective-permute-done((bf16[128,1152]{1,0:T(8,128)(2,1)S(1)}, bf16[128,1152]{1,0:T(8,128)(2,1)S(1)}, u32[]{:S(2)}, u32[]{:S(2)}) %collective-permute-start.8) | collective-permute-done | bytes 294944 | tf_op jit(solution)/shard_map/ppermute | solution.py:33
  127.4 18.7 %experts_local.1 = (bf16[256,1152]{1,0:T(8,128)(2,1)S(1)}, bf16[256,1152]{1,0:T(8,128)(2,1)S(1)}, f32[1,256]{1,0:T(1,128)S(1)}) custom-call(f32[1,256]{1,0:T(1,128)S(1)} %compare_select_fusion.1.codes, bf16[256,1152]{1,0:T(8,128)(2,1)S(1)} %multiply_convert_fusion.1.rows, bf16[256,1152]{1,0:T(8,128)(2,1)S(1)} %copy-done.4, bf16[8,1152,768]{2,1,0:T(8,128)(2,1)} %up.3, ...), custom_call_target="tpu_custom_call" | custom-call | tf_op jit(solution)/shard_map/experts_local/pallas_call | solution.py:375
  148.3 3.4 all-to-all-start.1
  155.5 16.7 %collective-permute-done.11 = bf16[128,1152]{1,0:T(8,128)(2,1)S(1)} collective-permute-done((bf16[128,1152]{1,0:T(8,128)(2,1)S(1)}, bf16[128,1152]{1,0:T(8,128)(2,1)S(1)}, u32[]{:S(2)}, u32[]{:S(2)}) %collective-permute-start.11) | collective-permute-done | bytes 294944 | tf_op jit(solution)/shard_map/ppermute | solution.py:33
  172.3 6.7 %collective-permute-done.14 = bf16[128,1152]{1,0:T(8,128)(2,1)S(1)} collective-permute-done((bf16[128,1152]{1,0:T(8,128)(2,1)S(1)}, bf16[128,1152]{1,0:T(8,128)(2,1)S(1)}, u32[]{:S(2)}, u32[]{:S(2)}) %collective-permute-start.14) | collective-permute-done | bytes 294944 | tf_op jit(solution)/shard_map/ppermute | solution.py:33
  182.1 3.1 multiply_reduce_fusion
  188.1 20.8 %scan_backward.1 = (f32[256,576]{1,0:T(8,128)}, bf16[256,576]{1,0:T(8,128)(2,1)}, bf16[256,576]{1,0:T(8,128)(2,1)}, f32[256,16,128]{2,1,0:T(8,128)}, f32[256,16,...) custom-call(f32[256,576]{1,0:T(8,128)} %fusion.29.grad, f32[256,576]{1,0:T(8,128)} %copy-done.8, ...), custom_call_target="tpu_custom_call" | custom-call | tf_op jit(solution)/shard_map/scan_backward/pallas_call | solution.py:250
  211.2 2.3 reduce_sum.186
  213.9 7.0 %all-gather.2 = f32[1024,104]{0,1:T(8,128)S(1)} all-gather(f32[256,104]{0,1:T(8,128)S(1)} %pad_maximum_fusion.4), channel_id=4, replica_groups=mesh['expert'=8,'hidden'=4] {'hidden'}, dimensions={0}, use_global_device_ids=true | all-gather | bytes 532480 | tf_op jit(solution)/shard_map/all_gather | solution.py:82
  236.9 5.5 %all-to-all-start.3 = ((bf16[8,364,72]{1,2,0:T(8,128)(2,1)}), bf16[8,364,72]{1,2,0:T(8,128)(2,1)}, u32[]{:S(2)}, u32[]{:S(2)}) async-start(bf16[8,364,72]{1,2,0:T(8,128)(2,1)} %pad_maximum_fusion.1), calls=%async_computation.3 | async-start | bytes 884736 | tf_op jit(solution)/shard_map/all_to_all | solution.py:641
  244.5 4.1 %gather_fusion = f32[8,72,1152]{2,1,0:T(8,128)} fusion(f32[8,72,1152]{2,1,0:T(8,128)} %bitcast.160, s32[1024]{0:T(1024)} %pad_clamp_fusion), kind=kCustom, calls=%fused_computation | custom fusion | bytes 5308448 | tf_op jit(solution)/shard_map/jit(_take)/gather | solution.py:57
  255.9 6.2 %collective-permute-done.17 = bf16[128,1152]{1,0:T(8,128)(2,1)S(1)} collective-permute-done((bf16[128,1152]{1,0:T(8,128)(2,1)S(1)}, bf16[128,1152]{1,0:T(8,128)(2,1)S(1)}, u32[]{:S(2)}, u32[]{:S(2)}) %collective-permute-start.17) | collective-permute-done | bytes 294944 | tf_op jit(solution)/shard_map/ppermute | solution.py:33
  262.3 5.8 %collective-permute-done.19 = bf16[4,72,1152]{2,1,0:T(8,128)(2,1)S(1)} collective-permute-done((bf16[4,72,1152]{2,1,0:T(8,128)(2,1)S(1)}, bf16[4,72,1152]{2,1,0:T(8,128)(2,1)S(1)}, u32[]{:S(2)}, u32[]{:S(2)}) %collective-permute-start.19) | collective-permute-done | bytes 663584 | tf_op jit(solution)/shard_map/ppermute | solution.py:33
  282.0 3.9 %all-to-all-start.2 = ((bf16[8,367,72]{1,2,0:T(8,128)(2,1)}), bf16[8,367,72]{1,2,0:T(8,128)(2,1)S(1)}, u32[]{:S(2)}, u32[]{:S(2)}) async-start(bf16[8,367,72]{1,2,0:T(8,128)(2,1)} %pad_maximum_fusion), calls=%async_computation.2 | async-start | bytes 884736 | tf_op jit(solution)/shard_map/all_to_all | solution.py:659
  287.2 3.0 collective-permute-start.21
  290.2 2.5 fusion.13
  292.7 11.9 %collective-permute-done.21 = bf16[1,72,1152]{2,1,0:T(8,128)(2,1)S(1)} collective-permute-done((bf16[1,72,1152]{2,1,0:T(8,128)(2,1)S(1)}, bf16[1,72,1152]{2,1,0:T(8,128)(2,1)S(1)}, u32[]{:S(2)}, u32[]{:S(2)}) %collective-permute-start.21) | collective-permute-done | bytes 165920 | tf_op jit(solution)/shard_map/ppermute | solution.py:33
  305.6 5.3 %all-gather.4 = f32[4,2,72]{2,1,0:T(2,128)S(1)} all-gather(f32[1,2,72]{2,1,0:T(2,128)S(1)} %copy.327), channel_id=5, replica_groups=mesh['expert'=8,'hidden'=4] {'hidden'}, dimensions={0}, use_global_device_ids=true | all-gather | bytes 2880 | tf_op jit(solution)/shard_map/all_gather | solution.py:82
  313.7 6.7 %fusion.49 = (bf16[2048,1152]{1,0:T(8,128)(2,1)S(1)}, bf16[2048,1152]{1,0:T(8,128)(2,1)}) fusion(bf16[2048,3456]{1,0:T(8,128)(2,1)} %all-gather.8.cloned.1.call-done), kind=kLoop, calls=%fused_computation.165 | loop fusion | bytes 18874368 | tf_op jit(solution)/shard_map/dynamic_slice | solution.py:677
  320.3 4.0 %constant_dynamic-slice_fusion.1.own_rows = bf16[2048,144]{1,0:T(8,128)(2,1)} fusion(bf16[2048,1152]{1,0:T(8,128)(2,1)} %get-tuple-element.192.rows, s32[]{:T(128)S(6)} %select_n.132), kind=kLoop, calls=%fused_computation.131 | loop fusion | bytes 1179652 | tf_op jit(solution)/shard_map/dynamic_slice | solution.py:685
  325.7 30.5 %expert_grads.1 = (f32[8,144,768]{2,1,0:T(8,128)}, f32[8,768,144]{2,1,0:T(8,128)}) custom-call(f32[8,1,256]{2,1,0:T(1,128)} %slice_bitcast_fusion.7.codes, f32[8,1,256]{2,1,0:T(1,128)} %copy-done.12, bf16[2048,1152]{1,0:T(8,128)(2,1)} %get-tuple-element.192.rows, bf16[2048,1152]{1,0:T(8,128)(2,1)} %copy-done.17, ...), custom_call_target="tpu_custom_call" | custom-call | tf_op jit(solution)/shard_map/expert_grads/pallas_call | solution.py:438
  356.2 5.8 %copy.347 = f32[8,768,144]{1,2,0:T(8,128)} copy(f32[8,768,144]{2,1,0:T(8,128)} %get-tuple-element.171) | data formatting | bytes 7077888
  362.0 3.9 %fusion.2 = f32[1152,72]{0,1:T(8,128)} fusion(bf16[2048,72]{0,1:T(8,128)(2,1)S(1)} %bitcast.180, bf16[2048,3456]{1,0:T(8,128)(2,1)} %all-gather.8.cloned.1.call-done), kind=kOutput, calls=%fused_computation.3 | convolution fusion | flops 339738624 | bytes 5345280 | tf_op jit(solution)/shard_map/td,tc->dc/dot_general | solution.py:24
  365.9 3.9 %fusion = f32[1152,72]{0,1:T(8,128)} fusion(bf16[2048,72]{0,1:T(8,128)(2,1)S(1)} %bitcast.179, bf16[2048,3456]{1,0:T(8,128)(2,1)} %all-gather.8.cloned.1.call-done), kind=kOutput, calls=%fused_computation.1 | convolution fusion | flops 339738624 | bytes 5345280 | tf_op jit(solution)/shard_map/td,tc->dc/dot_general | solution.py:24
  (380 shorter events, 102.0 us)
Async XLA Ops:
  7.2 28.5 %collective-permute-start = (bf16[72,1152]{1,0:T(8,128)(2,1)}, bf16[72,1152]{1,0:T(8,128)(2,1)S(1)}, u32[]{:S(2)}, u32[]{:S(2)}) collective-permute-start(bf16[72,1152]{1,0:T(8,128)(2,1)} %bitcast.183), channel_id=1, source_target_pairs={{0,4},{4,0},{8,12},{12,8},{16,20},{20,16},{24,28},{28,24},{1,5},{5... | collective-permute-start | bytes 497672 | tf_op jit(solution)/shard_map/ppermute | solution.py:33
  10.2 29.4 %collective-permute-start.1 = (bf16[72,1152]{1,0:T(8,128)(2,1)}, bf16[72,1152]{1,0:T(8,128)(2,1)S(1)}, u32[]{:S(2)}, u32[]{:S(2)}) collective-permute-start(bf16[72,1152]{1,0:T(8,128)(2,1)} %bitcast.184), channel_id=1, source_target_pairs={{0,8},{4,12},{8,0},{12,4},{16,24},{20,28},{24,16},{28,20},{1,9},{5... | collective-permute-start | bytes 497672 | tf_op jit(solution)/shard_map/ppermute | solution.py:33
  11.8 29.3 %collective-permute-start.2 = (bf16[72,1152]{1,0:T(8,128)(2,1)}, bf16[72,1152]{1,0:T(8,128)(2,1)S(1)}, u32[]{:S(2)}, u32[]{:S(2)}) collective-permute-start(bf16[72,1152]{1,0:T(8,128)(2,1)} %bitcast.185), channel_id=1, source_target_pairs={{0,12},{4,8},{8,4},{12,0},{16,28},{20,24},{24,20},{28,16},{1,13},{... | collective-permute-start | bytes 497672 | tf_op jit(solution)/shard_map/ppermute | solution.py:33
  11.8 29.4 %collective-permute-start.3 = (bf16[72,1152]{1,0:T(8,128)(2,1)}, bf16[72,1152]{1,0:T(8,128)(2,1)S(1)}, u32[]{:S(2)}, u32[]{:S(2)}) collective-permute-start(bf16[72,1152]{1,0:T(8,128)(2,1)} %bitcast.186), channel_id=1, source_target_pairs={{0,16},{4,20},{8,24},{12,28},{16,0},{20,4},{24,8},{28,12},{1,17},{... | collective-permute-start | bytes 497672 | tf_op jit(solution)/shard_map/ppermute | solution.py:33
  14.8 26.4 %collective-permute-start.4 = (bf16[72,1152]{1,0:T(8,128)(2,1)}, bf16[72,1152]{1,0:T(8,128)(2,1)S(1)}, u32[]{:S(2)}, u32[]{:S(2)}) collective-permute-start(bf16[72,1152]{1,0:T(8,128)(2,1)} %bitcast.187), channel_id=1, source_target_pairs={{0,20},{4,16},{8,28},{12,24},{16,4},{20,0},{24,12},{28,8},{1,21},{... | collective-permute-start | bytes 497672 | tf_op jit(solution)/shard_map/ppermute | solution.py:33
  24.6 23.6 %all-to-all-start = ((bf16[8,219,72]{1,2,0:T(8,128)(2,1)}), bf16[8,219,72]{1,2,0:T(8,128)(2,1)S(1)}, u32[]{:S(2)}, u32[]{:S(2)}) async-start(bf16[8,219,72]{1,2,0:T(8,128)(2,1)} %broadcast_in_dim.59), calls=%async_computation | async-start | bytes 589824 | tf_op jit(solution)/shard_map/all_to_all | solution.py:51
  29.5 65.0 %all-gather.10.cloned.1.call-start = ((), (), s32[]{:S(2)}) async-start(), calls=%async_computation.5 | async-start | bytes 2985984 | tf_op jit(solution)/shard_map/all_gather | solution.py:511
  30.3 283.4 %all-gather.8.cloned.1.call-start = ((), (), s32[]{:S(2)}) async-start(), calls=%async_computation.4 | async-start | bytes 14598144 | tf_op jit(solution)/shard_map/all_gather | solution.py:570
  34.9 65.1 %copy-start.7 = (f32[256,1]{1,0:T(8,128)}, f32[256,1]{1,0:T(8,128)S(1)}, u32[]{:S(2)}) copy-start(f32[256,1]{1,0:T(8,128)S(1)} %convert_element_type.329.keep) | copy-start | bytes 3076
  35.7 7.7 %collective-permute-start.5 = (bf16[72,1152]{1,0:T(8,128)(2,1)S(1)}, bf16[72,1152]{1,0:T(8,128)(2,1)S(1)}, u32[]{:S(2)}, u32[]{:S(2)}) collective-permute-start(bf16[72,1152]{1,0:T(8,128)(2,1)S(1)} %bitcast.188), channel_id=1, source_target_pairs={{0,24},{4,28},{8,16},{12,20},{16,8},{20,12},{24,0},{28,4},{1,25},{... | collective-permute-start | bytes 497672 | tf_op jit(solution)/shard_map/ppermute | solution.py:33
  39.6 8.5 %collective-permute-start.6 = (bf16[72,1152]{1,0:T(8,128)(2,1)S(1)}, bf16[72,1152]{1,0:T(8,128)(2,1)S(1)}, u32[]{:S(2)}, u32[]{:S(2)}) collective-permute-start(bf16[72,1152]{1,0:T(8,128)(2,1)S(1)} %bitcast.189), channel_id=1, source_target_pairs={{0,28},{4,24},{8,20},{12,16},{16,12},{20,8},{24,4},{28,0},{1,29},{... | collective-permute-start | bytes 497672 | tf_op jit(solution)/shard_map/ppermute | solution.py:33
  52.2 47.8 %copy-start.1 = (f32[256,576]{1,0:T(8,128)}, f32[256,576]{1,0:T(8,128)S(1)}, u32[]{:S(2)}) copy-start(f32[256,576]{1,0:T(8,128)S(1)} %get-tuple-element.188.act) | copy-start | bytes 1769476
  60.5 39.5 %copy-start.10 = (f32[1,576]{1,0:T(1,128)}, f32[1,576]{1,0:T(1,128)S(1)}, u32[]{:S(2)}) copy-start(f32[1,576]{1,0:T(1,128)S(1)} %reshape.398.bias) | copy-start | bytes 6916
  61.3 38.7 %copy-start.11 = (f32[1,576]{1,0:T(1,128)}, f32[1,576]{1,0:T(1,128)S(1)}, u32[]{:S(2)}) copy-start(f32[1,576]{1,0:T(1,128)S(1)} %reshape.400.skip) | copy-start | bytes 6916
  110.8 1.6 collective-permute-start.7
  112.4 9.1 %collective-permute-start.8 = (bf16[128,1152]{1,0:T(8,128)(2,1)S(1)}, bf16[128,1152]{1,0:T(8,128)(2,1)S(1)}, u32[]{:S(2)}, u32[]{:S(2)}) collective-permute-start(bf16[128,1152]{1,0:T(8,128)(2,1)S(1)} %add_convert_fusion.8), channel_id=1, source_target_pairs={{0,2},{1,3},{2,0},{3,1},{4,6},{5,7},{6,4},{7,5},{8,10},{9,11},{10,... | collective-permute-start | bytes 884744 | tf_op jit(solution)/shard_map/ppermute | solution.py:33
  121.7 1.6 collective-permute-start.9
  146.9 5.2 %collective-permute-start.10 = (bf16[128,1152]{1,0:T(8,128)(2,1)}, bf16[128,1152]{1,0:T(8,128)(2,1)}, u32[]{:S(2)}, u32[]{:S(2)}) collective-permute-start(bf16[128,1152]{1,0:T(8,128)(2,1)} %constant_dynamic-slice_fusion.3), channel_id=1, source_target_pairs={{0,1},{1,0},{2,3},{3,2},{4,5},{5,4},{6,7},{7,6},{8,9},{9,8},{10,11... | collective-permute-start | bytes 884744 | tf_op jit(solution)/shard_map/ppermute | solution.py:33
  148.3 31.9 %all-to-all-start.1 = ((f32[32,16,256]{2,1,0:T(8,128)}), f32[32,16,256]{2,1,0:T(8,128)S(1)}, u32[]{:S(2)}, u32[]{:S(2)}) async-start(f32[32,16,256]{2,1,0:T(8,128)} %broadcast_in_dim.133), calls=%async_computation.1 | async-start | bytes 1048576 | tf_op jit(solution)/shard_map/all_to_all | solution.py:51
  151.7 3.3 collective-permute-start.13
  153.2 19.0 %collective-permute-start.11 = (bf16[128,1152]{1,0:T(8,128)(2,1)S(1)}, bf16[128,1152]{1,0:T(8,128)(2,1)S(1)}, u32[]{:S(2)}, u32[]{:S(2)}) collective-permute-start(bf16[128,1152]{1,0:T(8,128)(2,1)S(1)} %add_convert_fusion.6), channel_id=1, source_target_pairs={{0,2},{1,3},{2,0},{3,1},{4,6},{5,7},{6,4},{7,5},{8,10},{9,11},{10,... | collective-permute-start | bytes 884744 | tf_op jit(solution)/shard_map/ppermute | solution.py:33
  155.1 24.0 %collective-permute-start.14 = (bf16[128,1152]{1,0:T(8,128)(2,1)S(1)}, bf16[128,1152]{1,0:T(8,128)(2,1)S(1)}, u32[]{:S(2)}, u32[]{:S(2)}) collective-permute-start(bf16[128,1152]{1,0:T(8,128)(2,1)S(1)} %add_convert_fusion.4), channel_id=1, source_target_pairs={{0,2},{1,3},{2,0},{3,1},{4,6},{5,7},{6,4},{7,5},{8,10},{9,11},{10,... | collective-permute-start | bytes 884744 | tf_op jit(solution)/shard_map/ppermute | solution.py:33
  172.2 9.8 %collective-permute-start.12 = (bf16[128,1152]{1,0:T(8,128)(2,1)S(1)}, bf16[128,1152]{1,0:T(8,128)(2,1)}, u32[]{:S(2)}, u32[]{:S(2)}) collective-permute-start(bf16[128,1152]{1,0:T(8,128)(2,1)S(1)} %add_convert_fusion.5), channel_id=1, source_target_pairs={{0,1},{1,0},{2,3},{3,2},{4,5},{5,4},{6,7},{7,6},{8,9},{9,8},{10,11... | collective-permute-start | bytes 884744 | tf_op jit(solution)/shard_map/ppermute | solution.py:33
  179.1 2.9 collective-permute-start.15
  230.7 22.1 %collective-permute-start.16 = (bf16[128,1152]{1,0:T(8,128)(2,1)}, bf16[128,1152]{1,0:T(8,128)(2,1)}, u32[]{:S(2)}, u32[]{:S(2)}) collective-permute-start(bf16[128,1152]{1,0:T(8,128)(2,1)} %dynamic-slice_convert_fusion), channel_id=1, source_target_pairs={{0,1},{1,0},{2,3},{3,2},{4,5},{5,4},{6,7},{7,6},{8,9},{9,8},{10,11... | collective-permute-start | bytes 884744 | tf_op jit(solution)/shard_map/ppermute | solution.py:33
  236.9 34.9 %all-to-all-start.3 = ((bf16[8,364,72]{1,2,0:T(8,128)(2,1)}), bf16[8,364,72]{1,2,0:T(8,128)(2,1)}, u32[]{:S(2)}, u32[]{:S(2)}) async-start(bf16[8,364,72]{1,2,0:T(8,128)(2,1)} %pad_maximum_fusion.1), calls=%async_computation.3 | async-start | bytes 884736 | tf_op jit(solution)/shard_map/all_to_all | solution.py:641
  250.7 17.3 %collective-permute-start.19 = (bf16[4,72,1152]{2,1,0:T(8,128)(2,1)S(1)}, bf16[4,72,1152]{2,1,0:T(8,128)(2,1)S(1)}, u32[]{:S(2)}, u32[]{:S(2)}) collective-permute-start(bf16[4,72,1152]{2,1,0:T(8,128)(2,1)S(1)} %fusion.17), channel_id=1, source_target_pairs={{0,4},{4,0},{8,12},{12,8},{16,20},{20,16},{24,28},{28,24},{1,5},{5... | collective-permute-start | bytes 1990664 | tf_op jit(solution)/shard_map/ppermute | solution.py:33
  253.8 8.3 %collective-permute-start.17 = (bf16[128,1152]{1,0:T(8,128)(2,1)S(1)}, bf16[128,1152]{1,0:T(8,128)(2,1)S(1)}, u32[]{:S(2)}, u32[]{:S(2)}) collective-permute-start(bf16[128,1152]{1,0:T(8,128)(2,1)S(1)} %add_convert_fusion.2), channel_id=1, source_target_pairs={{0,2},{1,3},{2,0},{3,1},{4,6},{5,7},{6,4},{7,5},{8,10},{9,11},{10,... | collective-permute-start | bytes 884744 | tf_op jit(solution)/shard_map/ppermute | solution.py:33
  262.2 16.0 %collective-permute-start.18 = (bf16[128,1152]{1,0:T(8,128)(2,1)S(1)}, bf16[128,1152]{1,0:T(8,128)(2,1)}, u32[]{:S(2)}, u32[]{:S(2)}) collective-permute-start(bf16[128,1152]{1,0:T(8,128)(2,1)S(1)} %add_convert_fusion.1), channel_id=1, source_target_pairs={{0,1},{1,0},{2,3},{3,2},{4,5},{5,4},{6,7},{7,6},{8,9},{9,8},{10,11... | collective-permute-start | bytes 884744 | tf_op jit(solution)/shard_map/ppermute | solution.py:33
  270.0 15.9 %collective-permute-start.20 = (bf16[2,72,1152]{2,1,0:T(8,128)(2,1)}, bf16[2,72,1152]{2,1,0:T(8,128)(2,1)}, u32[]{:S(2)}, u32[]{:S(2)}) collective-permute-start(bf16[2,72,1152]{2,1,0:T(8,128)(2,1)} %fusion.24), channel_id=1, source_target_pairs={{0,8},{4,12},{8,0},{12,4},{16,24},{20,28},{24,16},{28,20},{1,9},{5... | collective-permute-start | bytes 995336 | tf_op jit(solution)/shard_map/ppermute | solution.py:33
  282.0 23.4 %all-to-all-start.2 = ((bf16[8,367,72]{1,2,0:T(8,128)(2,1)}), bf16[8,367,72]{1,2,0:T(8,128)(2,1)S(1)}, u32[]{:S(2)}, u32[]{:S(2)}) async-start(bf16[8,367,72]{1,2,0:T(8,128)(2,1)} %pad_maximum_fusion), calls=%async_computation.2 | async-start | bytes 884736 | tf_op jit(solution)/shard_map/all_to_all | solution.py:659
  287.2 17.4 %collective-permute-start.21 = (bf16[1,72,1152]{2,1,0:T(8,128)(2,1)S(1)}, bf16[1,72,1152]{2,1,0:T(8,128)(2,1)S(1)}, u32[]{:S(2)}, u32[]{:S(2)}) collective-permute-start(bf16[1,72,1152]{2,1,0:T(8,128)(2,1)S(1)} %fusion.31), channel_id=1, source_target_pairs={{0,16},{4,20},{8,24},{12,28},{16,0},{20,4},{24,8},{28,12},{1,17},{... | collective-permute-start | bytes 497672 | tf_op jit(solution)/shard_map/ppermute | solution.py:33
  (72 other events, 519.6 us)
Sparse Core Ops, SparseCore 0:
  33.0 61.3 all-gather.9
  125.6 111.1 all-gather.7

commit v3 on v0

v3 whole, which is shorter than its diff:
```python
import functools

import jax
import jax.numpy as jnp
from jax import lax
from jax.experimental import pallas as pl
from jax.experimental.pallas import tpu as pltpu
from jax.sharding import PartitionSpec as P

SINK_ITERS = 8
GROUP = 8
LANES = 128
ROWS = 8
FAR = 1e30
LOG2E = 1.4426950408889634
epsilon = 1e-05
f32 = jnp.float32
bf16 = jnp.bfloat16


def dot(left, right, left_dim=1, right_dim=0):
    return lax.dot_general(
        left, right, (((left_dim,), (right_dim,)), ((), ())), preferred_element_type=f32
    )


def shape_of(*dims):
    return jax.ShapeDtypeStruct(dims, f32)


def low_of(*dims):
    return jax.ShapeDtypeStruct(dims, bf16)


def call(body, name, out_shape, scratch=(), scalars=0, operands=(), flops=0, limit=56, parts={}, after=0, known=False, **grid):
    if not grid:
        specs = [pl.BlockSpec(memory_space=pltpu.SMEM)] * scalars
        specs += [pl.BlockSpec(memory_space=pltpu.VMEM)] * (len(operands) - scalars)
        grid = {"in_specs": specs}
        if parts:
            specs[scalars:] = [whole(v.shape) for v in operands[scalars:]]
            for at, half in parts.items():
                specs[at] = column_half(operands[at], half)
            if after:
                specs[-after:] = [pl.BlockSpec(memory_space=pl.ANY)] * after
            grid.update(grid=(1,), out_specs=tuple(whole(v.shape) for v in out_shape))
    return pl.pallas_call(
        body,
        out_shape=out_shape,
        scratch_shapes=list(scratch),
        compiler_params=pltpu.CompilerParams(vmem_limit_bytes=limit * 2**20),
        cost_estimate=pl.CostEstimate(flops=flops if known else 0, bytes_accessed=0, transcendentals=0),
        name=name,
        **grid,
    )(*operands)


def whole(shape):
    return pl.BlockSpec(shape, lambda *i: (0,) * len(shape), pipeline_mode=pl.Buffered(1))


def column_half(array, half):
    rows, columns = array.shape
    return pl.BlockSpec(
        (rows, columns // 2), lambda i: (0, half), pipeline_mode=pl.Buffered(1)
    )


def swap(values, axis, bits):
    size = lax.axis_size(axis)
    return lax.ppermute(values, axis, [(i, i ^ bits) for i in range(size)])


def gather_direct(values, axis):
    size = lax.axis_size(axis)
    if size > GROUP:
        return lax.all_gather(values, axis)
    place = lax.axis_index(axis)
    whole = jnp.zeros((size,) + values.shape, values.dtype)
    for r in range(size):
        piece = swap(values, axis, r) if r > 0 else values
        whole = lax.dynamic_update_slice(whole, piece[None], (place ^ r,) + (0,) * values.ndim)
    return whole


def gather_small(values, axis):
    size = lax.axis_size(axis)
    copies = jnp.broadcast_to(values[None], (size,) + values.shape)
    return lax.all_to_all(copies, axis, 0, 0, tiled=True)


def hidden_pieces(piece):
    near = swap(piece, "hidden", 1)
    far = swap(piece, "hidden", 2)
    return piece, near, far, swap(far, "hidden", 1)


def nothing(*refs):
    pass


def after(values, *others):
    anywhere = pl.BlockSpec(memory_space=pl.ANY)
    return pl.pallas_call(
        nothing,
        out_shape=jax.ShapeDtypeStruct(values.shape, values.dtype),
        in_specs=[anywhere] * (1 + len(others)),
        out_specs=anywhere,
        input_output_aliases={0: 0},
        cost_estimate=pl.CostEstimate(flops=0, bytes_accessed=0, transcendentals=0),
        name="after",
    )(values, *others)


def hidden_halves(values):
    half = values.shape[0] // 2
    place = lax.axis_index("hidden") % 2
    kept = lax.dynamic_slice_in_dim(values, place * half, half, 0)
    given = lax.dynamic_slice_in_dim(values, (1 - place) * half, half, 0)
    low = (kept.astype(f32) + swap(given, "hidden", 1).astype(f32)).astype(bf16)
    low = (low.astype(f32) + swap(low, "hidden", 2).astype(f32)).astype(bf16)
    return low, swap(low, "hidden", 1)


def hidden_sum(values):
    low, other = hidden_halves(values)
    place = lax.axis_index("hidden") % 2
    return jnp.where(
        place == 0, jnp.concatenate([low, other]), jnp.concatenate([other, low])
    ).astype(f32)


def softplus(values):
    return jnp.maximum(values, 0.0) + jnp.log1p(jnp.exp(-jnp.abs(values)))


def sigmoid(values):
    return 1.0 / (1.0 + jnp.exp(-values))


def rms_scale(values):
    return lax.rsqrt(jnp.mean(values * values, axis=-1, keepdims=True) + epsilon)


def put(ref, values):
    width = values.shape[1]
    ref[:, :width] = values
    if ref.shape[1] > width:
        ref[:, width:] = jnp.zeros((values.shape[0], ref.shape[1] - width), ref.dtype)


def widen(tile, width):
    return jnp.concatenate([tile] * (width // LANES), axis=1)


def fold(values):
    total = values[:, :LANES]
    for k in range(1, values.shape[1] // LANES):
        total = total + values[:, k * LANES : (k + 1) * LANES]
    return total


def padded(count):
    return -(-count // LANES) * LANES


def same_segment(lengths, positions, delay):
    places = lax.broadcasted_iota(jnp.int32, (positions, 1), 0)
    first = lengths[0, 0]
    ending = first + lengths[0, 1]

    def segment(at):
        return (at >= first).astype(jnp.int32) + (at >= ending).astype(jnp.int32)

    same = (segment(places) == segment(places - delay)) & (places >= delay)
    return same.astype(f32)


def causal_conv(values, shifted, kernel, offset, lengths):
    positions = values.shape[0]
    taps = kernel.shape[0]
    shifted[:ROWS, :] = jnp.zeros((ROWS, values.shape[1]), f32)
    shifted[ROWS : ROWS + positions, :] = values
    result = offset + kernel[taps - 1 : taps] * values
    moved = [values]
    for delay in range(1, taps):
        part = shifted[ROWS - delay : ROWS - delay + positions, :]
        part = part * same_segment(lengths, positions, delay)
        moved.append(part)
        result = result + kernel[taps - 1 - delay : taps - delay] * part
    return result, moved


def column_tile(ref, first, entries, base):
    start = pl.multiple_of(base // LANES * LANES, LANES)
    tile = ref[first : first + entries, pl.ds(start, LANES)]
    return pltpu.roll(tile, lax.rem(LANES - lax.rem(base, LANES), LANES), 1)


def lane(tile, j, width):
    return jnp.broadcast_to(tile[:, j : j + 1], (tile.shape[0], width))


class Sizes:
    def __init__(self, entries, rank, taps, state):
        self.entries, self.rank, self.taps, self.state = entries, rank, taps, state
        self.step = entries
        self.proj = entries + rank
        self.conv = entries + rank + state
        self.rows = self.conv + ROWS
        self.vectors = 2 * ROWS


def mixer_in_body(
    sizes, lengths, places, tokens, cotangent, weight, pack,
    normed, inner, activity, part, small, vectors, share, shifted,
):
    devices, _, own = pack.shape
    for k in range(devices):
        piece = pack[k].astype(f32)
        small[:, k * own : (k + 1) * own] = piece[: sizes.rows]
        for half in range(2):
            at = (2 * k + half) * own
            row = sizes.rows + half * sizes.vectors
            vectors[:, at : at + own] = piece[row : row + sizes.vectors]
    values = tokens[...].astype(f32)
    low = (values * rms_scale(values) * vectors[0:1, :]).astype(bf16)
    normed[...] = low
    half = share.shape[0] // 2
    share[:half, :] = normed[pl.ds(pl.multiple_of(places[1] * half, half), half), :]
    size = half // 2
    for k in range(2):
        at = pl.multiple_of((places[0] ^ (2 * k)) * size, size)
        share[half + k * size : half + (k + 1) * size, :] = cotangent[pl.ds(at, size), :]
    values = dot(low, weight[...], 1, 1)
    inner[...] = values
    kernel = small[sizes.conv : sizes.conv + sizes.taps, :]
    offset = small[sizes.conv + sizes.taps : sizes.conv + sizes.taps + 1, :]
    result, _ = causal_conv(values, shifted, kernel, offset, lengths)
    low = (result * sigmoid(result)).astype(bf16)
    activity[...] = low
    part[...] = dot(low, small[sizes.proj : sizes.conv, :].astype(bf16), 1, 1)


def mixer_in(sizes, lengths, places, tokens, cotangent, weight, pack):
    positions, width = tokens.shape
    channels = weight.shape[0]
    return call(
        functools.partial(mixer_in_body, sizes),
        "mixer_in",
        (
            low_of(positions, width),
            shape_of(positions, channels),
            low_of(positions, channels),
            shape_of(positions, sizes.state),
            shape_of(sizes.rows, channels),
            shape_of(sizes.vectors, width),
            low_of(positions, width),
        ),
        [pltpu.VMEM((positions + 2 * ROWS, channels), f32)],
        2,
        (lengths, places, tokens, cotangent, weight, pack),
        3 * positions * width * channels,
    )


def scan_forward_body(
    sizes, lengths, parts, activity, small, out, states, pre, basis, rank_low,
    far_steps, inputs, rates, sums, wide,
):
    width = far_steps.shape[1]
    positions, channels = activity.shape
    entries, rank = sizes.entries, sizes.rank
    projected = jnp.sum(parts[...], axis=0)
    put(wide, projected)
    basis[...] = wide[...].T
    low = projected[:, :rank].astype(bf16)
    rank_low[...] = low
    values = dot(low, small[sizes.step : sizes.proj, :].astype(bf16))
    pre[...] = values
    at = sizes.conv + sizes.taps + 1
    step = softplus(values + small[at : at + 1, :])
    put(far_steps, jnp.where(same_segment(lengths, positions, 1) > 0, step, FAR))
    put(inputs, step * activity[...].astype(f32))
    put(rates, -LOG2E * jnp.exp(small[:entries, :]))
    rate = rates[...]

    def block(i, memory):
        base = pl.multiple_of(i * ROWS, ROWS)
        step_rows = far_steps[pl.ds(base, ROWS), :]
        input_rows = inputs[pl.ds(base, ROWS), :]
        tile_b = column_tile(basis, rank, entries, base)
        tile_c = column_tile(basis, rank + entries, entries, base)
        rows = []
        for j in range(ROWS):
            factor = jnp.exp2(step_rows[j : j + 1] * rate)
            memory = factor * memory + input_rows[j : j + 1] * lane(tile_b, j, width)
            states[base + j] = memory
            rows.append(jnp.sum(lane(tile_c, j, width) * memory, axis=0, keepdims=True))
        sums[pl.ds(base, ROWS), :] = jnp.concatenate(rows, axis=0)
        return memory

    lax.fori_loop(0, positions // ROWS, block, jnp.zeros(rate.shape, f32))
    out[...] = sums[:, :channels]


def scan_forward(sizes, lengths, parts, activity, small):
    positions, channels = activity.shape
    lanes = padded(channels)
    rows = pltpu.VMEM((positions, lanes), f32)
    state_lanes = padded(sizes.state)
    return call(
        functools.partial(scan_forward_body, sizes),
        "scan_forward",
        (
            shape_of(positions, channels),
            shape_of(positions, sizes.entries, lanes),
            shape_of(positions, channels),
            shape_of(state_lanes, positions),
            low_of(positions, sizes.rank),
        ),
        [rows, rows, pltpu.VMEM((sizes.entries, lanes), f32), rows, pltpu.VMEM((positions, state_lanes), f32)],
        1,
        (lengths, parts, activity, small),
        20 * positions * channels * sizes.entries * 16,
    )


def mixer_out_body(sizes, out, activity, normed, weight_z, weight_out, small, mixed, gate, branch):
    shade = dot(normed[...], weight_z[...], 1, 1)
    gate[...] = shade
    at = sizes.conv + sizes.taps + 2
    values = out[...] + small[at : at + 1, :] * activity[...].astype(f32)
    low = (values * (shade * sigmoid(shade))).astype(bf16)
    mixed[...] = low
    branch[...] = dot(low, weight_out[...]).astype(bf16)


def mixer_out(sizes, out, activity, normed, weights, small):
    positions, channels = activity.shape
    width = normed.shape[1]
    return call(
        functools.partial(mixer_out_body, sizes),
        "mixer_out",
        (low_of(positions, channels), shape_of(positions, channels), low_of(positions, width)),
        operands=(out, activity, normed, weights, weights, small),
        flops=4 * positions * width * channels,
        parts={3: 0, 4: 1},
    )


def slots_of(codes, experts, capacity):
    positions = codes.shape[1]
    member = lax.broadcasted_iota(jnp.int32, (experts, positions), 0).astype(f32) == codes
    member = member.astype(f32)
    shape = (positions, positions)
    prior = lax.broadcasted_iota(jnp.int32, shape, 0) < lax.broadcasted_iota(jnp.int32, shape, 1)
    before = dot(member.astype(bf16), prior.astype(f32).astype(bf16))
    rank = jnp.sum(before * member, axis=0, keepdims=True)
    return jnp.where(codes >= 0, codes * capacity + rank, -1.0)


def picks(slots, first, count):
    shape = (count, slots.shape[1])
    return ((lax.broadcasted_iota(jnp.int32, shape, 0) + first).astype(f32) == slots).astype(f32)


def gelu_pair(values):
    root = 0.7978845608028654
    square = values * values
    bent = jnp.tanh(root * values * (1.0 + 0.044715 * square))
    half = 0.5 * (1.0 + bent)
    slope = half + 0.5 * values * (1.0 - bent * bent) * root * (1.0 + 3 * 0.044715 * square)
    return values * half, slope


def middle_body(
    places, tokens, low, other, vectors, codes, cotangent,
    resid, normed_two, sent, sent_grad, share, logits,
):
    half = low.shape[0]
    experts = logits.shape[0]
    capacity = sent.shape[0] // experts
    resid[pl.ds(pl.multiple_of(places[1] * half, half), half), :] = low[...].astype(f32)
    resid[pl.ds(pl.multiple_of((1 - places[1]) * half, half), half), :] = other[...].astype(f32)
    values = tokens[...].astype(f32) + resid[...]
    resid[...] = values
    rows = (values * rms_scale(values) * vectors[1:2, :]).astype(bf16)
    normed_two[...] = rows
    logits[...] = dot(vectors[2 : 2 + experts, :].astype(bf16), rows, 1, 1)
    every = picks(slots_of(codes[...], experts, capacity), 0, sent.shape[0]).astype(bf16)
    sent[...] = dot(every, rows).astype(bf16)
    sent_grad[...] = dot(every, cotangent[...]).astype(bf16)
    size = share.shape[0] // 2
    for k in range(2):
        at = pl.multiple_of((places[0] ^ (2 * k)) * size, size)
        share[k * size : (k + 1) * size, :] = normed_two[pl.ds(at, size), :]


def middle(places, tokens, low, other, vectors, codes, cotangent, experts):
    positions, width = tokens.shape
    slots = 3 * positions // 2
    return call(
        middle_body,
        "middle",
        (
            shape_of(positions, width),
            low_of(positions, width),
            low_of(slots, width),
            low_of(slots, width),
            low_of(positions // 2, width),
            shape_of(experts, positions),
        ),
        (),
        1,
        (places, tokens, low, other, vectors, codes, cotangent),
        4 * positions * width * slots,
    )


def experts_body(
    codes, logits, rows, grads, up, down, out, back, packed, slots, outs, backs
):
    step = pl.program_id(0)
    experts = pl.num_programs(0)
    capacity = rows.shape[0]
    count = logits.shape[0]

    @pl.when(step == 0)
    def _():
        slots[...] = slots_of(codes[...], experts, capacity)
        packed[:count, :] = logits[...]
        packed[count:, :] = jnp.zeros((packed.shape[0] - count, packed.shape[1]), f32)
        packed[count : count + 1, :] = codes[...]

    first = pl.multiple_of(step * capacity, capacity)
    active, slope = gelu_pair(dot(rows[...], up[0]))
    plain = dot(grads[...], down[0], 1, 1)
    low = active.astype(bf16)
    gate_slots = jnp.sum(low.astype(f32) * plain, axis=1, keepdims=True)
    chosen = picks(slots[...], first, capacity)
    packed[count + 1 : count + 2, :] += jnp.sum(chosen * gate_slots, axis=0, keepdims=True)
    outs[pl.ds(first, capacity), :] = dot(low, down[0]).astype(bf16)
    backs[pl.ds(first, capacity), :] = dot((plain * slope).astype(bf16), up[0], 1, 1).astype(bf16)

    @pl.when(step == experts - 1)
    def _():
        every = picks(slots[...], 0, outs.shape[0]).astype(bf16)
        out[...] = dot(every, outs[...], 0, 0).astype(bf16)
        back[...] = dot(every, backs[...], 0, 0).astype(bf16)


def experts_local(codes, logits, rows, grads, up, down):
    slots, width = rows.shape
    experts, _, hidden = up.shape
    positions = codes.shape[1]
    capacity = slots // experts
    return call(
        experts_body,
        "experts_local",
        (
            low_of(positions, width),
            low_of(positions, width),
            shape_of(2 * ROWS, positions),
        ),
        [
            pltpu.VMEM((1, positions), f32),
            pltpu.VMEM((slots, width), bf16),
            pltpu.VMEM((slots, width), bf16),
        ],
        operands=(codes, logits, rows, grads, up, down),
        flops=8 * slots * width * hidden,
        limit=40,
        grid=(experts,),
        in_specs=[
            whole((1, positions)),
            whole((experts, positions)),
            pl.BlockSpec((capacity, width), lambda i: (i, 0)),
            pl.BlockSpec((capacity, width), lambda i: (i, 0)),
            pl.BlockSpec((1, width, hidden), lambda i: (i, 0, 0)),
            pl.BlockSpec((1, hidden, width), lambda i: (i, 0, 0)),
        ],
        out_specs=(
            whole((positions, width)),
            whole((positions, width)),
            whole((2 * ROWS, positions)),
        ),
    )


def expert_grads_body(
    places, codes, gates, *refs,
):
    rows, grads = refs[:2], refs[2:4]
    up, down, up_grad, down_grad, sent, sent_grad, gate_slots = refs[4:]
    step = pl.program_id(0)
    experts, total, width = sent.shape
    count, _, positions = codes.shape
    capacity = total // count
    block = up_grad.shape[1]
    window = min(padded(block + LANES), width)

    @pl.when(step == 0)
    def _():
        for r in range(count):
            chosen = picks(slots_of(codes[r], experts, capacity), 0, experts * capacity)
            pick = chosen.astype(bf16)
            gate = jnp.sum(chosen * gates[r], axis=1, keepdims=True)
            part = pl.ds(r * capacity, capacity)
            for pieces, target in ((rows, sent), (grads, sent_grad)):
                whole_rows = jnp.concatenate([piece[r] for piece in pieces], axis=0)
                moved = dot(pick, whole_rows).astype(bf16)
                for i in range(experts):
                    target[i, part, :] = moved[i * capacity : (i + 1) * capacity]
            for i in range(experts):
                gate_slots[i, part, :] = jnp.broadcast_to(
                    gate[i * capacity : (i + 1) * capacity], (capacity, LANES)
                )

    gate = gate_slots[step][:, :1]
    active, slope = gelu_pair(dot(sent[step], up[0]))
    plain = dot(sent_grad[step], down[0], 1, 1)
    grad_pre = (plain * slope * gate).astype(bf16)
    scaled = (active * gate).astype(bf16)
    start = jnp.minimum(places[2] * block // LANES * LANES, width - window)
    shift = lax.rem(window - (places[2] * block - start), window)
    own = pl.ds(pl.multiple_of(start, LANES), window)
    up_grad[0] = pltpu.roll(dot(sent[step, :, own], grad_pre, 0, 0), shift, 0)[:block]
    down_grad[0] = pltpu.roll(dot(sent_grad[step, :, own], scaled, 0, 0), shift, 0)[:block]


def expert_grads(places, codes, gates, rows, grads, up, down, block):
    count, _, positions = codes.shape
    experts, width, hidden = up.shape
    slots = count * (3 * positions // (2 * experts))
    shape = (experts, block, hidden)
    out = pl.BlockSpec((1, block, hidden), lambda i: (i, 0, 0))
    half = whole((count, positions // 2, width))
    second = pl.BlockSpec(
        (count, positions // 2, width), lambda i: (0, 1, 0), pipeline_mode=pl.Buffered(1)
    )
    return call(
        expert_grads_body,
        "expert_grads",
        (shape_of(*shape), shape_of(*shape)),
        [
            pltpu.VMEM((experts, slots, width), bf16),
            pltpu.VMEM((experts, slots, width), bf16),
            pltpu.VMEM((experts, slots, LANES), f32),
        ],
        operands=(places, codes, gates, *rows, *grads, up, down),
        flops=12 * experts * slots * width * hidden,
        known=True,
        limit=54,
        grid=(experts,),
        in_specs=[
            pl.BlockSpec(memory_space=pltpu.SMEM),
            whole((count, 1, positions)),
            whole((count, 1, positions)),
            *([half] * 2),
            *([second] * 2),
            pl.BlockSpec((1, width, hidden), lambda i: (i, 0, 0)),
            pl.BlockSpec((1, hidden, width), lambda i: (i, 0, 0)),
        ],
        out_specs=(out, out),
    )


def sinkhorn(packed, experts):
    start = jnp.exp(packed[:, 0, :experts, :])
    codes = packed[:, 0, experts : experts + 1, :]
    grad_gates = jnp.sum(packed[:, :, experts + 1 : experts + 2, :], axis=1)
    valid = (codes >= 0).astype(f32)
    onehot = (lax.broadcasted_iota(jnp.int32, start.shape, 1).astype(f32) == codes).astype(f32)
    weights = start
    history = []
    for _ in range(SINK_ITERS):
        columns = jnp.sum(jnp.sum(weights * valid, axis=2, keepdims=True), axis=0, keepdims=True)
        scaled = weights / columns
        row_sums = jnp.sum(scaled, axis=1, keepdims=True)
        weights = scaled / row_sums
        history.append((columns, scaled, row_sums, weights))
    gates = experts * jnp.sum(weights * onehot, axis=1, keepdims=True)
    grads = experts * grad_gates * onehot
    for columns, scaled, row_sums, result in reversed(history):
        grads = (grads - jnp.sum(grads * result, axis=1, keepdims=True)) / row_sums
        term = jnp.sum(jnp.sum(grads * scaled, axis=2, keepdims=True), axis=0, keepdims=True)
        grads = (grads - valid * term) / columns
    return gates, grads * start


def backward_body(
    sizes, lengths, places, packed, low, other, vectors, resid, normed_two, cotangent, mixed,
    weight_out, out, activity, gate, pre, small, basis, states, rank_low,
    gates, grad_resid, out_grad, grad_act, grad_gate, grad_part, early,
    all_gates, all_grads, branch_grad, far_steps, steps, inputs, outer, rates, sum_input,
    sum_step, sums, shares, square,
):
    positions, width = resid.shape
    channels = activity.shape[1]
    lanes = far_steps.shape[1]
    entries, rank = sizes.entries, sizes.rank
    devices, own, _ = early.shape
    experts = all_grads.shape[1]
    half = low.shape[0]

    every_gate, every_grad = sinkhorn(packed, experts)
    gates[...] = every_gate
    all_gates[...] = every_gate
    all_grads[...] = every_grad
    grad_logits = all_grads[places[2]].astype(bf16)
    square[...] = jnp.broadcast_to(all_gates[places[2]], square.shape)
    gate_column = square[...].T[:, :1]

    branch_grad[pl.ds(pl.multiple_of(places[1] * half, half), half), :] = low[...].astype(f32)
    branch_grad[pl.ds(pl.multiple_of((1 - places[1]) * half, half), half), :] = other[...].astype(f32)
    at = lax.broadcasted_iota(jnp.int32, (positions, 1), 0)
    valid = (at < lengths[0, 0] + lengths[0, 1]).astype(f32)
    grad_two = dot(grad_logits, vectors[2 : 2 + experts, :].astype(bf16), 0, 0)
    grad_two = grad_two + branch_grad[...] * (gate_column * valid)
    values = resid[...]
    scale = rms_scale(values)
    unit = values * scale
    shares[...] = jnp.zeros_like(shares)
    shares[0:1, :] = jnp.sum(grad_two * unit, axis=0, keepdims=True)
    shares[ROWS : ROWS + experts, :] = dot(grad_logits, normed_two[...])
    scaled = grad_two * vectors[1:2, :]
    total = cotangent[...].astype(f32) * valid + scale * (
        scaled - unit * jnp.mean(scaled * unit, axis=-1, keepdims=True)
    )
    grad_resid[...] = total
    branch = total.astype(bf16)
    out_grad[...] = dot(mixed[...], branch, 0, 0).astype(bf16)
    grad = dot(branch, weight_out[...], 1, 1)

    row = sizes.conv + sizes.taps + 1
    shifted = pre[...] + small[row : row + 1, :]
    skip = small[row + 1 : row + 2, :]
    step = softplus(shifted)
    act = activity[...].astype(f32)
    put(far_steps, jnp.where(same_segment(lengths, positions, 1) > 0, step, FAR))
    put(steps, step)
    put(inputs, step * act)
    put(rates, -jnp.exp(small[:entries, :]))
    level = gate[...]
    shade = sigmoid(level)
    through = grad * level * shade
    put(outer, through)
    grad_level = grad * (out[...] + skip * act) * (shade * (1.0 + level * (1.0 - shade)))
    grad_gate[...] = grad_level.astype(bf16)
    put(sum_input, grad_level)
    turned = sum_input[...].T
    for k in range(devices):
        early[k, :, :positions] = turned[k * own : (k + 1) * own].astype(bf16)
    sums[...] = jnp.zeros_like(sums)
    skip_row = entries + rank + 1
    sums[skip_row : skip_row + 1, :channels] = jnp.sum(through * act, axis=0, keepdims=True)
    rate = rates[...]
    quick = rate * LOG2E
    blocks = positions // ROWS
    grad_part[...] = jnp.zeros_like(grad_part)
    lane_ids = lax.broadcasted_iota(jnp.int32, (entries, LANES), 1)

    def block(i, carried):
        later, rate_sum = carried
        base = pl.multiple_of((blocks - 1 - i) * ROWS, ROWS)
        far_rows = far_steps[pl.ds(base, ROWS), :]
        step_rows = steps[pl.ds(base, ROWS), :]
        input_rows = inputs[pl.ds(base, ROWS), :]
        outer_rows = outer[pl.ds(base, ROWS), :]
        columns_b = column_tile(basis, rank, entries, base)
        columns_c = column_tile(basis, rank + entries, entries, base)
        input_sums = [None] * ROWS
        step_sums = [None] * ROWS
        found_b = jnp.zeros((entries, LANES), f32)
        found_c = jnp.zeros((entries, LANES), f32)
        for j in reversed(range(ROWS)):
            tile_b = lane(columns_b, j, lanes)
            outside = outer_rows[j : j + 1]
            inside = input_rows[j : j + 1]
            state = states[base + j]
            flow = lane(columns_c, j, lanes) * outside + later
            later = jnp.exp2(far_rows[j : j + 1] * quick) * flow
            in_b = jnp.sum(fold(flow * inside), axis=1, keepdims=True)
            in_c = jnp.sum(fold(outside * state), axis=1, keepdims=True)
            found_b = jnp.where(lane_ids == j, in_b, found_b)
            found_c = jnp.where(lane_ids == j, in_c, found_c)
            input_sums[j] = jnp.sum(flow * tile_b, axis=0, keepdims=True)
            change = flow * (state - inside * tile_b)
            step_sums[j] = jnp.sum(change * rate, axis=0, keepdims=True)
            rate_sum = rate_sum + change * step_rows[j : j + 1]
        sum_input[pl.ds(base, ROWS), :] = jnp.concatenate(input_sums, axis=0)
        sum_step[pl.ds(base, ROWS), :] = jnp.concatenate(step_sums, axis=0)
        start = pl.multiple_of(base // LANES * LANES, LANES)
        shift = lax.rem(base, LANES)
        for first, found in ((0, found_b), (entries, found_c)):
            basis_grad = square.at[first : first + entries, pl.ds(start, LANES)]
            basis_grad[...] += pltpu.roll(found, shift, 1)
        return later, rate_sum

    square[...] = jnp.zeros_like(square)
    zero = jnp.zeros(rate.shape, f32)
    _, rate_sum = lax.fori_loop(0, blocks, block, (zero, zero))
    sums[:entries, :] = rate_sum * rate
    back_input = sum_input[:, :channels]
    grad_act[...] = outer[:, :channels] * skip + back_input * step
    grad_step = (back_input * act + sum_step[:, :channels]) * sigmoid(shifted)
    grad_low = grad_step.astype(bf16)
    sums[entries + rank : entries + rank + 1, :channels] = jnp.sum(grad_step, axis=0, keepdims=True)
    sums[entries : entries + rank, :channels] = dot(rank_low[...], grad_low, 0, 0)
    grad_part[:, :rank] = dot(grad_low, small[sizes.step : sizes.proj, :].astype(bf16), 1, 1)
    grad_part[:, rank : rank + 2 * entries] = square[...].T[:, : 2 * entries]
    turned = sums[...].T
    spread = shares[...].T
    side = padded(sizes.vectors) - 2 * sizes.vectors
    for k in range(devices):
        early[k, :, positions : positions + side] = turned[k * own : (k + 1) * own, :side].astype(bf16)
        for piece in range(2):
            to = positions + side + piece * sizes.vectors
            source = (2 * k + piece) * own
            early[k, :, to : to + sizes.vectors] = spread[source : source + own].astype(bf16)


def backward(sizes, operands, experts, devices):
    (_, _, packed, _, _, _, resid, _, _, mixed, _, _, activity) = operands[:13]
    positions, width = resid.shape
    channels = activity.shape[1]
    lanes = padded(channels)
    rows = pltpu.VMEM((positions, lanes), f32)
    return call(
        functools.partial(backward_body, sizes),
        "backward",
        (
            shape_of(devices, 1, positions),
            shape_of(positions, width),
            low_of(channels, width),
            shape_of(positions, channels),
            low_of(positions, channels),
            shape_of(positions, padded(sizes.state)),
            low_of(devices, channels // devices, positions + LANES),
        ),
        [
            pltpu.VMEM((devices, 1, positions), f32),
            pltpu.VMEM((devices, experts, positions), f32),
            pltpu.VMEM((positions, width), f32),
            rows,
            rows,
            rows,
            rows,
            pltpu.VMEM((sizes.entries, lanes), f32),
            rows,
            rows,
            pltpu.VMEM((LANES, lanes), f32),
            pltpu.VMEM((sizes.vectors, width), f32),
            pltpu.VMEM((LANES, positions), f32),
        ],
        2,
        operands,
        40 * positions * width * channels,
        parts={10: 1},
    )


def mixer_back_body(
    sizes, lengths, parts, grad_act, activity, inner, small, weight_x, weight_z, grad_z, tokens,
    early, expert_out, out_grad, _near, both, late, shifted, wide, sums, shares,
):
    positions, channels = activity.shape
    devices, own, lanes = early.shape
    late[:, :, lanes : 2 * lanes] = early[...]
    late[:, :, 2 * lanes :] = out_grad[...]
    both[:positions, :] = expert_out[...]
    taps = sizes.taps
    low = jnp.sum(parts[...], axis=0)[:, : sizes.state].astype(bf16)
    state_grad = dot(activity[...], low, 0, 0)
    grad = grad_act[...] + dot(low, small[sizes.proj : sizes.conv, :].astype(bf16))
    kernel = small[sizes.conv : sizes.conv + taps, :]
    offset = small[sizes.conv + taps : sizes.conv + taps + 1, :]
    result, moved = causal_conv(inner[...], shifted, kernel, offset, lengths)
    shade = sigmoid(result)
    grad = grad * (shade * (1.0 + result * (1.0 - shade)))
    sums[...] = jnp.zeros_like(sums)
    sums[taps : taps + 1, :channels] = jnp.sum(grad, axis=0, keepdims=True)
    total = kernel[taps - 1 : taps] * grad
    shifted[positions : positions + ROWS, :] = jnp.zeros((ROWS, channels), f32)
    for delay in range(taps):
        row = taps - 1 - delay
        sums[row : row + 1, :channels] = jnp.sum(grad * moved[delay], axis=0, keepdims=True)
        if delay > 0:
            shifted[:positions, :] = grad * same_segment(lengths, positions, delay)
            total = total + kernel[row : row + 1] * shifted[delay : delay + positions, :]
    grad_x = total.astype(bf16)
    put(wide, total)
    turned = wide[...].T
    part = dot(grad_x, weight_x[...]) + dot(grad_z[...], weight_z[...])
    both[positions:, :] = part.astype(bf16)
    values = tokens[...].astype(f32)
    shares[...] = jnp.broadcast_to(
        jnp.sum(part * (values * rms_scale(values)), axis=0, keepdims=True), shares.shape
    )
    spread = shares[...].T
    turned_sums = sums[...].T
    at = positions + sizes.state
    for k in range(devices):
        rows = slice(k * own, (k + 1) * own)
        late[k, :, :positions] = turned[rows].astype(bf16)
        late[k, :, positions:at] = state_grad[rows].astype(bf16)
        late[k, :, at : at + ROWS] = turned_sums[rows].astype(bf16)
        for piece in range(2):
            to = at + (1 + piece) * ROWS
            source = (2 * k + piece) * own
            late[k, :, to : to + ROWS] = spread[source : source + own].astype(bf16)


def mixer_back(sizes, operands):
    activity, tokens, early = operands[3], operands[9], operands[10]
    positions, width = tokens.shape
    channels = activity.shape[1]
    return call(
        functools.partial(mixer_back_body, sizes),
        "mixer_back",
        (low_of(2 * positions, width), low_of(*early.shape[:2], 2 * early.shape[2] + width)),
        [
            pltpu.VMEM((positions + 2 * ROWS, channels), f32),
            pltpu.VMEM((positions, padded(channels)), f32),
            pltpu.VMEM((ROWS, padded(channels)), f32),
            pltpu.VMEM((ROWS, width), f32),
        ],
        1,
        operands,
        6 * positions * width * channels,
        parts={7: 0},
        after=1,
    )


def proj_grads_body(
    sizes, places, both, *refs,
):
    half, other, _ = refs[:3]
    grad_x, grad_z, state, conv, bias, gain_one, decay, proj, step_bias, skip, gain_two = refs[3:14]
    router, out, late_sum, early_sum = refs[14:]
    step = pl.program_id(0)
    count, own, lanes = both.shape
    width = half.shape[2]
    lanes = lanes - width
    size = half.shape[1]
    positions = 2 * size
    total_x = total_z = None
    add_late = add_early = add_out = None
    for r in range(count):
        part_x = part_z = 0.0
        for place, rows in ((places[1], half), (1 - places[1], other)):
            at = pl.multiple_of(place * size, size)
            part_x += dot(both[r, :, pl.ds(at, size)], rows[r])
            part_z += dot(both[r, :, pl.ds(at + lanes // 2, size)], rows[r])
        more_late = both[r, :, positions : lanes // 2].astype(f32)
        more_early = both[r, :, lanes // 2 + positions : lanes].astype(f32)
        more_out = both[r, :, lanes:].astype(f32)
        if r == 0:
            total_x, total_z, add_late, add_early = part_x, part_z, more_late, more_early
            add_out = more_out
        else:
            total_x, total_z = total_x + part_x, total_z + part_z
            add_late, add_early = add_late + more_late, add_early + more_early
            add_out = add_out + more_out

    @pl.when(step == 0)
    def _():
        grad_x[...] = total_x
        grad_z[...] = total_z
        out[...] = add_out
        late_sum[...] = jnp.zeros_like(late_sum)
        early_sum[...] = jnp.zeros_like(early_sum)
        late_sum[:own, :] = add_late
        early_sum[:own, :] = add_early

    @pl.when(step > 0)
    def _():
        grad_x[...] += total_x
        grad_z[...] += total_z
        out[...] += add_out
        late_sum[:own, :] += add_late
        early_sum[:own, :] += add_early

    @pl.when(step == pl.num_programs(0) - 1)
    def _():
        state[...] = late_sum[:own, : sizes.state]
        turned = late_sum[...].T[sizes.state :, :own]
        conv[...] = turned[: sizes.taps]
        bias[...] = turned[sizes.taps : sizes.taps + 1]
        gain_one[:, :own] = turned[ROWS : ROWS + 1]
        gain_one[:, own:] = turned[2 * ROWS : 2 * ROWS + 1]
        turned = early_sum[...].T[:, :own]
        at = sizes.entries + sizes.rank
        decay[...] = turned[: sizes.entries]
        proj[...] = turned[sizes.entries : at]
        step_bias[...] = turned[at : at + 1]
        skip[...] = turned[at + 1 : at + 2]
        for half_at, columns in ((0, slice(0, own)), (sizes.vectors, slice(own, 2 * own))):
            row = LANES - 2 * sizes.vectors + half_at
            gain_two[:, columns] = turned[row : row + 1]
            router[:, columns] = turned[row + ROWS : row + ROWS + router.shape[0]]


def proj_grads(sizes, experts, places, both, half, other, after):
    devices, own, lanes = both.shape
    width = half.shape[2]
    size = half.shape[1] // 2
    group = min(devices, GROUP)
    shapes = (
        (own, width),
        (own, width),
        (own, sizes.state),
        (sizes.taps, own),
        (1, own),
        (1, 2 * own),
        (sizes.entries, own),
        (sizes.rank, own),
        (1, own),
        (1, own),
        (1, 2 * own),
        (experts, 2 * own),
        (own, width),
    )
    few = pl.BlockSpec((group, own, lanes), lambda i: (i, 0, 0))
    return call(
        functools.partial(proj_grads_body, sizes),
        "proj_grads",
        tuple(shape_of(*shape) for shape in shapes),
        [
            pltpu.VMEM((padded(own), LANES), f32),
            pltpu.VMEM((padded(own), LANES), f32),
        ],
        operands=(places, both, half, other, after),
        flops=8 * devices * size * width * own,
        limit=40,
        grid=(devices // group,),
        in_specs=[
            pl.BlockSpec(memory_space=pltpu.SMEM),
            few,
            pl.BlockSpec((group, size, width), lambda i: (i, 0, 0)),
            pl.BlockSpec((group, size, width), lambda i: (i, 0, 0)),
            pl.BlockSpec(memory_space=pl.ANY),
        ],
        out_specs=tuple(whole(shape) for shape in shapes),
    )


def local(
    tokens,
    cotangent,
    seq_lengths,
    routes,
    mixer_gain,
    proj_x,
    proj_z,
    conv_weight,
    conv_bias,
    state_proj,
    step_proj,
    step_bias,
    decay_log,
    skip_gain,
    out_proj,
    moe_gain,
    router,
    expert_up,
    expert_down,
):
    devices = lax.axis_size("expert")
    hidden = lax.axis_size("hidden")
    index = lax.axis_index("expert")
    place = lax.axis_index("hidden")
    positions, width = tokens.shape
    block = mixer_gain.shape[0]
    experts = expert_up.shape[0]
    own = proj_x.shape[1]
    channels = devices * own
    taps = conv_weight.shape[0]
    sizes = Sizes(decay_log.shape[0], step_proj.shape[0], taps, state_proj.shape[1])
    places = jnp.stack([place, place % 2, index])

    valid = jnp.arange(positions, dtype=jnp.int32) < seq_lengths[0, 0] + seq_lengths[0, 1]
    codes = jnp.where(valid, routes[:, 0].astype(f32), -1.0)[None]

    later = jnp.concatenate([proj_z.T, out_proj], axis=1)
    later, turned_x = lax.optimization_barrier((later, proj_x.T))
    weights = lax.all_gather(later, "expert").reshape(channels, 2 * width)
    weight_x = gather_direct(turned_x, "expert").reshape(channels, width)
    vectors = jnp.concatenate([mixer_gain[None], moe_gain[None], router.T])
    vectors = jnp.pad(vectors, ((0, sizes.vectors - vectors.shape[0]), (0, 0)))
    few = jnp.concatenate([conv_weight, conv_bias[None], step_bias[None], skip_gain[None]])
    pack = [
        decay_log,
        step_proj,
        state_proj.T,
        jnp.pad(few, ((0, ROWS - few.shape[0]), (0, 0))),
        vectors[:, :own],
        vectors[:, own:],
    ]
    pack = gather_small(jnp.concatenate(pack), "expert")

    normed, inner_x, activity, part, small, vectors, share = mixer_in(
        sizes, seq_lengths, places, tokens, cotangent, weight_x, pack
    )
    parts = lax.all_gather(part, "hidden")
    scanned, states, step_pre, basis, rank_low = scan_forward(
        sizes, seq_lengths, parts, activity, small
    )
    quarter = positions // hidden
    share = lax.all_gather(share, "expert")
    mixed, gate_z, branch = mixer_out(sizes, scanned, activity, normed, weights, small)
    low, other = hidden_halves(branch)
    resid, normed_two, sent, sent_grad, own_half, logits = middle(
        places, tokens, low, other, vectors, codes, cotangent, experts
    )
    own_half = lax.all_gather(own_half, "expert")
    out_part, back_part, packed = experts_local(
        codes, logits, sent, sent_grad, expert_up, expert_down
    )
    packed = gather_small(packed, ("expert", "hidden"))
    packed = packed.reshape((devices, hidden) + packed.shape[1:])
    low, other = hidden_halves(back_part)
    share = after(share, packed, other)
    near = swap(share, "hidden", 1)
    operands = (
        seq_lengths, places, packed, low, other, vectors, resid, normed_two, cotangent, mixed,
        weights, scanned, activity, gate_z, step_pre, small, basis, states, rank_low,
    )
    gates, grad_resid, out_grad, grad_act, grad_z, grad_part, early = backward(
        sizes, operands, experts, devices
    )
    parts = lax.all_gather(grad_part, "hidden")
    both, late = mixer_back(
        sizes,
        (
            seq_lengths, parts, grad_act, activity, inner_x, small, weight_x, weights, grad_z,
            tokens, early, out_part, out_grad.reshape(devices, own, width), near,
        ),
    )
    late = lax.all_to_all(late, "expert", 0, 0, tiled=True)
    low, other = hidden_halves(both)
    first = place % 2 == 0
    returned = jnp.where(first, low, other).astype(f32)
    grad_normed = jnp.where(first, other, low).astype(f32)
    values = tokens.astype(f32)
    scale = rms_scale(values)
    unit = values * scale
    scaled = grad_normed * vectors[0:1]
    tokens_grad = grad_resid + scale * (
        scaled - unit * jnp.mean(scaled * unit, axis=-1, keepdims=True)
    )
    gate_values = lax.dynamic_index_in_dim(gates, index, 0, keepdims=False)[0]
    layer_out = valid.astype(f32)[:, None] * (resid + gate_values[:, None] * returned)

    all_codes = packed[:, 0, experts : experts + 1]
    halves = (own_half, swap(own_half, "hidden", 1))

    def by_piece(values):
        values = values.reshape(devices, 2, 2, quarter)
        values = jnp.where(place >= 2, values[:, ::-1], values)
        values = jnp.where(place % 2 == 1, values[:, :, ::-1], values)
        return values.transpose(0, 2, 1, 3).reshape(devices, 1, positions)

    group = min(devices, GROUP)
    pieces = (by_piece(all_codes), by_piece(gates), halves, (share, near))
    if group == devices:
        up_grad, down_grad = expert_grads(places, *pieces, expert_up, expert_down, block)
    else:

        def add(total, some):
            part = expert_grads(places, *some, expert_up, expert_down, block)
            return (total[0] + part[0], total[1] + part[1]), None

        grouped = jax.tree.map(lambda v: v.reshape((-1, group) + v.shape[1:]), pieces)
        zero = jnp.zeros((experts, block, expert_up.shape[2]), f32)
        (up_grad, down_grad), _ = lax.scan(add, (zero, zero), grouped)
    projected = proj_grads(sizes, experts, places, late, share, near, up_grad)
    grad_x, grad_zw, state_grad, conv_grad, conv_bias_grad, gain_one_grad = projected[:6]
    decay_grad, step_proj_grad, step_bias_grad, skip_grad, gain_two_grad = projected[6:11]
    router_grad, out_grad = projected[11:]
    gain_one_grad = jnp.sum(lax.all_gather(gain_one_grad, "hidden"), axis=0)
    return (
        layer_out.astype(bf16),
        tokens_grad,
        gain_one_grad.reshape(-1),
        grad_x.T,
        grad_zw.T,
        conv_grad,
        conv_bias_grad.reshape(-1),
        state_grad,
        step_proj_grad,
        step_bias_grad.reshape(-1),
        decay_grad,
        skip_grad.reshape(-1),
        out_grad,
        gain_two_grad.reshape(-1),
        router_grad.T,
        up_grad,
        down_grad.transpose(0, 2, 1),
    )


def solution(mesh):
    in_specs = (
        P("expert", None),
        P("expert", None),
        P("expert", None),
        P("expert", None),
        P("expert"),
        P(None, ("expert", "hidden")),
        P(None, ("expert", "hidden")),
        P(None, ("expert", "hidden")),
        P(("expert", "hidden")),
        P(("expert", "hidden"), None),
        P(None, ("expert", "hidden")),
        P(("expert", "hidden")),
        P(None, ("expert", "hidden")),
        P(("expert", "hidden")),
        P(("expert", "hidden"), None),
        P("expert"),
        P("expert", None),
        P(None, None, "hidden"),
        P(None, "hidden", None),
    )
    out_specs = (
        P("expert", None),
        P("expert", None),
        P("expert"),
        P(None, ("expert", "hidden")),
        P(None, ("expert", "hidden")),
        P(None, ("expert", "hidden")),
        P(("expert", "hidden")),
        P(("expert", "hidden"), None),
        P(None, ("expert", "hidden")),
        P(("expert", "hidden")),
        P(None, ("expert", "hidden")),
        P(("expert", "hidden")),
        P(("expert", "hidden"), None),
        P("expert"),
        P("expert", None),
        P(None, "expert", "hidden"),
        P(None, "hidden", "expert"),
    )
    return jax.shard_map(local, mesh=mesh, in_specs=in_specs, out_specs=out_specs, check_vma=False)
```

time: 3480 us -> 314 us (0.09); the launches traced: 3420 us -> 312 us
  waiting for transfers between devices: 1240 us -> 84.7 us
  local copies, waits for them, and re-layouts: 752 us -> 22.2 us
  blocking collectives: 677 us -> 22.6 us
  other arithmetic: 652 us -> 10 us
  Pallas kernels: 0 us -> 119 us
  matrix products: 50.6 us -> 0 us
    reduce_scatter x2 -> x0, waiting for transfers between devices: 905 us -> none  [the longest x1 453 us: local(): lax.psum_scatter(up_placed, 'expert', scatter_dimension=1, tiled=True)]
    pad x544 -> x1, local copies, waits for them, and re-layouts: 432 us -> 0.01 us  [local(): jnp.pad(few, ((0, ROWS - few.shape[0]), (0, 0)))]
    psum x19 -> x0, blocking collectives: 423 us -> none  [the longest x8 181 us: local(): column_term = lax.psum(jnp.sum(grad_scaled * scaled, axis=0), 'expert')]
    unnamed x20 -> x3, waiting for transfers between devices: 268 us -> 0.05 us
    mul x264 -> x0, other arithmetic: 249 us -> none  [the longest x208 190 us: combine_pair(): return (earlier[0] * later[0], later[0] * earlier[1] + later[1])]
    dynamic_update_slice x192 -> x8, local copies, waits for them, and re-layouts: 140 us -> 0.18 us  [gather_direct(): lax.dynamic_update_slice(whole, piece[None], (place ^ r,) + (0,) * values...]
    dynamic_update_slice x112 -> x0, other arithmetic: 131 us -> none  [mixer_core(): lax.scan(advance, initial, (shaped(step_size), shaped(activity), shaped(i...]
    all_gather x5 -> x3, blocking collectives: 151 us -> 22.6 us  [the longest x1 9.3 us: local(): parts = lax.all_gather(grad_part, 'hidden')]
  transfers between devices with their start and end apart: 17 -> 24, of which waited for: 9 -> 14; matrix products, arithmetic and copies ran while one was open for 41% -> 6% of each run, Pallas kernels for 0% -> 37%
where the time goes in v3:
time: 314 us; the launch traced here: 312 us
  Pallas kernels  119 us (38%)
  waiting for transfers between devices  84.7 us (27%)
  starting transfers between devices  38.4 us (12%)
  blocking collectives  22.6 us (7%)
  local copies, waits for them, and re-layouts  22.2 us (7%)
  between operations  15.6 us (5%)
  other arithmetic  10 us (3%)
    pallas_call x9, Pallas kernels, call(): pl.pallas_call(body, out_shape=out_shape, scratch_shapes=list(scratch), c...  119 us
    ppermute x18, waiting for transfers between devices, swap(): return lax.ppermute(values, axis, [(i, i ^ bits) for i in range(size)])  37.7 us
    all_to_all x2, waiting for transfers between devices, gather_small(): return lax.all_to_all(copies, axis, 0, 0, tiled=True)  27 us
    ppermute x18, starting transfers between devices, swap(): return lax.ppermute(values, axis, [(i, i ^ bits) for i in range(size)])  21 us
    all_to_all x2, starting transfers between devices, gather_small(): return lax.all_to_all(copies, axis, 0, 0, tiled=True)  13.3 us
    unnamed x49, local copies, waits for them, and re-layouts  11.5 us
    all_gather x1, blocking collectives, local(): parts = lax.all_gather(grad_part, 'hidden')  9.3 us
    all_gather x1, blocking collectives, local(): parts = lax.all_gather(part, 'hidden')  8.23 us
  transfers between devices with their start and end apart: 24, of which 14 were waited for; matrix products, arithmetic and copies ran while one was open for 6% of the time, Pallas kernels for 37%

profile of v3, /device:TPU:0, one launch (start us, length us, event | category | flops | bytes accessed | tf_op | source)
XLA Modules:
  0.0 312.4 jit_solution(12305741517859162369)
XLA Ops:
  9.0 3.0 collective-permute-start
  13.6 3.0 collective-permute-start.3
  23.5 4.9 %all-to-all-start = ((bf16[8,232,72]{1,2,0:T(8,128)(2,1)}), bf16[8,232,72]{1,2,0:T(8,128)(2,1)S(1)}, u32[]{:S(2)}, u32[]{:S(2)}) async-start(bf16[8,232,72]{1,2,0:T(8,128)(2,1)} %broadcast_in_dim.76), calls=%async_computation | async-start | bytes 589824 | tf_op jit(solution)/shard_map/all_to_all | solution.py:89
  29.3 3.8 %collective-permute-start.5 = (bf16[72,1152]{1,0:T(8,128)(2,1)S(1)}, bf16[72,1152]{1,0:T(8,128)(2,1)S(1)}, u32[]{:S(2)}, u32[]{:S(2)}) collective-permute-start(bf16[72,1152]{1,0:T(8,128)(2,1)S(1)} %bitcast.66), channel_id=1, source_target_pairs={{0,24},{4,28},{8,16},{12,20},{16,8},{20,12},{24,0},{28,4},{1,25},{... | collective-permute-start | bytes 497672 | tf_op jit(solution)/shard_map/ppermute | solution.py:71
  34.7 8.8 %collective-permute-done.4 = bf16[72,1152]{1,0:T(8,128)(2,1)S(1)} collective-permute-done((bf16[72,1152]{1,0:T(8,128)(2,1)}, bf16[72,1152]{1,0:T(8,128)(2,1)S(1)}, u32[]{:S(2)}, u32[]{:S(2)}) %collective-permute-start.4) | collective-permute-done | bytes 165920 | tf_op jit(solution)/shard_map/ppermute | solution.py:71
  43.5 6.3 %collective-permute-done.5 = bf16[72,1152]{1,0:T(8,128)(2,1)S(1)} collective-permute-done((bf16[72,1152]{1,0:T(8,128)(2,1)S(1)}, bf16[72,1152]{1,0:T(8,128)(2,1)S(1)}, u32[]{:S(2)}, u32[]{:S(2)}) %collective-permute-start.5) | collective-permute-done | bytes 165920 | tf_op jit(solution)/shard_map/ppermute | solution.py:71
  49.8 2.0 collective-permute-done.6
  51.9 2.1 all-to-all-done
  54.9 4.7 %mixer_in.1 = (bf16[256,1152]{1,0:T(8,128)(2,1)}, f32[256,576]{1,0:T(8,128)}, bf16[256,576]{1,0:T(8,128)(2,1)}, f32[256,104]{1,0:T(8,128)}, f32[200,576]{1,0:T(8...) custom-call(s32[1,2]{1,0:T(1,128)} %lengths.7, s32[3]{0:T(128)} %pad_add_fusion.places, bf16[256,1152]{1,0:T(8,128)(2,1)} %tokens.5, ...), custom_call_target="tpu_custom_call" | custom-call | tf_op jit(solution)/shard_map/mixer_in/pallas_call | solution.py:47
  59.6 8.2 %all-gather = f32[1024,104]{1,0:T(8,128)} all-gather(f32[256,104]{1,0:T(8,128)} %get-tuple-element.68), channel_id=2, replica_groups=mesh['expert'=8,'hidden'=4] {'hidden'}, dimensions={0}, use_global_device_ids=true | all-gather | bytes 532480 | tf_op jit(solution)/shard_map/all_gather | solution.py:1007
  67.8 14.3 %scan_forward.1 = (f32[256,576]{1,0:T(8,128)}, f32[256,16,640]{2,1,0:T(8,128)}, f32[256,576]{1,0:T(8,128)}, f32[128,256]{1,0:T(8,128)}, bf16[256,72]{1,0:T(8,128)(2,1)}) custom-call(s32[1,2]{1,0:T(1,128)} %lengths.7, f32[4,256,104]{2,1,0:T(8,128)} %bitcast.58, bf16[256,576]{1,0:T(8,128)(2,1)} %get-tuple-element.69.activity, f32[200,576]{1,0:T(8,128)} %get-tuple-element.70.small), custom_call_target="tpu_custom_call" | custom-call | tf_op jit(solution)/shard_map/scan_forward/pallas_call | solution.py:47
  82.1 6.5 %all-gather.11.cloned.1.call-done.weight_z.weight_out = bf16[576,2304]{1,0:T(8,128)(2,1)} async-done(((bf16[72,2304]{1,0:T(8,128)(2,1)}), bf16[576,2304]{1,0:T(8,128)(2,1)}) %all-gather.11.cloned.1.call-update) | async-done | bytes 2654224 | tf_op jit(solution)/shard_map/all_gather | solution.py:989
  88.6 4.5 %mixer_out.1 = (bf16[256,576]{1,0:T(8,128)(2,1)}, f32[256,576]{1,0:T(8,128)}, bf16[256,1152]{1,0:T(8,128)(2,1)}) custom-call(f32[256,576]{1,0:T(8,128)} %get-tuple-element.71.out, bf16[256,576]{1,0:T(8,128)(2,1)} %get-tuple-element.69.activity, bf16[256,1152]{1,0:T(8,128)(2,1)} %get-tuple-element.72.normed, ...), custom_call_target="tpu_custom_call" | custom-call | tf_op jit(solution)/shard_map/mixer_out/pallas_call | solution.py:47
  98.7 7.3 %collective-permute-done.8 = bf16[128,1152]{1,0:T(8,128)(2,1)S(1)} collective-permute-done((bf16[128,1152]{1,0:T(8,128)(2,1)S(1)}, bf16[128,1152]{1,0:T(8,128)(2,1)S(1)}, u32[]{:S(2)}, u32[]{:S(2)}) %collective-permute-start.8) | collective-permute-done | bytes 294944 | tf_op jit(solution)/shard_map/ppermute | solution.py:71
  109.4 3.8 %middle.1 = (f32[256,1152]{1,0:T(8,128)}, bf16[256,1152]{1,0:T(8,128)(2,1)}, bf16[384,1152]{1,0:T(8,128)(2,1)}, bf16[384,1152]{1,0:T(8,128)(2,1)}, bf16[128,1152]{1,0:T(8,128)(2,1)}, /*index=5*/f32[8,256]{1,0:T(8,128)}) custom-call(s32[3]{0:T(128)} %pad_add_fusion.places, bf16[256,1152]{1,0:T(8,128)(2,1)} %tokens.5, bf16[128,1152]{1,0:T(8,128)(2,1)} %copy-done.14, ...), custom_call_target="tpu_custom_call" | custom-call | tf_op jit(solution)/shard_map/middle/pallas_call | solution.py:47
  116.2 17.2 %experts_local.1 = (bf16[256,1152]{1,0:T(8,128)(2,1)S(1)}, bf16[256,1152]{1,0:T(8,128)(2,1)S(1)}, f32[16,256]{1,0:T(8,128)S(1)}) custom-call(f32[1,256]{1,0:T(1,128)S(1)} %copy-done.6, f32[8,256]{1,0:T(8,128)S(1)} %copy-done.7, bf16[384,1152]{1,0:T(8,128)(2,1)S(1)} %copy-done.2, bf16[384,1152]{1,0:T(8,128)(2,1)S(1)} %copy-done.3, ...), custom_call_target="tpu_custom_call" | custom-call | tf_op jit(solution)/shard_map/experts_local/pallas_call | solution.py:47
  136.3 1.8 collective-permute-start.11
  138.9 8.4 %all-to-all-start.1 = ((f32[32,16,256]{2,1,0:T(8,128)}), f32[32,16,256]{2,1,0:T(8,128)S(1)}, u32[]{:S(2)}, u32[]{:S(2)}) async-start(f32[32,16,256]{2,1,0:T(8,128)} %broadcast_in_dim.78), calls=%async_computation.1 | async-start | bytes 1048576 | tf_op jit(solution)/shard_map/all_to_all | solution.py:89
  149.3 25.0 %all-to-all-done.1 = f32[32,16,256]{2,1,0:T(8,128)S(1)} async-done(((f32[32,16,256]{2,1,0:T(8,128)}), f32[32,16,256]{2,1,0:T(8,128)S(1)}, u32[]{:S(2)}, u32[]{:S(2)}) %all-to-all-start.1) | async-done | bytes 524320 | tf_op jit(solution)/shard_map/all_to_all | solution.py:89
  174.3 3.7 %all-gather.13.cloned.1.call-done = bf16[2048,1152]{1,0:T(8,128)(2,1)} async-done(((bf16[256,1152]{1,0:T(8,128)(2,1)}), bf16[2048,1152]{1,0:T(8,128)(2,1)}) %all-gather.13.cloned.1.call-update) | async-done | bytes 4718608 | tf_op jit(solution)/shard_map/all_gather | solution.py:1012
  178.1 28.8 %backward.1 = (f32[8,1,256]{2,1,0:T(1,128)}, f32[256,1152]{1,0:T(8,128)}, bf16[576,1152]{1,0:T(8,128)(2,1)}, f32[256,576]{1,0:T(8,128)}, bf16[256,576]{1,0:T(8,1...) custom-call(s32[1,2]{1,0:T(1,128)} %lengths.7, s32[3]{0:T(128)} %pad_add_fusion.places, ...), custom_call_target="tpu_custom_call" | custom-call | tf_op jit(solution)/shard_map/backward/pallas_call | solution.py:47
  206.9 9.3 %all-gather.2 = f32[1024,128]{1,0:T(8,128)} all-gather(f32[256,128]{1,0:T(8,128)} %get-tuple-element.90), channel_id=4, replica_groups=mesh['expert'=8,'hidden'=4] {'hidden'}, dimensions={0}, use_global_device_ids=true | all-gather | bytes 655360 | tf_op jit(solution)/shard_map/all_gather | solution.py:1034
  216.2 8.3 %mixer_back.1 = (bf16[512,1152]{1,0:T(8,128)(2,1)}, bf16[8,72,1920]{2,1,0:T(8,128)(2,1)}) custom-call(s32[1,2]{1,0:T(1,128)} %lengths.7, f32[4,256,128]{2,1,0:T(8,128)} %bitcast.57, f32[256,576]{1,0:T(8,128)} %get-tuple-element.91.grad_act, bf16[256,576]{1,0:T(8,128)(2,1)} %get-tuple-element.69.activity, f32[256,576]{1,0:T(8,128)} %get-tuple-element.92.inner, ...), custom_call_target="tpu_custom_call" | custom-call | tf_op jit(solution)/shard_map/mixer_back/pallas_call | solution.py:47
  226.5 4.8 %all-gather.15.cloned.1.call-done = bf16[1024,1152]{1,0:T(8,128)(2,1)} async-done(((bf16[128,1152]{1,0:T(8,128)(2,1)}), bf16[1024,1152]{1,0:T(8,128)(2,1)}) %all-gather.15.cloned.1.call-update) | async-done | bytes 2359312 | tf_op jit(solution)/shard_map/all_gather | solution.py:1018
  236.4 3.8 %all-to-all-start.2 = ((bf16[8,72,1920]{2,1,0:T(8,128)(2,1)}), bf16[8,72,1920]{2,1,0:T(8,128)(2,1)S(1)}, u32[]{:S(2)}, u32[]{:S(2)}) async-start(bf16[8,72,1920]{2,1,0:T(8,128)(2,1)} %get-tuple-element.100), calls=%async_computation.2 | async-start | bytes 4423680 | tf_op jit(solution)/shard_map/all_to_all | solution.py:1042
  240.2 9.1 %collective-permute-done.15 = bf16[256,1152]{1,0:T(8,128)(2,1)} collective-permute-done((bf16[256,1152]{1,0:T(8,128)(2,1)S(1)}, bf16[256,1152]{1,0:T(8,128)(2,1)}, u32[]{:S(2)}, u32[]{:S(2)}) %collective-permute-start.15) | collective-permute-done | bytes 589856 | tf_op jit(solution)/shard_map/ppermute | solution.py:71
  250.6 32.6 %expert_grads.1 = (f32[8,144,768]{2,1,0:T(8,128)}, f32[8,144,768]{2,1,0:T(8,128)}) custom-call(s32[3]{0:T(128)} %pad_add_fusion.places, f32[8,1,256]{2,1,0:T(1,128)} %reshape.117.codes, f32[8,1,256]{2,1,0:T(1,128)} %reshape.119.gates, bf16[8,128,1152]{2,1,0:T(8,128)(2,1)} %bitcast.76, bf16[8,128,1152]{2,1,0:T(8,128)(2,1)} %collective-permute-done.17.refs_1_, ...), custom_call_target="tpu_custom_call" | custom-call | flops 32614907904 | tf_op jit(solution)/shard_map/expert_grads/pallas_call | solution.py:47
  286.3 5.0 %all-to-all-done.2.both = bf16[8,72,1920]{2,1,0:T(8,128)(2,1)S(1)} async-done(((bf16[8,72,1920]{2,1,0:T(8,128)(2,1)}), bf16[8,72,1920]{2,1,0:T(8,128)(2,1)S(1)}, u32[]{:S(2)}, u32[]{:S(2)}) %all-to-all-start.2) | async-done | bytes 2211872 | tf_op jit(solution)/shard_map/all_to_all | solution.py:1042
  291.3 2.3 copy-done
  293.6 2.0 copy-done.1
  295.6 4.6 %proj_grads.1 = (f32[72,1152]{1,0:T(8,128)}, f32[72,1152]{1,0:T(8,128)}, f32[72,104]{1,0:T(8,128)}, f32[4,72]{1,0:T(4,128)}, f32[1,72]{1,0:T(1,128)}, /*index=5*...) custom-call(s32[3]{0:T(128)S(1)} %copy-done.5, ...), custom_call_target="tpu_custom_call" | custom-call | tf_op jit(solution)/shard_map/proj_grads/pallas_call | solution.py:47
  300.2 5.1 %all-gather.6 = f32[4,1,144]{2,1,0:T(1,128)S(1)} all-gather(f32[1,1,144]{2,1,0:T(1,128)S(1)} %bitcast.51), channel_id=7, replica_groups=mesh['expert'=8,'hidden'=4] {'hidden'}, dimensions={0}, use_global_device_ids=true | all-gather | bytes 2880 | tf_op jit(solution)/shard_map/all_gather | solution.py:1083
  (137 shorter events, 41.8 us)
Async XLA Ops:
  7.2 15.5 %copy-start.20 = (bf16[72,104]{1,0:T(8,128)(2,1)S(1)}, bf16[72,104]{1,0:T(8,128)(2,1)}, u32[]{:S(2)}) copy-start(bf16[72,104]{1,0:T(8,128)(2,1)} %param.28) | copy-start | bytes 44932
  7.2 81.4 %all-gather.11.cloned.1.call-start = ((), (), s32[]{:S(2)}) async-start(), calls=%async_computation.3 | async-start | bytes 2985984 | tf_op jit(solution)/shard_map/all_gather | solution.py:989
  9.0 20.2 %collective-permute-start = (bf16[72,1152]{1,0:T(8,128)(2,1)}, bf16[72,1152]{1,0:T(8,128)(2,1)S(1)}, u32[]{:S(2)}, u32[]{:S(2)}) collective-permute-start(bf16[72,1152]{1,0:T(8,128)(2,1)} %bitcast.60), channel_id=1, source_target_pairs={{0,4},{4,0},{8,12},{12,8},{16,20},{20,16},{24,28},{28,24},{1,5},{5... | collective-permute-start | bytes 497672 | tf_op jit(solution)/shard_map/ppermute | solution.py:71
  12.0 21.0 %collective-permute-start.1 = (bf16[72,1152]{1,0:T(8,128)(2,1)}, bf16[72,1152]{1,0:T(8,128)(2,1)S(1)}, u32[]{:S(2)}, u32[]{:S(2)}) collective-permute-start(bf16[72,1152]{1,0:T(8,128)(2,1)} %bitcast.61), channel_id=1, source_target_pairs={{0,8},{4,12},{8,0},{12,4},{16,24},{20,28},{24,16},{28,20},{1,9},{5... | collective-permute-start | bytes 497672 | tf_op jit(solution)/shard_map/ppermute | solution.py:71
  13.6 21.0 %collective-permute-start.2 = (bf16[72,1152]{1,0:T(8,128)(2,1)}, bf16[72,1152]{1,0:T(8,128)(2,1)S(1)}, u32[]{:S(2)}, u32[]{:S(2)}) collective-permute-start(bf16[72,1152]{1,0:T(8,128)(2,1)} %bitcast.62), channel_id=1, source_target_pairs={{0,12},{4,8},{8,4},{12,0},{16,28},{20,24},{24,20},{28,16},{1,13},{... | collective-permute-start | bytes 497672 | tf_op jit(solution)/shard_map/ppermute | solution.py:71
  13.6 21.0 %collective-permute-start.3 = (bf16[72,1152]{1,0:T(8,128)(2,1)}, bf16[72,1152]{1,0:T(8,128)(2,1)S(1)}, u32[]{:S(2)}, u32[]{:S(2)}) collective-permute-start(bf16[72,1152]{1,0:T(8,128)(2,1)} %bitcast.63), channel_id=1, source_target_pairs={{0,16},{4,20},{8,24},{12,28},{16,0},{20,4},{24,8},{28,12},{1,17},{... | collective-permute-start | bytes 497672 | tf_op jit(solution)/shard_map/ppermute | solution.py:71
  16.6 26.9 %collective-permute-start.4 = (bf16[72,1152]{1,0:T(8,128)(2,1)}, bf16[72,1152]{1,0:T(8,128)(2,1)S(1)}, u32[]{:S(2)}, u32[]{:S(2)}) collective-permute-start(bf16[72,1152]{1,0:T(8,128)(2,1)} %bitcast.64), channel_id=1, source_target_pairs={{0,20},{4,16},{8,28},{12,24},{16,4},{20,0},{24,12},{28,8},{1,21},{... | collective-permute-start | bytes 497672 | tf_op jit(solution)/shard_map/ppermute | solution.py:71
  23.5 30.4 %all-to-all-start = ((bf16[8,232,72]{1,2,0:T(8,128)(2,1)}), bf16[8,232,72]{1,2,0:T(8,128)(2,1)S(1)}, u32[]{:S(2)}, u32[]{:S(2)}) async-start(bf16[8,232,72]{1,2,0:T(8,128)(2,1)} %broadcast_in_dim.76), calls=%async_computation | async-start | bytes 589824 | tf_op jit(solution)/shard_map/all_to_all | solution.py:89
  28.4 149.5 %all-gather.13.cloned.1.call-start = ((), (), s32[]{:S(2)}) async-start(), calls=%async_computation.4 | async-start | bytes 5308416 | tf_op jit(solution)/shard_map/all_gather | solution.py:1012
  29.3 20.5 %collective-permute-start.5 = (bf16[72,1152]{1,0:T(8,128)(2,1)S(1)}, bf16[72,1152]{1,0:T(8,128)(2,1)S(1)}, u32[]{:S(2)}, u32[]{:S(2)}) collective-permute-start(bf16[72,1152]{1,0:T(8,128)(2,1)S(1)} %bitcast.66), channel_id=1, source_target_pairs={{0,24},{4,28},{8,16},{12,20},{16,8},{20,12},{24,0},{28,4},{1,25},{... | collective-permute-start | bytes 497672 | tf_op jit(solution)/shard_map/ppermute | solution.py:71
  33.1 18.8 %collective-permute-start.6 = (bf16[72,1152]{1,0:T(8,128)(2,1)S(1)}, bf16[72,1152]{1,0:T(8,128)(2,1)S(1)}, u32[]{:S(2)}, u32[]{:S(2)}) collective-permute-start(bf16[72,1152]{1,0:T(8,128)(2,1)S(1)} %bitcast.67), channel_id=1, source_target_pairs={{0,28},{4,24},{8,20},{12,16},{16,12},{20,8},{24,4},{28,0},{1,29},{... | collective-permute-start | bytes 497672 | tf_op jit(solution)/shard_map/ppermute | solution.py:71
  93.2 13.0 %copy-start.19 = (s32[1,2]{1,0:T(1,128)S(1)}, s32[1,2]{1,0:T(1,128)}, u32[]{:S(2)}) copy-start(s32[1,2]{1,0:T(1,128)} %lengths.7) | copy-start | bytes 28
  93.2 14.9 %copy-start.22 = (s32[256,1]{0,1:T(1,128)S(1)}, s32[256,1]{0,1:T(1,128)}, u32[]{:S(2)}) copy-start(s32[256,1]{0,1:T(1,128)} %param.22) | copy-start | bytes 3076
  94.2 1.6 collective-permute-start.7
  96.9 9.1 %collective-permute-start.8 = (bf16[128,1152]{1,0:T(8,128)(2,1)S(1)}, bf16[128,1152]{1,0:T(8,128)(2,1)S(1)}, u32[]{:S(2)}, u32[]{:S(2)}) collective-permute-start(bf16[128,1152]{1,0:T(8,128)(2,1)S(1)} %add_convert_fusion.5), channel_id=1, source_target_pairs={{0,2},{1,3},{2,0},{3,1},{4,6},{5,7},{6,4},{7,5},{8,10},{9,11},{10,... | collective-permute-start | bytes 884744 | tf_op jit(solution)/shard_map/ppermute | solution.py:71
  106.1 2.6 collective-permute-start.9
  134.3 1.8 collective-permute-start.10
  136.3 11.3 %collective-permute-start.11 = (bf16[128,1152]{1,0:T(8,128)(2,1)S(1)}, bf16[128,1152]{1,0:T(8,128)(2,1)S(1)}, u32[]{:S(2)}, u32[]{:S(2)}) collective-permute-start(bf16[128,1152]{1,0:T(8,128)(2,1)S(1)} %add_convert_fusion.3), channel_id=1, source_target_pairs={{0,2},{1,3},{2,0},{3,1},{4,6},{5,7},{6,4},{7,5},{8,10},{9,11},{10,... | collective-permute-start | bytes 884744 | tf_op jit(solution)/shard_map/ppermute | solution.py:71
  138.9 35.3 %all-to-all-start.1 = ((f32[32,16,256]{2,1,0:T(8,128)}), f32[32,16,256]{2,1,0:T(8,128)S(1)}, u32[]{:S(2)}, u32[]{:S(2)}) async-start(f32[32,16,256]{2,1,0:T(8,128)} %broadcast_in_dim.78), calls=%async_computation.1 | async-start | bytes 1048576 | tf_op jit(solution)/shard_map/all_to_all | solution.py:89
  147.3 83.9 %all-gather.15.cloned.1.call-start = ((), (), s32[]{:S(2)}) async-start(), calls=%async_computation.5 | async-start | bytes 2654208 | tf_op jit(solution)/shard_map/all_gather | solution.py:1018
  147.6 30.3 %copy-start.16 = (bf16[128,1152]{1,0:T(8,128)(2,1)}, bf16[128,1152]{1,0:T(8,128)(2,1)S(1)}, u32[]{:S(2)}) copy-start(bf16[128,1152]{1,0:T(8,128)(2,1)S(1)} %add_convert_fusion.2.low) | copy-start | bytes 884740
  147.6 1.6 collective-permute-start.12
  149.3 28.6 %copy-start.15 = (bf16[128,1152]{1,0:T(8,128)(2,1)}, bf16[128,1152]{1,0:T(8,128)(2,1)S(1)}, u32[]{:S(2)}) copy-start(bf16[128,1152]{1,0:T(8,128)(2,1)S(1)} %collective-permute-done.12.other.refs_2_) | copy-start | bytes 884740
  177.9 38.3 %collective-permute-start.13 = (bf16[8,256,1152]{2,1,0:T(8,128)(2,1)}, bf16[8,256,1152]{2,1,0:T(8,128)(2,1)}, u32[]{:S(2)}, u32[]{:S(2)}) collective-permute-start(bf16[8,256,1152]{2,1,0:T(8,128)(2,1)} %after.1.refs_2_.refs_0_), channel_id=1, source_target_pairs={{0,1},{1,0},{2,3},{3,2},{4,5},{5,4},{6,7},{7,6},{8,9},{9,8},{10,11... | collective-permute-start | bytes 14155784 | tf_op jit(solution)/shard_map/ppermute | solution.py:71
  224.6 7.5 %copy-start.21 = (f32[8,1,256]{2,1,0:T(1,128)S(1)}, f32[8,1,256]{2,1,0:T(1,128)}, u32[]{:S(2)}) copy-start(f32[8,1,256]{2,1,0:T(1,128)} %get-tuple-element.89) | copy-start | bytes 24580
  224.6 8.7 %copy-start.12 = (bf16[512,1152]{1,0:T(8,128)(2,1)S(1)}, bf16[512,1152]{1,0:T(8,128)(2,1)}, u32[]{:S(2)}) copy-start(bf16[512,1152]{1,0:T(8,128)(2,1)} %get-tuple-element.98) | copy-start | bytes 3538948
  225.9 7.4 %collective-permute-start.14 = (bf16[256,1152]{1,0:T(8,128)(2,1)S(1)}, bf16[256,1152]{1,0:T(8,128)(2,1)S(1)}, u32[]{:S(2)}, u32[]{:S(2)}) collective-permute-start(bf16[256,1152]{1,0:T(8,128)(2,1)S(1)} %constant_dynamic-slice_fusion), channel_id=1, source_target_pairs={{0,1},{1,0},{2,3},{3,2},{4,5},{5,4},{6,7},{7,6},{8,9},{9,8},{10,11... | collective-permute-start | bytes 1769480 | tf_op jit(solution)/shard_map/ppermute | solution.py:71
  231.3 19.4 %collective-permute-start.17 = (bf16[8,128,1152]{2,1,0:T(8,128)(2,1)}, bf16[8,128,1152]{2,1,0:T(8,128)(2,1)}, u32[]{:S(2)}, u32[]{:S(2)}) collective-permute-start(bf16[8,128,1152]{2,1,0:T(8,128)(2,1)} %bitcast.75), channel_id=1, source_target_pairs={{0,1},{1,0},{2,3},{3,2},{4,5},{5,4},{6,7},{7,6},{8,9},{9,8},{10,11... | collective-permute-start | bytes 7077896 | tf_op jit(solution)/shard_map/ppermute | solution.py:71
  233.4 15.9 %collective-permute-start.15 = (bf16[256,1152]{1,0:T(8,128)(2,1)S(1)}, bf16[256,1152]{1,0:T(8,128)(2,1)}, u32[]{:S(2)}, u32[]{:S(2)}) collective-permute-start(bf16[256,1152]{1,0:T(8,128)(2,1)S(1)} %add_convert_fusion.1), channel_id=1, source_target_pairs={{0,2},{1,3},{2,0},{3,1},{4,6},{5,7},{6,4},{7,5},{8,10},{9,11},{10,... | collective-permute-start | bytes 1769480 | tf_op jit(solution)/shard_map/ppermute | solution.py:71
  236.4 54.9 %all-to-all-start.2 = ((bf16[8,72,1920]{2,1,0:T(8,128)(2,1)}), bf16[8,72,1920]{2,1,0:T(8,128)(2,1)S(1)}, u32[]{:S(2)}, u32[]{:S(2)}) async-start(bf16[8,72,1920]{2,1,0:T(8,128)(2,1)} %get-tuple-element.100), calls=%async_computation.2 | async-start | bytes 4423680 | tf_op jit(solution)/shard_map/all_to_all | solution.py:1042
  250.5 32.7 %collective-permute-start.16 = (bf16[256,1152]{1,0:T(8,128)(2,1)S(1)}, bf16[256,1152]{1,0:T(8,128)(2,1)S(1)}, u32[]{:S(2)}, u32[]{:S(2)}) collective-permute-start(bf16[256,1152]{1,0:T(8,128)(2,1)S(1)} %add_convert_fusion), channel_id=1, source_target_pairs={{0,1},{1,0},{2,3},{3,2},{4,5},{5,4},{6,7},{7,6},{8,9},{9,8},{10,11... | collective-permute-start | bytes 1769480 | tf_op jit(solution)/shard_map/ppermute | solution.py:71
  250.6 33.0 %copy-start.13 = (f32[256,1152]{1,0:T(8,128)S(1)}, f32[256,1152]{1,0:T(8,128)}, u32[]{:S(2)}) copy-start(f32[256,1152]{1,0:T(8,128)} %get-tuple-element.99) | copy-start | bytes 3538948
  (15 other events, 38.5 us)
Sparse Core Ops, SparseCore 0:
  10.8 77.8 all-gather.10
  90.8 87.0 all-gather.12
  180.1 51.0 all-gather.14

commit v4 on v3

--- a/solution.py
+++ b/solution.py
@@ -32,7 +32,7 @@
     return jax.ShapeDtypeStruct(dims, bf16)
 
 
-def call(body, name, out_shape, scratch=(), scalars=0, operands=(), flops=0, limit=56, parts={}, after=0, known=False, **grid):
+def call(body, name, out_shape, scratch=(), scalars=0, operands=(), flops=0, limit=60, parts={}, after=0, known=False, **grid):
     if not grid:
         specs = [pl.BlockSpec(memory_space=pltpu.SMEM)] * scalars
         specs += [pl.BlockSpec(memory_space=pltpu.VMEM)] * (len(operands) - scalars)
@@ -112,22 +112,13 @@
     )(values, *others)
 
 
-def hidden_halves(values):
-    half = values.shape[0] // 2
-    place = lax.axis_index("hidden") % 2
-    kept = lax.dynamic_slice_in_dim(values, place * half, half, 0)
-    given = lax.dynamic_slice_in_dim(values, (1 - place) * half, half, 0)
+def hidden_halves(kept, given, *others):
     low = (kept.astype(f32) + swap(given, "hidden", 1).astype(f32)).astype(bf16)
-    low = (low.astype(f32) + swap(low, "hidden", 2).astype(f32)).astype(bf16)
+    far = swap(low, "hidden", 2)
+    if others:
+        far = after(far, *others)
+    low = (low.astype(f32) + far.astype(f32)).astype(bf16)
     return low, swap(low, "hidden", 1)
-
-
-def hidden_sum(values):
-    low, other = hidden_halves(values)
-    place = lax.axis_index("hidden") % 2
-    return jnp.where(
-        place == 0, jnp.concatenate([low, other]), jnp.concatenate([other, low])
-    ).astype(f32)
 
 
 def softplus(values):
@@ -199,6 +190,13 @@
 
 def lane(tile, j, width):
     return jnp.broadcast_to(tile[:, j : j + 1], (tile.shape[0], width))
+
+
+def split(values, place, kept, given):
+    half = values.shape[0] // 2
+    first = place == 0
+    kept[...] = jnp.where(first, values[:half], values[half:]).astype(bf16)
+    given[...] = jnp.where(first, values[half:], values[:half]).astype(bf16)
 
 
 class Sizes:
@@ -226,12 +224,10 @@
     values = tokens[...].astype(f32)
     low = (values * rms_scale(values) * vectors[0:1, :]).astype(bf16)
     normed[...] = low
-    half = share.shape[0] // 2
-    share[:half, :] = normed[pl.ds(pl.multiple_of(places[1] * half, half), half), :]
-    size = half // 2
-    for k in range(2):
-        at = pl.multiple_of((places[0] ^ (2 * k)) * size, size)
-        share[half + k * size : half + (k + 1) * size, :] = cotangent[pl.ds(at, size), :]
+    size = share.shape[0] // 2
+    at = pl.ds(pl.multiple_of(places[0] * size, size), size)
+    share[:size, :] = normed[at, :]
+    share[size:, :] = cotangent[at, :]
     values = dot(low, weight[...], 1, 1)
     inner[...] = values
     kernel = small[sizes.conv : sizes.conv + sizes.taps, :]
@@ -255,7 +251,7 @@
             shape_of(positions, sizes.state),
             shape_of(sizes.rows, channels),
             shape_of(sizes.vectors, width),
-            low_of(positions, width),
+            low_of(positions // 2, width),
         ),
         [pltpu.VMEM((positions + 2 * ROWS, channels), f32)],
         2,
@@ -326,26 +322,34 @@
     )
 
 
-def mixer_out_body(sizes, out, activity, normed, weight_z, weight_out, small, mixed, gate, branch):
+def mixer_out_body(
+    sizes, places, out, activity, normed, weight_z, weight_out, small, mixed, gate, kept, given
+):
     shade = dot(normed[...], weight_z[...], 1, 1)
     gate[...] = shade
     at = sizes.conv + sizes.taps + 2
     values = out[...] + small[at : at + 1, :] * activity[...].astype(f32)
     low = (values * (shade * sigmoid(shade))).astype(bf16)
     mixed[...] = low
-    branch[...] = dot(low, weight_out[...]).astype(bf16)
-
-
-def mixer_out(sizes, out, activity, normed, weights, small):
+    split(dot(low, weight_out[...]), places[1], kept, given)
+
+
+def mixer_out(sizes, places, out, activity, normed, weights, small):
     positions, channels = activity.shape
     width = normed.shape[1]
     return call(
         functools.partial(mixer_out_body, sizes),
         "mixer_out",
-        (low_of(positions, channels), shape_of(positions, channels), low_of(positions, width)),
-        operands=(out, activity, normed, weights, weights, small),
+        (
+            low_of(positions, channels),
+            shape_of(positions, channels),
+            low_of(positions // 2, width),
+            low_of(positions // 2, width),
+        ),
+        scalars=1,
+        operands=(places, out, activity, normed, weights, weights, small),
         flops=4 * positions * width * channels,
-        parts={3: 0, 4: 1},
+        parts={4: 0, 5: 1},
     )
 
 
@@ -379,7 +383,7 @@
     resid, normed_two, sent, sent_grad, share, logits,
 ):
     half = low.shape[0]
-    experts = logits.shape[0]
+    experts = logits.shape[0] - ROWS
     capacity = sent.shape[0] // experts
     resid[pl.ds(pl.multiple_of(places[1] * half, half), half), :] = low[...].astype(f32)
     resid[pl.ds(pl.multiple_of((1 - places[1]) * half, half), half), :] = other[...].astype(f32)
@@ -387,7 +391,8 @@
     resid[...] = values
     rows = (values * rms_scale(values) * vectors[1:2, :]).astype(bf16)
     normed_two[...] = rows
-    logits[...] = dot(vectors[2 : 2 + experts, :].astype(bf16), rows, 1, 1)
+    logits[:experts, :] = dot(vectors[2 : 2 + experts, :].astype(bf16), rows, 1, 1)
+    logits[experts:, :] = jnp.broadcast_to(codes[...], (ROWS, codes.shape[1]))
     every = picks(slots_of(codes[...], experts, capacity), 0, sent.shape[0]).astype(bf16)
     sent[...] = dot(every, rows).astype(bf16)
     sent_grad[...] = dot(every, cotangent[...]).astype(bf16)
@@ -409,7 +414,7 @@
             low_of(slots, width),
             low_of(slots, width),
             low_of(positions // 2, width),
-            shape_of(experts, positions),
+            shape_of(experts + ROWS, positions),
         ),
         (),
         1,
@@ -419,19 +424,16 @@
 
 
 def experts_body(
-    codes, logits, rows, grads, up, down, out, back, packed, slots, outs, backs
+    places, codes, logits, rows, grads, up, down, out, kept, given, packed, slots, outs, backs, gate_row
 ):
     step = pl.program_id(0)
     experts = pl.num_programs(0)
     capacity = rows.shape[0]
-    count = logits.shape[0]
 
     @pl.when(step == 0)
     def _():
         slots[...] = slots_of(codes[...], experts, capacity)
-        packed[:count, :] = logits[...]
-        packed[count:, :] = jnp.zeros((packed.shape[0] - count, packed.shape[1]), f32)
-        packed[count : count + 1, :] = codes[...]
+        gate_row[...] = jnp.zeros_like(gate_row)
 
     first = pl.multiple_of(step * capacity, capacity)
     active, slope = gelu_pair(dot(rows[...], up[0]))
@@ -439,7 +441,7 @@
     low = active.astype(bf16)
     gate_slots = jnp.sum(low.astype(f32) * plain, axis=1, keepdims=True)
     chosen = picks(slots[...], first, capacity)
-    packed[count + 1 : count + 2, :] += jnp.sum(chosen * gate_slots, axis=0, keepdims=True)
+    gate_row[...] += jnp.sum(chosen * gate_slots, axis=0, keepdims=True)
     outs[pl.ds(first, capacity), :] = dot(low, down[0]).astype(bf16)
     backs[pl.ds(first, capacity), :] = dot((plain * slope).astype(bf16), up[0], 1, 1).astype(bf16)
 
@@ -447,64 +449,72 @@
     def _():
         every = picks(slots[...], 0, outs.shape[0]).astype(bf16)
         out[...] = dot(every, outs[...], 0, 0).astype(bf16)
-        back[...] = dot(every, backs[...], 0, 0).astype(bf16)
-
-
-def experts_local(codes, logits, rows, grads, up, down):
+        split(dot(every, backs[...], 0, 0), places[1], kept, given)
+        packed[...] = logits[...]
+        packed[experts + 1 : experts + 2, :] = gate_row[...]
+
+
+def experts_local(places, codes, logits, rows, grads, up, down):
     slots, width = rows.shape
     experts, _, hidden = up.shape
     positions = codes.shape[1]
     capacity = slots // experts
+    shapes = (
+        low_of(positions, width),
+        low_of(positions // 2, width),
+        low_of(positions // 2, width),
+        shape_of(*logits.shape),
+    )
     return call(
         experts_body,
         "experts_local",
-        (
-            low_of(positions, width),
-            low_of(positions, width),
-            shape_of(2 * ROWS, positions),
-        ),
+        shapes,
         [
             pltpu.VMEM((1, positions), f32),
             pltpu.VMEM((slots, width), bf16),
             pltpu.VMEM((slots, width), bf16),
+            pltpu.VMEM((1, positions), f32),
         ],
-        operands=(codes, logits, rows, grads, up, down),
+        operands=(places, codes, logits, rows, grads, up, down),
         flops=8 * slots * width * hidden,
-        limit=40,
         grid=(experts,),
         in_specs=[
+            pl.BlockSpec(memory_space=pltpu.SMEM),
             whole((1, positions)),
-            whole((experts, positions)),
+            whole(logits.shape),
             pl.BlockSpec((capacity, width), lambda i: (i, 0)),
             pl.BlockSpec((capacity, width), lambda i: (i, 0)),
             pl.BlockSpec((1, width, hidden), lambda i: (i, 0, 0)),
             pl.BlockSpec((1, hidden, width), lambda i: (i, 0, 0)),
         ],
-        out_specs=(
-            whole((positions, width)),
-            whole((positions, width)),
-            whole((2 * ROWS, positions)),
-        ),
+        out_specs=tuple(whole(v.shape) for v in shapes),
     )
 
 
 def expert_grads_body(
     places, codes, gates, *refs,
 ):
-    rows, grads = refs[:2], refs[2:4]
-    up, down, up_grad, down_grad, sent, sent_grad, gate_slots = refs[4:]
+    rows, grads = refs[:2], refs[2:6]
+    up, down, up_grad, down_grad, sent, sent_grad, gate_slots = refs[6:]
     step = pl.program_id(0)
     experts, total, width = sent.shape
     count, _, positions = codes.shape
     capacity = total // count
+    quarter = positions // 4
     block = up_grad.shape[1]
-    window = min(padded(block + LANES), width)
+    window = min(padded(block + LANES - 2 * ROWS), width)
 
     @pl.when(step == 0)
     def _():
+        shape = (positions, positions)
+        lanes = lax.broadcasted_iota(jnp.int32, shape, 1)
+        part = lanes // quarter
+        home = ((part % 2 * 2 + part // 2) ^ places[0]) * quarter + lanes % quarter
+        order = (lax.broadcasted_iota(jnp.int32, shape, 0) == home).astype(f32).astype(bf16)
         for r in range(count):
-            chosen = picks(slots_of(codes[r], experts, capacity), 0, experts * capacity)
-            pick = chosen.astype(bf16)
+            code = codes[r, experts : experts + 1, :]
+            chosen = picks(slots_of(code, experts, capacity), 0, experts * capacity)
+            pick = dot(chosen.astype(bf16), order).astype(bf16)
             gate = jnp.sum(chosen * gates[r], axis=1, keepdims=True)
             part = pl.ds(r * capacity, capacity)
             for pieces, target in ((rows, sent), (grads, sent_grad)):
@@ -536,9 +546,12 @@
     shape = (experts, block, hidden)
     out = pl.BlockSpec((1, block, hidden), lambda i: (i, 0, 0))
     half = whole((count, positions // 2, width))
-    second = pl.BlockSpec(
-        (count, positions // 2, width), lambda i: (0, 1, 0), pipeline_mode=pl.Buffered(1)
-    )
+
+    def piece(values):
+        last = values.shape[1] * 4 // positions - 1
+        shape = (count, positions // 4, width)
+        return pl.BlockSpec(shape, lambda i: (0, last, 0), pipeline_mode=pl.Buffered(1))
+
     return call(
         expert_grads_body,
         "expert_grads",
@@ -551,14 +564,14 @@
         operands=(places, codes, gates, *rows, *grads, up, down),
         flops=12 * experts * slots * width * hidden,
         known=True,
-        limit=54,
         grid=(experts,),
         in_specs=[
             pl.BlockSpec(memory_space=pltpu.SMEM),
+            whole((count, codes.shape[1], positions)),
             whole((count, 1, positions)),
-            whole((count, 1, positions)),
-            *([half] * 2),
-            *([second] * 2),
+            half,
+            half,
+            *(piece(values) for values in grads),
             pl.BlockSpec((1, width, hidden), lambda i: (i, 0, 0)),
             pl.BlockSpec((1, hidden, width), lambda i: (i, 0, 0)),
         ],
@@ -566,10 +579,10 @@
     )
 
 
-def sinkhorn(packed, experts):
-    start = jnp.exp(packed[:, 0, :experts, :])
-    codes = packed[:, 0, experts : experts + 1, :]
-    grad_gates = jnp.sum(packed[:, :, experts + 1 : experts + 2, :], axis=1)
+def sinkhorn(packed, gate_parts, experts):
+    start = jnp.exp(packed[:, :experts, :])
+    codes = packed[:, experts : experts + 1, :]
+    grad_gates = jnp.sum(gate_parts[...], axis=0)
     valid = (codes >= 0).astype(f32)
     onehot = (lax.broadcasted_iota(jnp.int32, start.shape, 1).astype(f32) == codes).astype(f32)
     weights = start
@@ -590,7 +603,7 @@
 
 
 def backward_body(
-    sizes, lengths, places, packed, low, other, vectors, resid, normed_two, cotangent, mixed,
+    sizes, lengths, places, packed, gate_parts, low, other, vectors, resid, normed_two, cotangent, mixed,
     weight_out, out, activity, gate, pre, small, basis, states, rank_low,
     gates, grad_resid, out_grad, grad_act, grad_gate, grad_part, early,
     all_gates, all_grads, branch_grad, far_steps, steps, inputs, outer, rates, sum_input,
@@ -604,7 +617,7 @@
     experts = all_grads.shape[1]
     half = low.shape[0]
 
-    every_gate, every_grad = sinkhorn(packed, experts)
+    every_gate, every_grad = sinkhorn(packed, gate_parts, experts)
     gates[...] = every_gate
     all_gates[...] = every_gate
     all_grads[...] = every_grad
@@ -722,7 +735,7 @@
 
 
 def backward(sizes, operands, experts, devices):
-    (_, _, packed, _, _, _, resid, _, _, mixed, _, _, activity) = operands[:13]
+    resid, activity = operands[7], operands[13]
     positions, width = resid.shape
     channels = activity.shape[1]
     lanes = padded(channels)
@@ -757,19 +770,18 @@
         2,
         operands,
         40 * positions * width * channels,
-        parts={10: 1},
+        parts={11: 1},
     )
 
 
 def mixer_back_body(
-    sizes, lengths, parts, grad_act, activity, inner, small, weight_x, weight_z, grad_z, tokens,
-    early, expert_out, out_grad, _near, both, late, shifted, wide, sums, shares,
+    sizes, lengths, places, parts, grad_act, activity, inner, small, weight_x, weight_z, grad_z, tokens,
+    early, expert_out, out_grad, _grads, _rows, kept, given, late, shifted, wide, sums, shares,
 ):
     positions, channels = activity.shape
     devices, own, lanes = early.shape
     late[:, :, lanes : 2 * lanes] = early[...]
     late[:, :, 2 * lanes :] = out_grad[...]
-    both[:positions, :] = expert_out[...]
     taps = sizes.taps
     low = jnp.sum(parts[...], axis=0)[:, : sizes.state].astype(bf16)
     state_grad = dot(activity[...], low, 0, 0)
@@ -793,7 +805,10 @@
     put(wide, total)
     turned = wide[...].T
     part = dot(grad_x, weight_x[...]) + dot(grad_z[...], weight_z[...])
-    both[positions:, :] = part.astype(bf16)
+    first = places[1] == 0
+    low = part.astype(bf16)
+    kept[...] = jnp.where(first, expert_out[...], low)
+    given[...] = jnp.where(first, low, expert_out[...])
     values = tokens[...].astype(f32)
     shares[...] = jnp.broadcast_to(
         jnp.sum(part * (values * rms_scale(values)), axis=0, keepdims=True), shares.shape
@@ -813,47 +828,46 @@
 
 
 def mixer_back(sizes, operands):
-    activity, tokens, early = operands[3], operands[9], operands[10]
+    activity, tokens, early = operands[4], operands[10], operands[11]
     positions, width = tokens.shape
     channels = activity.shape[1]
     return call(
         functools.partial(mixer_back_body, sizes),
         "mixer_back",
-        (low_of(2 * positions, width), low_of(*early.shape[:2], 2 * early.shape[2] + width)),
+        (low_of(positions, width), low_of(positions, width), low_of(*early.shape[:2], 2 * early.shape[2] + width)),
         [
             pltpu.VMEM((positions + 2 * ROWS, channels), f32),
             pltpu.VMEM((positions, padded(channels)), f32),
             pltpu.VMEM((ROWS, padded(channels)), f32),
             pltpu.VMEM((ROWS, width), f32),
         ],
-        1,
+        2,
         operands,
         6 * positions * width * channels,
-        parts={7: 0},
-        after=1,
+        parts={8: 0},
+        after=2,
     )
 
 
 def proj_grads_body(
     sizes, places, both, *refs,
 ):
-    half, other, _ = refs[:3]
-    grad_x, grad_z, state, conv, bias, gain_one, decay, proj, step_bias, skip, gain_two = refs[3:14]
-    router, out, late_sum, early_sum = refs[14:]
+    pieces = refs[:4]
+    grad_x, grad_z, state, conv, bias, gain_one, decay, proj, step_bias, skip, gain_two = refs[4:15]
+    router, out, late_sum, early_sum, buffer = refs[15:]
     step = pl.program_id(0)
     count, own, lanes = both.shape
-    width = half.shape[2]
+    _, size, width = pieces[0].shape
     lanes = lanes - width
-    size = half.shape[1]
-    positions = 2 * size
+    positions = 4 * size
     total_x = total_z = None
     add_late = add_early = add_out = None
     for r in range(count):
-        part_x = part_z = 0.0
-        for place, rows in ((places[1], half), (1 - places[1], other)):
-            at = pl.multiple_of(place * size, size)
-            part_x += dot(both[r, :, pl.ds(at, size)], rows[r])
-            part_z += dot(both[r, :, pl.ds(at + lanes // 2, size)], rows[r])
+        for k, piece in enumerate(pieces):
+            at = pl.multiple_of((places[0] ^ k) * size, size)
+            buffer[r, pl.ds(at, size), :] = piece[r]
+        part_x = dot(both[r, :, :positions], buffer[r])
+        part_z = dot(both[r, :, lanes // 2 : lanes // 2 + positions], buffer[r])
         more_late = both[r, :, positions : lanes // 2].astype(f32)
         more_early = both[r, :, lanes // 2 + positions : lanes].astype(f32)
         more_out = both[r, :, lanes:].astype(f32)
@@ -903,10 +917,10 @@
             router[:, columns] = turned[row + ROWS : row + ROWS + router.shape[0]]
 
 
-def proj_grads(sizes, experts, places, both, half, other, after):
+def proj_grads(sizes, experts, places, both, pieces):
     devices, own, lanes = both.shape
-    width = half.shape[2]
-    size = half.shape[1] // 2
+    _, size, width = pieces[-1].shape
+    positions = 4 * size
     group = min(devices, GROUP)
     shapes = (
         (own, width),
@@ -931,17 +945,15 @@
         [
             pltpu.VMEM((padded(own), LANES), f32),
             pltpu.VMEM((padded(own), LANES), f32),
+            pltpu.VMEM((group, positions, width), bf16),
         ],
-        operands=(places, both, half, other, after),
+        operands=(places, both, *pieces),
         flops=8 * devices * size * width * own,
-        limit=40,
         grid=(devices // group,),
         in_specs=[
             pl.BlockSpec(memory_space=pltpu.SMEM),
             few,
-            pl.BlockSpec((group, size, width), lambda i: (i, 0, 0)),
-            pl.BlockSpec((group, size, width), lambda i: (i, 0, 0)),
-            pl.BlockSpec(memory_space=pl.ANY),
+            *([pl.BlockSpec((group, size, width), lambda i: (i, 0, 0))] * 4),
         ],
         out_specs=tuple(whole(shape) for shape in shapes),
     )
@@ -1010,37 +1022,58 @@
     )
     quarter = positions // hidden
     share = lax.all_gather(share, "expert")
-    mixed, gate_z, branch = mixer_out(sizes, scanned, activity, normed, weights, small)
-    low, other = hidden_halves(branch)
+    mixed, gate_z, kept, given = mixer_out(
+        sizes, places, scanned, activity, normed, weights, small
+    )
+    low, other = hidden_halves(kept, given)
     resid, normed_two, sent, sent_grad, own_half, logits = middle(
         places, tokens, low, other, vectors, codes, cotangent, experts
     )
     own_half = lax.all_gather(own_half, "expert")
-    out_part, back_part, packed = experts_local(
-        codes, logits, sent, sent_grad, expert_up, expert_down
-    )
-    packed = gather_small(packed, ("expert", "hidden"))
-    packed = packed.reshape((devices, hidden) + packed.shape[1:])
-    low, other = hidden_halves(back_part)
-    share = after(share, packed, other)
+    out_part, kept, given, packed = experts_local(
+        places, codes, logits, sent, sent_grad, expert_up, expert_down
+    )
+    packed = gather_small(packed, "expert")
+    gate_parts = lax.all_gather(packed[:, experts + 1 : experts + 2], "hidden")
+    low, other = hidden_halves(kept, given, gate_parts)
+    share = after(share, gate_parts, other)
     near = swap(share, "hidden", 1)
+    far = swap(share[:, quarter:], "hidden", 2)
     operands = (
-        seq_lengths, places, packed, low, other, vectors, resid, normed_two, cotangent, mixed,
+        seq_lengths, places, packed, gate_parts, low, other, vectors, resid, normed_two, cotangent, mixed,
         weights, scanned, activity, gate_z, step_pre, small, basis, states, rank_low,
     )
     gates, grad_resid, out_grad, grad_act, grad_z, grad_part, early = backward(
         sizes, operands, experts, devices
     )
+    own_half = after(own_half, gates)
     parts = lax.all_gather(grad_part, "hidden")
-    both, late = mixer_back(
+    kept, given, late = mixer_back(
         sizes,
         (
-            seq_lengths, parts, grad_act, activity, inner_x, small, weight_x, weights, grad_z,
-            tokens, early, out_part, out_grad.reshape(devices, own, width), near,
+            seq_lengths, places, parts, grad_act, activity, inner_x, small, weight_x, weights, grad_z,
+            tokens, early, out_part, out_grad.reshape(devices, own, width),
+            far, own_half,
         ),
     )
     late = lax.all_to_all(late, "expert", 0, 0, tiled=True)
-    low, other = hidden_halves(both)
+    halves = (own_half, swap(own_half, "hidden", 1))
+
+    last = swap(far, "hidden", 1)
+    group = min(devices, GROUP)
+    pieces = (packed, gates, halves, (share, far, near, last))
+    if group == devices:
+        up_grad, down_grad = expert_grads(places, *pieces, expert_up, expert_down, block)
+    else:
+
+        def add(total, some):
+            part = expert_grads(places, *some, expert_up, expert_down, block)
+            return (total[0] + part[0], total[1] + part[1]), None
+
+        grouped = jax.tree.map(lambda v: v.reshape((-1, group) + v.shape[1:]), pieces)
+        zero = jnp.zeros((experts, block, expert_up.shape[2]), f32)
+        (up_grad, down_grad), _ = lax.scan(add, (zero, zero), grouped)
+    low, other = hidden_halves(kept, given, up_grad)
     first = place % 2 == 0
     returned = jnp.where(first, low, other).astype(f32)
     grad_normed = jnp.where(first, other, low).astype(f32)
@@ -1054,29 +1087,9 @@
     gate_values = lax.dynamic_index_in_dim(gates, index, 0, keepdims=False)[0]
     layer_out = valid.astype(f32)[:, None] * (resid + gate_values[:, None] * returned)
 
-    all_codes = packed[:, 0, experts : experts + 1]
-    halves = (own_half, swap(own_half, "hidden", 1))
-
-    def by_piece(values):
-        values = values.reshape(devices, 2, 2, quarter)
-        values = jnp.where(place >= 2, values[:, ::-1], values)
-        values = jnp.where(place % 2 == 1, values[:, :, ::-1], values)
-        return values.transpose(0, 2, 1, 3).reshape(devices, 1, positions)
-
-    group = min(devices, GROUP)
-    pieces = (by_piece(all_codes), by_piece(gates), halves, (share, near))
-    if group == devices:
-        up_grad, down_grad = expert_grads(places, *pieces, expert_up, expert_down, block)
-    else:
-
-        def add(total, some):
-            part = expert_grads(places, *some, expert_up, expert_down, block)
-            return (total[0] + part[0], total[1] + part[1]), None
-
-        grouped = jax.tree.map(lambda v: v.reshape((-1, group) + v.shape[1:]), pieces)
-        zero = jnp.zeros((experts, block, expert_up.shape[2]), f32)
-        (up_grad, down_grad), _ = lax.scan(add, (zero, zero), grouped)
-    projected = proj_grads(sizes, experts, places, late, share, near, up_grad)
+    normed_far = swap(after(share[:, :quarter], kept), "hidden", 2)
+    normed_pieces = (share, near, normed_far, swap(normed_far, "hidden", 1))
+    projected = proj_grads(sizes, experts, places, late, normed_pieces)
     grad_x, grad_zw, state_grad, conv_grad, conv_bias_grad, gain_one_grad = projected[:6]
     decay_grad, step_proj_grad, step_bias_grad, skip_grad, gain_two_grad = projected[6:11]
     router_grad, out_grad = projected[11:]

time: 314 us -> 289 us (0.920)
  waiting for transfers between devices: 84.7 us -> 48.9 us
  blocking collectives: 22.6 us -> 43.7 us
  local copies, waits for them, and re-layouts: 22.2 us -> 14.4 us
  starting transfers between devices: 38.4 us -> 33 us
    all_to_all x2 -> x1, waiting for transfers between devices: 27 us -> 2.08 us  [gather_small(): return lax.all_to_all(copies, axis, 0, 0, tiled=True)]
    all_to_all x0 -> x1, blocking collectives: none -> 15.9 us  [gather_small(): return lax.all_to_all(copies, axis, 0, 0, tiled=True)]
    all_to_all x2 -> x1, starting transfers between devices: 13.3 us -> 4.88 us  [gather_small(): return lax.all_to_all(copies, axis, 0, 0, tiled=True)]
    ppermute x18 -> x22, waiting for transfers between devices: 37.7 us -> 30.7 us  [swap(): return lax.ppermute(values, axis, [(i, i ^ bits) for i in range(size)])]
    unnamed x49 -> x39, local copies, waits for them, and re-layouts: 11.5 us -> 4.76 us
    all_gather x0 -> x1, blocking collectives: none -> 5.82 us  [local(): gate_parts = lax.all_gather(packed[:, experts + 1:experts + 2], 'hidden')]
    all_gather x1, waiting for transfers between devices: 4.77 us -> 0.02 us  [local(): own_half = lax.all_gather(own_half, 'expert')]
    all_to_all x1, waiting for transfers between devices: 5.01 us -> 9.31 us  [local(): late = lax.all_to_all(late, 'expert', 0, 0, tiled=True)]
  transfers between devices with their start and end apart: 24 -> 27, of which waited for: 14 -> 11; matrix products, arithmetic and copies ran while one was open for 6% -> 8% of each run, Pallas kernels for 37% -> 40%
where the time goes in v4:
time: 289 us; the launch traced here: 288 us
  Pallas kernels  120 us (42%)
  waiting for transfers between devices  48.9 us (17%)
  blocking collectives  43.7 us (15%)
  starting transfers between devices  33 us (11%)
  between operations  15.5 us (5%)
  local copies, waits for them, and re-layouts  14.4 us (5%)
  other arithmetic  13.1 us (5%)
    pallas_call x9, Pallas kernels, call(): pl.pallas_call(body, out_shape=out_shape, scratch_shapes=list(scratch), c...  120 us
    ppermute x22, waiting for transfers between devices, swap(): return lax.ppermute(values, axis, [(i, i ^ bits) for i in range(size)])  30.7 us
    ppermute x22, starting transfers between devices, swap(): return lax.ppermute(values, axis, [(i, i ^ bits) for i in range(size)])  23.3 us
    all_to_all x1, blocking collectives, gather_small(): return lax.all_to_all(copies, axis, 0, 0, tiled=True)  15.9 us
    all_to_all x1, waiting for transfers between devices, local(): late = lax.all_to_all(late, 'expert', 0, 0, tiled=True)  9.31 us
    all_gather x1, blocking collectives, local(): parts = lax.all_gather(grad_part, 'hidden')  8.5 us
    all_gather x1, blocking collectives, local(): parts = lax.all_gather(part, 'hidden')  8.24 us
    all_gather x1, waiting for transfers between devices, local(): weights = lax.all_gather(later, 'expert').reshape(channels, 2 * width)  6.72 us
  transfers between devices with their start and end apart: 27, of which 11 were waited for; matrix products, arithmetic and copies ran while one was open for 8% of the time, Pallas kernels for 40%

profile of v4, /device:TPU:0, one launch (start us, length us, event | category | flops | bytes accessed | tf_op | source)
XLA Modules:
  0.0 288.4 jit_solution(15323930544159186677)
XLA Ops:
  7.2 1.7 pad_maximum_fusion
  9.0 3.0 %collective-permute-start = (bf16[72,1152]{1,0:T(8,128)(2,1)}, bf16[72,1152]{1,0:T(8,128)(2,1)S(1)}, u32[]{:S(2)}, u32[]{:S(2)}) collective-permute-start(bf16[72,1152]{1,0:T(8,128)(2,1)} %bitcast.56), channel_id=1, source_target_pairs={{0,4},{4,0},{8,12},{12,8},{16,20},{20,16},{24,28},{28,24},{1,5},{5... | collective-permute-start | bytes 497672 | tf_op jit(solution)/shard_map/ppermute | solution.py:71
  13.6 3.0 %collective-permute-start.3 = (bf16[72,1152]{1,0:T(8,128)(2,1)}, bf16[72,1152]{1,0:T(8,128)(2,1)S(1)}, u32[]{:S(2)}, u32[]{:S(2)}) collective-permute-start(bf16[72,1152]{1,0:T(8,128)(2,1)} %bitcast.59), channel_id=1, source_target_pairs={{0,16},{4,20},{8,24},{12,28},{16,0},{20,4},{24,8},{28,12},{1,17},{... | collective-permute-start | bytes 497672 | tf_op jit(solution)/shard_map/ppermute | solution.py:71
  23.5 4.9 %all-to-all-start = ((bf16[8,232,72]{1,2,0:T(8,128)(2,1)}), bf16[8,232,72]{1,2,0:T(8,128)(2,1)S(1)}, u32[]{:S(2)}, u32[]{:S(2)}) async-start(bf16[8,232,72]{1,2,0:T(8,128)(2,1)} %broadcast_in_dim.76), calls=%async_computation | async-start | bytes 589824 | tf_op jit(solution)/shard_map/all_to_all | solution.py:89
  29.3 3.8 %collective-permute-start.5 = (bf16[72,1152]{1,0:T(8,128)(2,1)S(1)}, bf16[72,1152]{1,0:T(8,128)(2,1)S(1)}, u32[]{:S(2)}, u32[]{:S(2)}) collective-permute-start(bf16[72,1152]{1,0:T(8,128)(2,1)S(1)} %bitcast.62), channel_id=1, source_target_pairs={{0,24},{4,28},{8,16},{12,20},{16,8},{20,12},{24,0},{28,4},{1,25},{... | collective-permute-start | bytes 497672 | tf_op jit(solution)/shard_map/ppermute | solution.py:71
  34.7 8.8 %collective-permute-done.4 = bf16[72,1152]{1,0:T(8,128)(2,1)S(1)} collective-permute-done((bf16[72,1152]{1,0:T(8,128)(2,1)}, bf16[72,1152]{1,0:T(8,128)(2,1)S(1)}, u32[]{:S(2)}, u32[]{:S(2)}) %collective-permute-start.4) | collective-permute-done | bytes 165920 | tf_op jit(solution)/shard_map/ppermute | solution.py:71
  43.5 6.3 %collective-permute-done.5 = bf16[72,1152]{1,0:T(8,128)(2,1)S(1)} collective-permute-done((bf16[72,1152]{1,0:T(8,128)(2,1)S(1)}, bf16[72,1152]{1,0:T(8,128)(2,1)S(1)}, u32[]{:S(2)}, u32[]{:S(2)}) %collective-permute-start.5) | collective-permute-done | bytes 165920 | tf_op jit(solution)/shard_map/ppermute | solution.py:71
  49.8 2.0 collective-permute-done.6
  51.9 2.1 all-to-all-done
  54.9 4.5 %mixer_in.1 = (bf16[256,1152]{1,0:T(8,128)(2,1)}, f32[256,576]{1,0:T(8,128)}, bf16[256,576]{1,0:T(8,128)(2,1)}, f32[256,104]{1,0:T(8,128)}, f32[200,576]{1,0:T(8...) custom-call(s32[1,2]{1,0:T(1,128)} %lengths.7, s32[3]{0:T(128)} %pad_add_fusion.places, bf16[256,1152]{1,0:T(8,128)(2,1)} %tokens.5, ...), custom_call_target="tpu_custom_call" | custom-call | tf_op jit(solution)/shard_map/mixer_in/pallas_call | solution.py:47
  59.5 8.2 %all-gather = f32[1024,104]{1,0:T(8,128)} all-gather(f32[256,104]{1,0:T(8,128)} %get-tuple-element.71), channel_id=2, replica_groups=mesh['expert'=8,'hidden'=4] {'hidden'}, dimensions={0}, use_global_device_ids=true | all-gather | bytes 532480 | tf_op jit(solution)/shard_map/all_gather | solution.py:1019
  67.8 14.4 %scan_forward.1 = (f32[256,576]{1,0:T(8,128)}, f32[256,16,640]{2,1,0:T(8,128)}, f32[256,576]{1,0:T(8,128)}, f32[128,256]{1,0:T(8,128)}, bf16[256,72]{1,0:T(8,128)(2,1)}) custom-call(s32[1,2]{1,0:T(1,128)} %lengths.7, f32[4,256,104]{2,1,0:T(8,128)} %bitcast.51, bf16[256,576]{1,0:T(8,128)(2,1)} %get-tuple-element.72.activity, f32[200,576]{1,0:T(8,128)} %get-tuple-element.73.small), custom_call_target="tpu_custom_call" | custom-call | tf_op jit(solution)/shard_map/scan_forward/pallas_call | solution.py:47
  82.1 6.7 %all-gather.12.cloned.1.call-done.weight_z.weight_out = bf16[576,2304]{1,0:T(8,128)(2,1)} async-done(((bf16[72,2304]{1,0:T(8,128)(2,1)}), bf16[576,2304]{1,0:T(8,128)(2,1)}) %all-gather.12.cloned.1.call-update) | async-done | bytes 2654224 | tf_op jit(solution)/shard_map/all_gather | solution.py:1001
  88.9 4.5 %mixer_out.1 = (bf16[256,576]{1,0:T(8,128)(2,1)}, f32[256,576]{1,0:T(8,128)}, bf16[128,1152]{1,0:T(8,128)(2,1)}, bf16[128,1152]{1,0:T(8,128)(2,1)}) custom-call(s32[3]{0:T(128)} %pad_add_fusion.places, f32[256,576]{1,0:T(8,128)} %get-tuple-element.74.out, bf16[256,576]{1,0:T(8,128)(2,1)} %get-tuple-element.72.activity, ...), custom_call_target="tpu_custom_call" | custom-call | tf_op jit(solution)/shard_map/mixer_out/pallas_call | solution.py:47
  93.5 1.8 collective-permute-done.7
  97.9 7.5 %collective-permute-done.8 = bf16[128,1152]{1,0:T(8,128)(2,1)S(1)} collective-permute-done((bf16[128,1152]{1,0:T(8,128)(2,1)S(1)}, bf16[128,1152]{1,0:T(8,128)(2,1)S(1)}, u32[]{:S(2)}, u32[]{:S(2)}) %collective-permute-start.8) | collective-permute-done | bytes 294944 | tf_op jit(solution)/shard_map/ppermute | solution.py:71
  108.8 3.8 %middle.1 = (f32[256,1152]{1,0:T(8,128)}, bf16[256,1152]{1,0:T(8,128)(2,1)}, bf16[384,1152]{1,0:T(8,128)(2,1)}, bf16[384,1152]{1,0:T(8,128)(2,1)}, bf16[128,1152]{1,0:T(8,128)(2,1)}, /*index=5*/f32[16,256]{1,0:T(8,128)}) custom-call(s32[3]{0:T(128)} %pad_add_fusion.places, bf16[256,1152]{1,0:T(8,128)(2,1)} %tokens.5, bf16[128,1152]{1,0:T(8,128)(2,1)} %copy-done.9, ...), custom_call_target="tpu_custom_call" | custom-call | tf_op jit(solution)/shard_map/middle/pallas_call | solution.py:47
  112.6 18.6 %experts_local.1 = (bf16[256,1152]{1,0:T(8,128)(2,1)}, bf16[128,1152]{1,0:T(8,128)(2,1)}, bf16[128,1152]{1,0:T(8,128)(2,1)}, f32[16,256]{1,0:T(8,128)}) custom-call(s32[3]{0:T(128)} %pad_add_fusion.places, f32[1,256]{1,0:T(1,128)} %compare_select_fusion.codes, f32[16,256]{1,0:T(8,128)} %get-tuple-element.81.logits, ...), custom_call_target="tpu_custom_call" | custom-call | tf_op jit(solution)/shard_map/experts_local/pallas_call | solution.py:47
  134.2 1.7 collective-permute-start.11
  136.6 15.9 %all_to_all.15.packed.codes = f32[8,16,256]{2,1,0:T(8,128)S(1)} all-to-all(f32[8,16,256]{2,1,0:T(8,128)S(1)} %broadcast_in_dim.78), channel_id=1, replica_groups=mesh['expert'=8,'hidden'=4] {'expert'}, dimensions={0} | all-to-all | bytes 262144 | tf_op jit(solution)/shard_map/all_to_all | solution.py:89
  152.5 5.8 %all-gather.2 = f32[32,1,256]{2,1,0:T(1,128)} all-gather(f32[8,1,256]{2,1,0:T(1,128)S(1)} %slice.34), channel_id=4, replica_groups=mesh['expert'=8,'hidden'=4] {'hidden'}, dimensions={0}, use_global_device_ids=true | all-gather | bytes 40960 | tf_op jit(solution)/shard_map/all_gather | solution.py:1037
  162.5 3.0 %fusion.12 = (bf16[8,64,1152]{2,1,0:T(8,128)(2,1)}, bf16[8,64,1152]{2,1,0:T(8,128)(2,1)S(1)}) fusion(bf16[8,128,1152]{2,1,0:T(8,128)(2,1)} %after.6.refs_2_.refs_0_), kind=kLoop, calls=%fused_computation.41 | loop fusion | bytes 4718592 | tf_op jit(solution)/shard_map/slice | solution.py:1090
  166.8 29.0 %backward.1 = (f32[8,1,256]{2,1,0:T(1,128)}, f32[256,1152]{1,0:T(8,128)}, bf16[576,1152]{1,0:T(8,128)(2,1)}, f32[256,576]{1,0:T(8,128)}, bf16[256,576]{1,0:T(8,1...) custom-call(s32[1,2]{1,0:T(1,128)} %lengths.7, s32[3]{0:T(128)} %pad_add_fusion.places, ...), custom_call_target="tpu_custom_call" | custom-call | tf_op jit(solution)/shard_map/backward/pallas_call | solution.py:47
  196.5 8.5 %all-gather.3 = f32[1024,128]{1,0:T(8,128)} all-gather(f32[256,128]{1,0:T(8,128)} %get-tuple-element.95), channel_id=5, replica_groups=mesh['expert'=8,'hidden'=4] {'hidden'}, dimensions={0}, use_global_device_ids=true | all-gather | bytes 655360 | tf_op jit(solution)/shard_map/all_gather | solution.py:1050
  205.0 8.1 %mixer_back.1 = (bf16[256,1152]{1,0:T(8,128)(2,1)}, bf16[256,1152]{1,0:T(8,128)(2,1)}, bf16[8,72,1920]{2,1,0:T(8,128)(2,1)}) custom-call(s32[1,2]{1,0:T(1,128)} %lengths.7, s32[3]{0:T(128)} %pad_add_fusion.places, f32[4,256,128]{2,1,0:T(8,128)} %bitcast.50, f32[256,576]{1,0:T(8,128)} %get-tuple-element.96.grad_act, ...), custom_call_target="tpu_custom_call" | custom-call | tf_op jit(solution)/shard_map/mixer_back/pallas_call | solution.py:47
  214.9 4.7 %all-to-all-start.2 = ((bf16[8,72,1920]{2,1,0:T(8,128)(2,1)}), bf16[8,72,1920]{2,1,0:T(8,128)(2,1)}, u32[]{:S(2)}, u32[]{:S(2)}) async-start(bf16[8,72,1920]{2,1,0:T(8,128)(2,1)} %get-tuple-element.108), calls=%async_computation.2 | async-start | bytes 4423680 | tf_op jit(solution)/shard_map/all_to_all | solution.py:1059
  221.6 31.2 %expert_grads.1 = (f32[8,144,768]{2,1,0:T(8,128)}, f32[8,144,768]{2,1,0:T(8,128)}) custom-call(s32[3]{0:T(128)} %pad_add_fusion.places, f32[8,16,256]{2,1,0:T(8,128)} %copy-done.12, f32[8,1,256]{2,1,0:T(1,128)} %get-tuple-element.94.refs_1_.gates, bf16[8,128,1152]{2,1,0:T(8,128)(2,1)} %after.7._rows.refs_0_, ...), custom_call_target="tpu_custom_call" | custom-call | flops 32614907904 | tf_op jit(solution)/shard_map/expert_grads/pallas_call | solution.py:47
  252.8 1.6 collective-permute-done.15.refs_0_
  259.3 1.8 fusion.5
  261.1 9.3 %all-to-all-done.2.both = bf16[8,72,1920]{2,1,0:T(8,128)(2,1)} async-done(((bf16[8,72,1920]{2,1,0:T(8,128)(2,1)}), bf16[8,72,1920]{2,1,0:T(8,128)(2,1)}, u32[]{:S(2)}, u32[]{:S(2)}) %all-to-all-start.2) | async-done | bytes 2211872 | tf_op jit(solution)/shard_map/all_to_all | solution.py:1059
  270.4 5.6 %proj_grads.1 = (f32[72,1152]{1,0:T(8,128)}, f32[72,1152]{1,0:T(8,128)}, f32[72,104]{1,0:T(8,128)}, f32[4,72]{1,0:T(4,128)}, f32[1,72]{1,0:T(1,128)}, /*index=5*...) custom-call(s32[3]{0:T(128)} %pad_add_fusion.places, ...), custom_call_target="tpu_custom_call" | custom-call | tf_op jit(solution)/shard_map/proj_grads/pallas_call | solution.py:47
  276.0 5.3 %all-gather.7 = f32[4,1,144]{2,1,0:T(1,128)S(1)} all-gather(f32[1,1,144]{2,1,0:T(1,128)} %bitcast.68), channel_id=8, replica_groups=mesh['expert'=8,'hidden'=4] {'hidden'}, dimensions={0}, use_global_device_ids=true | all-gather | bytes 2880 | tf_op jit(solution)/shard_map/all_gather | solution.py:1096
  (125 shorter events, 35.6 us)
Async XLA Ops:
  7.2 15.5 %copy-start.15 = (bf16[72,104]{1,0:T(8,128)(2,1)S(1)}, bf16[72,104]{1,0:T(8,128)(2,1)}, u32[]{:S(2)}) copy-start(bf16[72,104]{1,0:T(8,128)(2,1)} %param.28) | copy-start | bytes 44932
  7.2 81.7 %all-gather.12.cloned.1.call-start = ((), (), s32[]{:S(2)}) async-start(), calls=%async_computation.3 | async-start | bytes 2985984 | tf_op jit(solution)/shard_map/all_gather | solution.py:1001
  9.0 20.3 %collective-permute-start = (bf16[72,1152]{1,0:T(8,128)(2,1)}, bf16[72,1152]{1,0:T(8,128)(2,1)S(1)}, u32[]{:S(2)}, u32[]{:S(2)}) collective-permute-start(bf16[72,1152]{1,0:T(8,128)(2,1)} %bitcast.56), channel_id=1, source_target_pairs={{0,4},{4,0},{8,12},{12,8},{16,20},{20,16},{24,28},{28,24},{1,5},{5... | collective-permute-start | bytes 497672 | tf_op jit(solution)/shard_map/ppermute | solution.py:71
  12.0 21.1 %collective-permute-start.1 = (bf16[72,1152]{1,0:T(8,128)(2,1)}, bf16[72,1152]{1,0:T(8,128)(2,1)S(1)}, u32[]{:S(2)}, u32[]{:S(2)}) collective-permute-start(bf16[72,1152]{1,0:T(8,128)(2,1)} %bitcast.57), channel_id=1, source_target_pairs={{0,8},{4,12},{8,0},{12,4},{16,24},{20,28},{24,16},{28,20},{1,9},{5... | collective-permute-start | bytes 497672 | tf_op jit(solution)/shard_map/ppermute | solution.py:71
  13.6 21.0 %collective-permute-start.2 = (bf16[72,1152]{1,0:T(8,128)(2,1)}, bf16[72,1152]{1,0:T(8,128)(2,1)S(1)}, u32[]{:S(2)}, u32[]{:S(2)}) collective-permute-start(bf16[72,1152]{1,0:T(8,128)(2,1)} %bitcast.58), channel_id=1, source_target_pairs={{0,12},{4,8},{8,4},{12,0},{16,28},{20,24},{24,20},{28,16},{1,13},{... | collective-permute-start | bytes 497672 | tf_op jit(solution)/shard_map/ppermute | solution.py:71
  13.6 21.1 %collective-permute-start.3 = (bf16[72,1152]{1,0:T(8,128)(2,1)}, bf16[72,1152]{1,0:T(8,128)(2,1)S(1)}, u32[]{:S(2)}, u32[]{:S(2)}) collective-permute-start(bf16[72,1152]{1,0:T(8,128)(2,1)} %bitcast.59), channel_id=1, source_target_pairs={{0,16},{4,20},{8,24},{12,28},{16,0},{20,4},{24,8},{28,12},{1,17},{... | collective-permute-start | bytes 497672 | tf_op jit(solution)/shard_map/ppermute | solution.py:71
  16.6 26.9 %collective-permute-start.4 = (bf16[72,1152]{1,0:T(8,128)(2,1)}, bf16[72,1152]{1,0:T(8,128)(2,1)S(1)}, u32[]{:S(2)}, u32[]{:S(2)}) collective-permute-start(bf16[72,1152]{1,0:T(8,128)(2,1)} %bitcast.60), channel_id=1, source_target_pairs={{0,20},{4,16},{8,28},{12,24},{16,4},{20,0},{24,12},{28,8},{1,21},{... | collective-permute-start | bytes 497672 | tf_op jit(solution)/shard_map/ppermute | solution.py:71
  22.7 5.9 %copy-start.14 = (bf16[1152,72]{0,1:T(8,128)(2,1)S(1)}, bf16[1152,72]{0,1:T(8,128)(2,1)}, u32[]{:S(2)}) copy-start(bf16[1152,72]{0,1:T(8,128)(2,1)} %param.24) | copy-start | bytes 497668
  23.5 30.4 %all-to-all-start = ((bf16[8,232,72]{1,2,0:T(8,128)(2,1)}), bf16[8,232,72]{1,2,0:T(8,128)(2,1)S(1)}, u32[]{:S(2)}, u32[]{:S(2)}) async-start(bf16[8,232,72]{1,2,0:T(8,128)(2,1)} %broadcast_in_dim.76), calls=%async_computation | async-start | bytes 589824 | tf_op jit(solution)/shard_map/all_to_all | solution.py:89
  28.4 132.0 %all-gather.14.cloned.1.call-start = ((), (), s32[]{:S(2)}) async-start(), calls=%async_computation.4 | async-start | bytes 2654208 | tf_op jit(solution)/shard_map/all_gather | solution.py:1024
  29.3 20.5 %collective-permute-start.5 = (bf16[72,1152]{1,0:T(8,128)(2,1)S(1)}, bf16[72,1152]{1,0:T(8,128)(2,1)S(1)}, u32[]{:S(2)}, u32[]{:S(2)}) collective-permute-start(bf16[72,1152]{1,0:T(8,128)(2,1)S(1)} %bitcast.62), channel_id=1, source_target_pairs={{0,24},{4,28},{8,16},{12,20},{16,8},{20,12},{24,0},{28,4},{1,25},{... | collective-permute-start | bytes 497672 | tf_op jit(solution)/shard_map/ppermute | solution.py:71
  33.1 18.8 %collective-permute-start.6 = (bf16[72,1152]{1,0:T(8,128)(2,1)S(1)}, bf16[72,1152]{1,0:T(8,128)(2,1)S(1)}, u32[]{:S(2)}, u32[]{:S(2)}) collective-permute-start(bf16[72,1152]{1,0:T(8,128)(2,1)S(1)} %bitcast.63), channel_id=1, source_target_pairs={{0,28},{4,24},{8,20},{12,16},{16,12},{20,8},{24,4},{28,0},{1,29},{... | collective-permute-start | bytes 497672 | tf_op jit(solution)/shard_map/ppermute | solution.py:71
  59.5 136.4 %all-gather.16.cloned.1.call-start = ((), (), s32[]{:S(2)}) async-start(), calls=%async_computation.5 | async-start | bytes 2654208 | tf_op jit(solution)/shard_map/all_gather | solution.py:1032
  93.4 12.2 %copy-start.16 = (s32[1,2]{1,0:T(1,128)S(1)}, s32[1,2]{1,0:T(1,128)}, u32[]{:S(2)}) copy-start(s32[1,2]{1,0:T(1,128)} %lengths.7) | copy-start | bytes 28
  93.4 14.1 %copy-start.17 = (s32[256,1]{0,1:T(1,128)S(1)}, s32[256,1]{0,1:T(1,128)}, u32[]{:S(2)}) copy-start(s32[256,1]{0,1:T(1,128)} %param.22) | copy-start | bytes 3076
  93.4 1.9 collective-permute-start.7
  96.3 9.1 %collective-permute-start.8 = (bf16[128,1152]{1,0:T(8,128)(2,1)S(1)}, bf16[128,1152]{1,0:T(8,128)(2,1)S(1)}, u32[]{:S(2)}, u32[]{:S(2)}) collective-permute-start(bf16[128,1152]{1,0:T(8,128)(2,1)S(1)} %add_convert_fusion.5), channel_id=1, source_target_pairs={{0,2},{1,3},{2,0},{3,1},{4,6},{5,7},{6,4},{7,5},{8,10},{9,11},{10,... | collective-permute-start | bytes 884744 | tf_op jit(solution)/shard_map/ppermute | solution.py:71
  105.5 2.6 collective-permute-start.9
  131.3 1.8 collective-permute-start.10
  134.2 24.1 %collective-permute-start.11 = (bf16[128,1152]{1,0:T(8,128)(2,1)S(1)}, bf16[128,1152]{1,0:T(8,128)(2,1)S(1)}, u32[]{:S(2)}, u32[]{:S(2)}) collective-permute-start(bf16[128,1152]{1,0:T(8,128)(2,1)S(1)} %add_convert_fusion.3), channel_id=1, source_target_pairs={{0,2},{1,3},{2,0},{3,1},{4,6},{5,7},{6,4},{7,5},{8,10},{9,11},{10,... | collective-permute-start | bytes 884744 | tf_op jit(solution)/shard_map/ppermute | solution.py:71
  160.1 1.6 collective-permute-start.12
  165.5 31.0 %collective-permute-start.13 = (bf16[8,64,1152]{2,1,0:T(8,128)(2,1)S(1)}, bf16[8,64,1152]{2,1,0:T(8,128)(2,1)}, u32[]{:S(2)}, u32[]{:S(2)}) collective-permute-start(bf16[8,64,1152]{2,1,0:T(8,128)(2,1)S(1)} %get-tuple-element.124), channel_id=1, source_target_pairs={{0,2},{1,3},{2,0},{3,1},{4,6},{5,7},{6,4},{7,5},{8,10},{9,11},{10,... | collective-permute-start | bytes 3538952 | tf_op jit(solution)/shard_map/ppermute | solution.py:71
  166.8 54.8 %collective-permute-start.17 = (bf16[8,128,1152]{2,1,0:T(8,128)(2,1)S(1)}, bf16[8,128,1152]{2,1,0:T(8,128)(2,1)}, u32[]{:S(2)}, u32[]{:S(2)}) collective-permute-start(bf16[8,128,1152]{2,1,0:T(8,128)(2,1)S(1)} %copy-done), channel_id=1, source_target_pairs={{0,1},{1,0},{2,3},{3,2},{4,5},{5,4},{6,7},{7,6},{8,9},{9,8},{10,11... | collective-permute-start | bytes 7077896 | tf_op jit(solution)/shard_map/ppermute | solution.py:71
  195.9 25.7 %collective-permute-start.16 = (bf16[8,128,1152]{2,1,0:T(8,128)(2,1)}, bf16[8,128,1152]{2,1,0:T(8,128)(2,1)}, u32[]{:S(2)}, u32[]{:S(2)}) collective-permute-start(bf16[8,128,1152]{2,1,0:T(8,128)(2,1)} %after.7._rows.refs_0_), channel_id=1, source_target_pairs={{0,1},{1,0},{2,3},{3,2},{4,5},{5,4},{6,7},{7,6},{8,9},{9,8},{10,11... | collective-permute-start | bytes 7077896 | tf_op jit(solution)/shard_map/ppermute | solution.py:71
  196.4 25.1 %collective-permute-start.18 = (bf16[8,64,1152]{2,1,0:T(8,128)(2,1)}, bf16[8,64,1152]{2,1,0:T(8,128)(2,1)}, u32[]{:S(2)}, u32[]{:S(2)}) collective-permute-start(bf16[8,64,1152]{2,1,0:T(8,128)(2,1)} %collective-permute-done.13._grads.refs_3_), channel_id=1, source_target_pairs={{0,1},{1,0},{2,3},{3,2},{4,5},{5,4},{6,7},{7,6},{8,9},{9,8},{10,11... | collective-permute-start | bytes 3538952 | tf_op jit(solution)/shard_map/ppermute | solution.py:71
  213.2 6.4 %collective-permute-start.14 = (bf16[256,1152]{1,0:T(8,128)(2,1)}, bf16[256,1152]{1,0:T(8,128)(2,1)}, u32[]{:S(2)}, u32[]{:S(2)}) collective-permute-start(bf16[256,1152]{1,0:T(8,128)(2,1)} %get-tuple-element.105), channel_id=1, source_target_pairs={{0,1},{1,0},{2,3},{3,2},{4,5},{5,4},{6,7},{7,6},{8,9},{9,8},{10,11... | collective-permute-start | bytes 1769480 | tf_op jit(solution)/shard_map/ppermute | solution.py:71
  213.5 44.2 %collective-permute-start.20 = (bf16[8,64,1152]{2,1,0:T(8,128)(2,1)}, bf16[8,64,1152]{2,1,0:T(8,128)(2,1)}, u32[]{:S(2)}, u32[]{:S(2)}) collective-permute-start(bf16[8,64,1152]{2,1,0:T(8,128)(2,1)} %after.9), channel_id=1, source_target_pairs={{0,2},{1,3},{2,0},{3,1},{4,6},{5,7},{6,4},{7,5},{8,10},{9,11},{10,... | collective-permute-start | bytes 3538952 | tf_op jit(solution)/shard_map/ppermute | solution.py:71
  214.9 55.5 %all-to-all-start.2 = ((bf16[8,72,1920]{2,1,0:T(8,128)(2,1)}), bf16[8,72,1920]{2,1,0:T(8,128)(2,1)}, u32[]{:S(2)}, u32[]{:S(2)}) async-start(bf16[8,72,1920]{2,1,0:T(8,128)(2,1)} %get-tuple-element.108), calls=%async_computation.2 | async-start | bytes 4423680 | tf_op jit(solution)/shard_map/all_to_all | solution.py:1059
  220.8 33.6 %collective-permute-start.15 = (bf16[256,1152]{1,0:T(8,128)(2,1)S(1)}, bf16[256,1152]{1,0:T(8,128)(2,1)S(1)}, u32[]{:S(2)}, u32[]{:S(2)}) collective-permute-start(bf16[256,1152]{1,0:T(8,128)(2,1)S(1)} %add_convert_fusion.1), channel_id=1, source_target_pairs={{0,2},{1,3},{2,0},{3,1},{4,6},{5,7},{6,4},{7,5},{8,10},{9,11},{10,... | collective-permute-start | bytes 1769480 | tf_op jit(solution)/shard_map/ppermute | solution.py:71
  256.5 2.3 collective-permute-start.19
  257.8 3.3 %collective-permute-start.21 = (bf16[8,64,1152]{2,1,0:T(8,128)(2,1)}, bf16[8,64,1152]{2,1,0:T(8,128)(2,1)S(1)}, u32[]{:S(2)}, u32[]{:S(2)}) collective-permute-start(bf16[8,64,1152]{2,1,0:T(8,128)(2,1)} %collective-permute-done.20.refs_2_), channel_id=1, source_target_pairs={{0,1},{1,0},{2,3},{3,2},{4,5},{5,4},{6,7},{7,6},{8,9},{9,8},{10,11... | collective-permute-start | bytes 3538952 | tf_op jit(solution)/shard_map/ppermute | solution.py:71
  261.1 9.3 %copy-start.6 = (bf16[8,64,1152]{2,1,0:T(8,128)(2,1)}, bf16[8,64,1152]{2,1,0:T(8,128)(2,1)S(1)}, u32[]{:S(2)}) copy-start(bf16[8,64,1152]{2,1,0:T(8,128)(2,1)S(1)} %collective-permute-done.21.refs_3_) | copy-start | bytes 3538948
  (13 other events, 32.1 us)
Sparse Core Ops, SparseCore 0:
  10.8 78.0 all-gather.11
  91.6 50.1 all-gather.13
  144.0 50.5 all-gather.15

commit v5 on v4

--- a/solution.py
+++ b/solution.py
@@ -235,7 +235,7 @@
     result, _ = causal_conv(values, shifted, kernel, offset, lengths)
     low = (result * sigmoid(result)).astype(bf16)
     activity[...] = low
-    part[...] = dot(low, small[sizes.proj : sizes.conv, :].astype(bf16), 1, 1)
+    part[...] = dot(low, small[sizes.proj : sizes.conv, :].astype(bf16), 1, 1).astype(bf16)
 
 
 def mixer_in(sizes, lengths, places, tokens, cotangent, weight, pack):
@@ -248,7 +248,7 @@
             low_of(positions, width),
             shape_of(positions, channels),
             low_of(positions, channels),
-            shape_of(positions, sizes.state),
+            low_of(positions, sizes.state),
             shape_of(sizes.rows, channels),
             shape_of(sizes.vectors, width),
             low_of(positions // 2, width),
@@ -267,7 +267,7 @@
     width = far_steps.shape[1]
     positions, channels = activity.shape
     entries, rank = sizes.entries, sizes.rank
-    projected = jnp.sum(parts[...], axis=0)
+    projected = jnp.sum(parts[...].astype(f32), axis=0)
     put(wide, projected)
     basis[...] = wide[...].T
     low = projected[:, :rank].astype(bf16)
@@ -721,8 +721,10 @@
     grad_low = grad_step.astype(bf16)
     sums[entries + rank : entries + rank + 1, :channels] = jnp.sum(grad_step, axis=0, keepdims=True)
     sums[entries : entries + rank, :channels] = dot(rank_low[...], grad_low, 0, 0)
-    grad_part[:, :rank] = dot(grad_low, small[sizes.step : sizes.proj, :].astype(bf16), 1, 1)
-    grad_part[:, rank : rank + 2 * entries] = square[...].T[:, : 2 * entries]
+    grad_part[:, :rank] = dot(
+        grad_low, small[sizes.step : sizes.proj, :].astype(bf16), 1, 1
+    ).astype(bf16)
+    grad_part[:, rank : rank + 2 * entries] = square[...].T[:, : 2 * entries].astype(bf16)
     turned = sums[...].T
     spread = shares[...].T
     side = padded(sizes.vectors) - 2 * sizes.vectors
@@ -749,7 +751,7 @@
             low_of(channels, width),
             shape_of(positions, channels),
             low_of(positions, channels),
-            shape_of(positions, padded(sizes.state)),
+            low_of(positions, padded(sizes.state)),
             low_of(devices, channels // devices, positions + LANES),
         ),
         [
@@ -783,7 +785,7 @@
     late[:, :, lanes : 2 * lanes] = early[...]
     late[:, :, 2 * lanes :] = out_grad[...]
     taps = sizes.taps
-    low = jnp.sum(parts[...], axis=0)[:, : sizes.state].astype(bf16)
+    low = jnp.sum(parts[...].astype(f32), axis=0)[:, : sizes.state].astype(bf16)
     state_grad = dot(activity[...], low, 0, 0)
     grad = grad_act[...] + dot(low, small[sizes.proj : sizes.conv, :].astype(bf16))
     kernel = small[sizes.conv : sizes.conv + taps, :]

time: 289 us -> 287 us (level)
  no operation moved by 1% of the time
where the time goes in v5:
time: 287 us; the launch traced here: 286 us
  Pallas kernels  120 us (42%)
  waiting for transfers between devices  49.2 us (17%)
  blocking collectives  41.2 us (14%)
  starting transfers between devices  32.9 us (11%)
  between operations  15.5 us (5%)
  local copies, waits for them, and re-layouts  14.4 us (5%)
  other arithmetic  13.1 us (5%)
    pallas_call x9, Pallas kernels, call(): pl.pallas_call(body, out_shape=out_shape, scratch_shapes=list(scratch), c...  120 us
    ppermute x22, waiting for transfers between devices, swap(): return lax.ppermute(values, axis, [(i, i ^ bits) for i in range(size)])  30.6 us
    ppermute x22, starting transfers between devices, swap(): return lax.ppermute(values, axis, [(i, i ^ bits) for i in range(size)])  23.2 us
    all_to_all x1, blocking collectives, gather_small(): return lax.all_to_all(copies, axis, 0, 0, tiled=True)  15.1 us
    all_to_all x1, waiting for transfers between devices, local(): late = lax.all_to_all(late, 'expert', 0, 0, tiled=True)  8.91 us
    all_gather x1, blocking collectives, local(): parts = lax.all_gather(grad_part, 'hidden')  7.58 us
    all_gather x1, waiting for transfers between devices, local(): weights = lax.all_gather(later, 'expert').reshape(channels, 2 * width)  7.49 us
    all_gather x1, blocking collectives, local(): parts = lax.all_gather(part, 'hidden')  7.4 us
  transfers between devices with their start and end apart: 27, of which 11 were waited for; matrix products, arithmetic and copies ran while one was open for 8% of the time, Pallas kernels for 40%

profile of v5, /device:TPU:0, one launch (start us, length us, event | category | flops | bytes accessed | tf_op | source)
XLA Modules:
  0.0 286.1 jit_solution(14929886662577057048)
XLA Ops:
  9.0 3.0 %collective-permute-start = (bf16[72,1152]{1,0:T(8,128)(2,1)}, bf16[72,1152]{1,0:T(8,128)(2,1)S(1)}, u32[]{:S(2)}, u32[]{:S(2)}) collective-permute-start(bf16[72,1152]{1,0:T(8,128)(2,1)} %bitcast.56), channel_id=1, source_target_pairs={{0,4},{4,0},{8,12},{12,8},{16,20},{20,16},{24,28},{28,24},{1,5},{5... | collective-permute-start | bytes 497672 | tf_op jit(solution)/shard_map/ppermute | solution.py:71
  13.6 3.0 %collective-permute-start.3 = (bf16[72,1152]{1,0:T(8,128)(2,1)}, bf16[72,1152]{1,0:T(8,128)(2,1)S(1)}, u32[]{:S(2)}, u32[]{:S(2)}) collective-permute-start(bf16[72,1152]{1,0:T(8,128)(2,1)} %bitcast.59), channel_id=1, source_target_pairs={{0,16},{4,20},{8,24},{12,28},{16,0},{20,4},{24,8},{28,12},{1,17},{... | collective-permute-start | bytes 497672 | tf_op jit(solution)/shard_map/ppermute | solution.py:71
  23.5 4.9 %all-to-all-start = ((bf16[8,232,72]{1,2,0:T(8,128)(2,1)}), bf16[8,232,72]{1,2,0:T(8,128)(2,1)S(1)}, u32[]{:S(2)}, u32[]{:S(2)}) async-start(bf16[8,232,72]{1,2,0:T(8,128)(2,1)} %broadcast_in_dim.76), calls=%async_computation | async-start | bytes 589824 | tf_op jit(solution)/shard_map/all_to_all | solution.py:89
  29.3 3.8 %collective-permute-start.5 = (bf16[72,1152]{1,0:T(8,128)(2,1)S(1)}, bf16[72,1152]{1,0:T(8,128)(2,1)S(1)}, u32[]{:S(2)}, u32[]{:S(2)}) collective-permute-start(bf16[72,1152]{1,0:T(8,128)(2,1)S(1)} %bitcast.62), channel_id=1, source_target_pairs={{0,24},{4,28},{8,16},{12,20},{16,8},{20,12},{24,0},{28,4},{1,25},{... | collective-permute-start | bytes 497672 | tf_op jit(solution)/shard_map/ppermute | solution.py:71
  34.8 8.7 %collective-permute-done.4 = bf16[72,1152]{1,0:T(8,128)(2,1)S(1)} collective-permute-done((bf16[72,1152]{1,0:T(8,128)(2,1)}, bf16[72,1152]{1,0:T(8,128)(2,1)S(1)}, u32[]{:S(2)}, u32[]{:S(2)}) %collective-permute-start.4) | collective-permute-done | bytes 165920 | tf_op jit(solution)/shard_map/ppermute | solution.py:71
  43.5 6.3 %collective-permute-done.5 = bf16[72,1152]{1,0:T(8,128)(2,1)S(1)} collective-permute-done((bf16[72,1152]{1,0:T(8,128)(2,1)S(1)}, bf16[72,1152]{1,0:T(8,128)(2,1)S(1)}, u32[]{:S(2)}, u32[]{:S(2)}) %collective-permute-start.5) | collective-permute-done | bytes 165920 | tf_op jit(solution)/shard_map/ppermute | solution.py:71
  49.8 2.0 collective-permute-done.6
  51.9 2.1 all-to-all-done
  54.9 4.5 %mixer_in.1 = (bf16[256,1152]{1,0:T(8,128)(2,1)}, f32[256,576]{1,0:T(8,128)}, bf16[256,576]{1,0:T(8,128)(2,1)}, bf16[256,104]{1,0:T(8,128)(2,1)}, f32[200,576]{1...) custom-call(s32[1,2]{1,0:T(1,128)} %lengths.7, s32[3]{0:T(128)} %pad_add_fusion.places, ...), custom_call_target="tpu_custom_call" | custom-call | tf_op jit(solution)/shard_map/mixer_in/pallas_call | solution.py:47
  59.5 7.4 %all-gather = bf16[1024,104]{1,0:T(8,128)(2,1)} all-gather(bf16[256,104]{1,0:T(8,128)(2,1)} %get-tuple-element.71), channel_id=2, replica_groups=mesh['expert'=8,'hidden'=4] {'hidden'}, dimensions={0}, use_global_device_ids=true | all-gather | bytes 266240 | tf_op jit(solution)/shard_map/all_gather | solution.py:1021
  66.9 14.2 %scan_forward.1 = (f32[256,576]{1,0:T(8,128)}, f32[256,16,640]{2,1,0:T(8,128)}, f32[256,576]{1,0:T(8,128)}, f32[128,256]{1,0:T(8,128)}, bf16[256,72]{1,0:T(8,128)(2,1)}) custom-call(s32[1,2]{1,0:T(1,128)} %lengths.7, bf16[4,256,104]{2,1,0:T(8,128)(2,1)} %bitcast.52, bf16[256,576]{1,0:T(8,128)(2,1)} %get-tuple-element.72.activity, ...), custom_call_target="tpu_custom_call" | custom-call | tf_op jit(solution)/shard_map/scan_forward/pallas_call | solution.py:47
  81.2 7.5 %all-gather.12.cloned.1.call-done.weight_z.weight_out = bf16[576,2304]{1,0:T(8,128)(2,1)} async-done(((bf16[72,2304]{1,0:T(8,128)(2,1)}), bf16[576,2304]{1,0:T(8,128)(2,1)}) %all-gather.12.cloned.1.call-update) | async-done | bytes 2654224 | tf_op jit(solution)/shard_map/all_gather | solution.py:1003
  88.7 4.5 %mixer_out.1 = (bf16[256,576]{1,0:T(8,128)(2,1)}, f32[256,576]{1,0:T(8,128)}, bf16[128,1152]{1,0:T(8,128)(2,1)}, bf16[128,1152]{1,0:T(8,128)(2,1)}) custom-call(s32[3]{0:T(128)} %pad_add_fusion.places, f32[256,576]{1,0:T(8,128)} %get-tuple-element.74.out, bf16[256,576]{1,0:T(8,128)(2,1)} %get-tuple-element.72.activity, ...), custom_call_target="tpu_custom_call" | custom-call | tf_op jit(solution)/shard_map/mixer_out/pallas_call | solution.py:47
  93.3 1.8 collective-permute-done.7
  96.1 1.8 collective-permute-start.8
  97.9 7.3 %collective-permute-done.8 = bf16[128,1152]{1,0:T(8,128)(2,1)S(1)} collective-permute-done((bf16[128,1152]{1,0:T(8,128)(2,1)S(1)}, bf16[128,1152]{1,0:T(8,128)(2,1)S(1)}, u32[]{:S(2)}, u32[]{:S(2)}) %collective-permute-start.8) | collective-permute-done | bytes 294944 | tf_op jit(solution)/shard_map/ppermute | solution.py:71
  108.6 3.8 %middle.1 = (f32[256,1152]{1,0:T(8,128)}, bf16[256,1152]{1,0:T(8,128)(2,1)}, bf16[384,1152]{1,0:T(8,128)(2,1)}, bf16[384,1152]{1,0:T(8,128)(2,1)}, bf16[128,1152]{1,0:T(8,128)(2,1)}, /*index=5*/f32[16,256]{1,0:T(8,128)}) custom-call(s32[3]{0:T(128)} %pad_add_fusion.places, bf16[256,1152]{1,0:T(8,128)(2,1)} %tokens.5, bf16[128,1152]{1,0:T(8,128)(2,1)} %copy-done.9, ...), custom_call_target="tpu_custom_call" | custom-call | tf_op jit(solution)/shard_map/middle/pallas_call | solution.py:47
  112.4 18.7 %experts_local.1 = (bf16[256,1152]{1,0:T(8,128)(2,1)}, bf16[128,1152]{1,0:T(8,128)(2,1)}, bf16[128,1152]{1,0:T(8,128)(2,1)}, f32[16,256]{1,0:T(8,128)}) custom-call(s32[3]{0:T(128)} %pad_add_fusion.places, f32[1,256]{1,0:T(1,128)} %compare_select_fusion.codes, f32[16,256]{1,0:T(8,128)} %get-tuple-element.81.logits, ...), custom_call_target="tpu_custom_call" | custom-call | tf_op jit(solution)/shard_map/experts_local/pallas_call | solution.py:47
  134.1 1.8 collective-permute-start.11
  136.6 15.1 %all_to_all.15.packed.codes = f32[8,16,256]{2,1,0:T(8,128)S(1)} all-to-all(f32[8,16,256]{2,1,0:T(8,128)S(1)} %broadcast_in_dim.78), channel_id=1, replica_groups=mesh['expert'=8,'hidden'=4] {'expert'}, dimensions={0} | all-to-all | bytes 262144 | tf_op jit(solution)/shard_map/all_to_all | solution.py:89
  151.7 5.8 %all-gather.2 = f32[32,1,256]{2,1,0:T(1,128)} all-gather(f32[8,1,256]{2,1,0:T(1,128)S(1)} %slice.34), channel_id=4, replica_groups=mesh['expert'=8,'hidden'=4] {'hidden'}, dimensions={0}, use_global_device_ids=true | all-gather | bytes 40960 | tf_op jit(solution)/shard_map/all_gather | solution.py:1039
  161.7 3.0 %fusion.12 = (bf16[8,64,1152]{2,1,0:T(8,128)(2,1)}, bf16[8,64,1152]{2,1,0:T(8,128)(2,1)S(1)}) fusion(bf16[8,128,1152]{2,1,0:T(8,128)(2,1)} %after.6.refs_2_.refs_0_), kind=kLoop, calls=%fused_computation.41 | loop fusion | bytes 4718592 | tf_op jit(solution)/shard_map/slice | solution.py:1092
  165.8 29.1 %backward.1 = (f32[8,1,256]{2,1,0:T(1,128)}, f32[256,1152]{1,0:T(8,128)}, bf16[576,1152]{1,0:T(8,128)(2,1)}, f32[256,576]{1,0:T(8,128)}, bf16[256,576]{1,0:T(8,1...) custom-call(s32[1,2]{1,0:T(1,128)} %lengths.7, s32[3]{0:T(128)} %pad_add_fusion.places, ...), custom_call_target="tpu_custom_call" | custom-call | tf_op jit(solution)/shard_map/backward/pallas_call | solution.py:47
  195.6 7.6 %all-gather.3 = bf16[1024,128]{1,0:T(8,128)(2,1)} all-gather(bf16[256,128]{1,0:T(8,128)(2,1)} %get-tuple-element.95), channel_id=5, replica_groups=mesh['expert'=8,'hidden'=4] {'hidden'}, dimensions={0}, use_global_device_ids=true | all-gather | bytes 327680 | tf_op jit(solution)/shard_map/all_gather | solution.py:1052
  203.2 8.1 %mixer_back.1 = (bf16[256,1152]{1,0:T(8,128)(2,1)}, bf16[256,1152]{1,0:T(8,128)(2,1)}, bf16[8,72,1920]{2,1,0:T(8,128)(2,1)}) custom-call(s32[1,2]{1,0:T(1,128)} %lengths.7, s32[3]{0:T(128)} %pad_add_fusion.places, bf16[4,256,128]{2,1,0:T(8,128)(2,1)} %bitcast.51, f32[256,576]{1,0:T(8,128)} %get-tuple-element.96.grad_act, ...), custom_call_target="tpu_custom_call" | custom-call | tf_op jit(solution)/shard_map/mixer_back/pallas_call | solution.py:47
  212.4 4.7 %all-to-all-start.2 = ((bf16[8,72,1920]{2,1,0:T(8,128)(2,1)}), bf16[8,72,1920]{2,1,0:T(8,128)(2,1)}, u32[]{:S(2)}, u32[]{:S(2)}) async-start(bf16[8,72,1920]{2,1,0:T(8,128)(2,1)} %get-tuple-element.108), calls=%async_computation.2 | async-start | bytes 4423680 | tf_op jit(solution)/shard_map/all_to_all | solution.py:1061
  219.5 31.2 %expert_grads.1 = (f32[8,144,768]{2,1,0:T(8,128)}, f32[8,144,768]{2,1,0:T(8,128)}) custom-call(s32[3]{0:T(128)} %pad_add_fusion.places, f32[8,16,256]{2,1,0:T(8,128)} %copy-done.12, f32[8,1,256]{2,1,0:T(1,128)} %get-tuple-element.94.refs_1_.gates, bf16[8,128,1152]{2,1,0:T(8,128)(2,1)} %after.7._rows.refs_0_, ...), custom_call_target="tpu_custom_call" | custom-call | flops 32614907904 | tf_op jit(solution)/shard_map/expert_grads/pallas_call | solution.py:47
  250.7 1.8 collective-permute-done.15.refs_0_
  257.4 1.8 fusion.5
  259.2 8.9 %all-to-all-done.2.both = bf16[8,72,1920]{2,1,0:T(8,128)(2,1)} async-done(((bf16[8,72,1920]{2,1,0:T(8,128)(2,1)}), bf16[8,72,1920]{2,1,0:T(8,128)(2,1)}, u32[]{:S(2)}, u32[]{:S(2)}) %all-to-all-start.2) | async-done | bytes 2211872 | tf_op jit(solution)/shard_map/all_to_all | solution.py:1061
  268.1 5.6 %proj_grads.1 = (f32[72,1152]{1,0:T(8,128)}, f32[72,1152]{1,0:T(8,128)}, f32[72,104]{1,0:T(8,128)}, f32[4,72]{1,0:T(4,128)}, f32[1,72]{1,0:T(1,128)}, /*index=5*...) custom-call(s32[3]{0:T(128)} %pad_add_fusion.places, ...), custom_call_target="tpu_custom_call" | custom-call | tf_op jit(solution)/shard_map/proj_grads/pallas_call | solution.py:47
  273.8 5.3 %all-gather.7 = f32[4,1,144]{2,1,0:T(1,128)S(1)} all-gather(f32[1,1,144]{2,1,0:T(1,128)} %bitcast.68), channel_id=8, replica_groups=mesh['expert'=8,'hidden'=4] {'hidden'}, dimensions={0}, use_global_device_ids=true | all-gather | bytes 2880 | tf_op jit(solution)/shard_map/all_gather | solution.py:1098
  (125 shorter events, 35.4 us)
Async XLA Ops:
  7.2 15.5 %copy-start.15 = (bf16[72,104]{1,0:T(8,128)(2,1)S(1)}, bf16[72,104]{1,0:T(8,128)(2,1)}, u32[]{:S(2)}) copy-start(bf16[72,104]{1,0:T(8,128)(2,1)} %param.28) | copy-start | bytes 44932
  7.2 81.5 %all-gather.12.cloned.1.call-start = ((), (), s32[]{:S(2)}) async-start(), calls=%async_computation.3 | async-start | bytes 2985984 | tf_op jit(solution)/shard_map/all_gather | solution.py:1003
  9.0 20.3 %collective-permute-start = (bf16[72,1152]{1,0:T(8,128)(2,1)}, bf16[72,1152]{1,0:T(8,128)(2,1)S(1)}, u32[]{:S(2)}, u32[]{:S(2)}) collective-permute-start(bf16[72,1152]{1,0:T(8,128)(2,1)} %bitcast.56), channel_id=1, source_target_pairs={{0,4},{4,0},{8,12},{12,8},{16,20},{20,16},{24,28},{28,24},{1,5},{5... | collective-permute-start | bytes 497672 | tf_op jit(solution)/shard_map/ppermute | solution.py:71
  12.0 21.1 %collective-permute-start.1 = (bf16[72,1152]{1,0:T(8,128)(2,1)}, bf16[72,1152]{1,0:T(8,128)(2,1)S(1)}, u32[]{:S(2)}, u32[]{:S(2)}) collective-permute-start(bf16[72,1152]{1,0:T(8,128)(2,1)} %bitcast.57), channel_id=1, source_target_pairs={{0,8},{4,12},{8,0},{12,4},{16,24},{20,28},{24,16},{28,20},{1,9},{5... | collective-permute-start | bytes 497672 | tf_op jit(solution)/shard_map/ppermute | solution.py:71
  13.6 21.1 %collective-permute-start.2 = (bf16[72,1152]{1,0:T(8,128)(2,1)}, bf16[72,1152]{1,0:T(8,128)(2,1)S(1)}, u32[]{:S(2)}, u32[]{:S(2)}) collective-permute-start(bf16[72,1152]{1,0:T(8,128)(2,1)} %bitcast.58), channel_id=1, source_target_pairs={{0,12},{4,8},{8,4},{12,0},{16,28},{20,24},{24,20},{28,16},{1,13},{... | collective-permute-start | bytes 497672 | tf_op jit(solution)/shard_map/ppermute | solution.py:71
  13.6 21.1 %collective-permute-start.3 = (bf16[72,1152]{1,0:T(8,128)(2,1)}, bf16[72,1152]{1,0:T(8,128)(2,1)S(1)}, u32[]{:S(2)}, u32[]{:S(2)}) collective-permute-start(bf16[72,1152]{1,0:T(8,128)(2,1)} %bitcast.59), channel_id=1, source_target_pairs={{0,16},{4,20},{8,24},{12,28},{16,0},{20,4},{24,8},{28,12},{1,17},{... | collective-permute-start | bytes 497672 | tf_op jit(solution)/shard_map/ppermute | solution.py:71
  16.6 26.9 %collective-permute-start.4 = (bf16[72,1152]{1,0:T(8,128)(2,1)}, bf16[72,1152]{1,0:T(8,128)(2,1)S(1)}, u32[]{:S(2)}, u32[]{:S(2)}) collective-permute-start(bf16[72,1152]{1,0:T(8,128)(2,1)} %bitcast.60), channel_id=1, source_target_pairs={{0,20},{4,16},{8,28},{12,24},{16,4},{20,0},{24,12},{28,8},{1,21},{... | collective-permute-start | bytes 497672 | tf_op jit(solution)/shard_map/ppermute | solution.py:71
  22.7 5.9 %copy-start.14 = (bf16[1152,72]{0,1:T(8,128)(2,1)S(1)}, bf16[1152,72]{0,1:T(8,128)(2,1)}, u32[]{:S(2)}) copy-start(bf16[1152,72]{0,1:T(8,128)(2,1)} %param.24) | copy-start | bytes 497668
  23.5 30.4 %all-to-all-start = ((bf16[8,232,72]{1,2,0:T(8,128)(2,1)}), bf16[8,232,72]{1,2,0:T(8,128)(2,1)S(1)}, u32[]{:S(2)}, u32[]{:S(2)}) async-start(bf16[8,232,72]{1,2,0:T(8,128)(2,1)} %broadcast_in_dim.76), calls=%async_computation | async-start | bytes 589824 | tf_op jit(solution)/shard_map/all_to_all | solution.py:89
  28.4 131.3 %all-gather.14.cloned.1.call-start = ((), (), s32[]{:S(2)}) async-start(), calls=%async_computation.4 | async-start | bytes 2654208 | tf_op jit(solution)/shard_map/all_gather | solution.py:1026
  29.3 20.4 %collective-permute-start.5 = (bf16[72,1152]{1,0:T(8,128)(2,1)S(1)}, bf16[72,1152]{1,0:T(8,128)(2,1)S(1)}, u32[]{:S(2)}, u32[]{:S(2)}) collective-permute-start(bf16[72,1152]{1,0:T(8,128)(2,1)S(1)} %bitcast.62), channel_id=1, source_target_pairs={{0,24},{4,28},{8,16},{12,20},{16,8},{20,12},{24,0},{28,4},{1,25},{... | collective-permute-start | bytes 497672 | tf_op jit(solution)/shard_map/ppermute | solution.py:71
  33.1 18.7 %collective-permute-start.6 = (bf16[72,1152]{1,0:T(8,128)(2,1)S(1)}, bf16[72,1152]{1,0:T(8,128)(2,1)S(1)}, u32[]{:S(2)}, u32[]{:S(2)}) collective-permute-start(bf16[72,1152]{1,0:T(8,128)(2,1)S(1)} %bitcast.63), channel_id=1, source_target_pairs={{0,28},{4,24},{8,20},{12,16},{16,12},{20,8},{24,4},{28,0},{1,29},{... | collective-permute-start | bytes 497672 | tf_op jit(solution)/shard_map/ppermute | solution.py:71
  59.5 135.5 %all-gather.16.cloned.1.call-start = ((), (), s32[]{:S(2)}) async-start(), calls=%async_computation.5 | async-start | bytes 2654208 | tf_op jit(solution)/shard_map/all_gather | solution.py:1034
  93.2 12.2 %copy-start.16 = (s32[1,2]{1,0:T(1,128)S(1)}, s32[1,2]{1,0:T(1,128)}, u32[]{:S(2)}) copy-start(s32[1,2]{1,0:T(1,128)} %lengths.7) | copy-start | bytes 28
  93.2 14.1 %copy-start.17 = (s32[256,1]{0,1:T(1,128)S(1)}, s32[256,1]{0,1:T(1,128)}, u32[]{:S(2)}) copy-start(s32[256,1]{0,1:T(1,128)} %param.22) | copy-start | bytes 3076
  93.2 1.9 collective-permute-start.7
  96.1 9.1 %collective-permute-start.8 = (bf16[128,1152]{1,0:T(8,128)(2,1)S(1)}, bf16[128,1152]{1,0:T(8,128)(2,1)S(1)}, u32[]{:S(2)}, u32[]{:S(2)}) collective-permute-start(bf16[128,1152]{1,0:T(8,128)(2,1)S(1)} %add_convert_fusion.5), channel_id=1, source_target_pairs={{0,2},{1,3},{2,0},{3,1},{4,6},{5,7},{6,4},{7,5},{8,10},{9,11},{10,... | collective-permute-start | bytes 884744 | tf_op jit(solution)/shard_map/ppermute | solution.py:71
  105.3 2.6 collective-permute-start.9
  131.2 1.9 collective-permute-start.10
  134.1 23.5 %collective-permute-start.11 = (bf16[128,1152]{1,0:T(8,128)(2,1)S(1)}, bf16[128,1152]{1,0:T(8,128)(2,1)S(1)}, u32[]{:S(2)}, u32[]{:S(2)}) collective-permute-start(bf16[128,1152]{1,0:T(8,128)(2,1)S(1)} %add_convert_fusion.3), channel_id=1, source_target_pairs={{0,2},{1,3},{2,0},{3,1},{4,6},{5,7},{6,4},{7,5},{8,10},{9,11},{10,... | collective-permute-start | bytes 884744 | tf_op jit(solution)/shard_map/ppermute | solution.py:71
  159.3 1.6 collective-permute-start.12
  164.7 30.8 %collective-permute-start.13 = (bf16[8,64,1152]{2,1,0:T(8,128)(2,1)S(1)}, bf16[8,64,1152]{2,1,0:T(8,128)(2,1)}, u32[]{:S(2)}, u32[]{:S(2)}) collective-permute-start(bf16[8,64,1152]{2,1,0:T(8,128)(2,1)S(1)} %get-tuple-element.124), channel_id=1, source_target_pairs={{0,2},{1,3},{2,0},{3,1},{4,6},{5,7},{6,4},{7,5},{8,10},{9,11},{10,... | collective-permute-start | bytes 3538952 | tf_op jit(solution)/shard_map/ppermute | solution.py:71
  165.8 53.7 %collective-permute-start.17 = (bf16[8,128,1152]{2,1,0:T(8,128)(2,1)S(1)}, bf16[8,128,1152]{2,1,0:T(8,128)(2,1)}, u32[]{:S(2)}, u32[]{:S(2)}) collective-permute-start(bf16[8,128,1152]{2,1,0:T(8,128)(2,1)S(1)} %copy-done), channel_id=1, source_target_pairs={{0,1},{1,0},{2,3},{3,2},{4,5},{5,4},{6,7},{7,6},{8,9},{9,8},{10,11... | collective-permute-start | bytes 7077896 | tf_op jit(solution)/shard_map/ppermute | solution.py:71
  195.0 24.5 %collective-permute-start.16 = (bf16[8,128,1152]{2,1,0:T(8,128)(2,1)}, bf16[8,128,1152]{2,1,0:T(8,128)(2,1)}, u32[]{:S(2)}, u32[]{:S(2)}) collective-permute-start(bf16[8,128,1152]{2,1,0:T(8,128)(2,1)} %after.7._rows.refs_0_), channel_id=1, source_target_pairs={{0,1},{1,0},{2,3},{3,2},{4,5},{5,4},{6,7},{7,6},{8,9},{9,8},{10,11... | collective-permute-start | bytes 7077896 | tf_op jit(solution)/shard_map/ppermute | solution.py:71
  195.5 24.0 %collective-permute-start.18 = (bf16[8,64,1152]{2,1,0:T(8,128)(2,1)}, bf16[8,64,1152]{2,1,0:T(8,128)(2,1)}, u32[]{:S(2)}, u32[]{:S(2)}) collective-permute-start(bf16[8,64,1152]{2,1,0:T(8,128)(2,1)} %collective-permute-done.13._grads.refs_3_), channel_id=1, source_target_pairs={{0,1},{1,0},{2,3},{3,2},{4,5},{5,4},{6,7},{7,6},{8,9},{9,8},{10,11... | collective-permute-start | bytes 3538952 | tf_op jit(solution)/shard_map/ppermute | solution.py:71
  211.3 5.9 %collective-permute-start.14 = (bf16[256,1152]{1,0:T(8,128)(2,1)}, bf16[256,1152]{1,0:T(8,128)(2,1)}, u32[]{:S(2)}, u32[]{:S(2)}) collective-permute-start(bf16[256,1152]{1,0:T(8,128)(2,1)} %get-tuple-element.105), channel_id=1, source_target_pairs={{0,1},{1,0},{2,3},{3,2},{4,5},{5,4},{6,7},{7,6},{8,9},{9,8},{10,11... | collective-permute-start | bytes 1769480 | tf_op jit(solution)/shard_map/ppermute | solution.py:71
  211.4 44.4 %collective-permute-start.20 = (bf16[8,64,1152]{2,1,0:T(8,128)(2,1)}, bf16[8,64,1152]{2,1,0:T(8,128)(2,1)}, u32[]{:S(2)}, u32[]{:S(2)}) collective-permute-start(bf16[8,64,1152]{2,1,0:T(8,128)(2,1)} %after.9), channel_id=1, source_target_pairs={{0,2},{1,3},{2,0},{3,1},{4,6},{5,7},{6,4},{7,5},{8,10},{9,11},{10,... | collective-permute-start | bytes 3538952 | tf_op jit(solution)/shard_map/ppermute | solution.py:71
  212.4 55.7 %all-to-all-start.2 = ((bf16[8,72,1920]{2,1,0:T(8,128)(2,1)}), bf16[8,72,1920]{2,1,0:T(8,128)(2,1)}, u32[]{:S(2)}, u32[]{:S(2)}) async-start(bf16[8,72,1920]{2,1,0:T(8,128)(2,1)} %get-tuple-element.108), calls=%async_computation.2 | async-start | bytes 4423680 | tf_op jit(solution)/shard_map/all_to_all | solution.py:1061
  218.4 34.1 %collective-permute-start.15 = (bf16[256,1152]{1,0:T(8,128)(2,1)S(1)}, bf16[256,1152]{1,0:T(8,128)(2,1)S(1)}, u32[]{:S(2)}, u32[]{:S(2)}) collective-permute-start(bf16[256,1152]{1,0:T(8,128)(2,1)S(1)} %add_convert_fusion.1), channel_id=1, source_target_pairs={{0,2},{1,3},{2,0},{3,1},{4,6},{5,7},{6,4},{7,5},{8,10},{9,11},{10,... | collective-permute-start | bytes 1769480 | tf_op jit(solution)/shard_map/ppermute | solution.py:71
  254.6 2.3 collective-permute-start.19
  255.9 3.3 %collective-permute-start.21 = (bf16[8,64,1152]{2,1,0:T(8,128)(2,1)}, bf16[8,64,1152]{2,1,0:T(8,128)(2,1)S(1)}, u32[]{:S(2)}, u32[]{:S(2)}) collective-permute-start(bf16[8,64,1152]{2,1,0:T(8,128)(2,1)} %collective-permute-done.20.refs_2_), channel_id=1, source_target_pairs={{0,1},{1,0},{2,3},{3,2},{4,5},{5,4},{6,7},{7,6},{8,9},{9,8},{10,11... | collective-permute-start | bytes 3538952 | tf_op jit(solution)/shard_map/ppermute | solution.py:71
  259.2 8.9 %copy-start.6 = (bf16[8,64,1152]{2,1,0:T(8,128)(2,1)}, bf16[8,64,1152]{2,1,0:T(8,128)(2,1)S(1)}, u32[]{:S(2)}) copy-start(bf16[8,64,1152]{2,1,0:T(8,128)(2,1)S(1)} %collective-permute-done.21.refs_3_) | copy-start | bytes 3538948
  (13 other events, 31.9 us)
Sparse Core Ops, SparseCore 0:
  10.8 77.8 all-gather.11
  91.4 50.3 all-gather.13
  144.0 50.5 all-gather.15
